TPU v7x, 256 devices: a whole 4x4x8 slice. The times are simulated.
256 devices in a mesh: prompt: 16 (over y, x_hi, core), resp: 16 (over x_lo, z).
Axes of the slice: x: 4 (x_hi: 2, x_lo: 2; x = x_hi * 2 + x_lo), y: 4, z: 8, core: 2. Of those that a mesh axis runs over, the one named last changes fastest.
Arguments:
- q_prefix: bfloat16 [16, 1024, 1024], P('prompt', 'resp'), may hold values from -40 to 40
- q_resp: bfloat16 [16, 4, 1024, 1024], P('prompt', None, 'resp'), may hold values from -40 to 40
- k_prefix: bfloat16 [16, 1024, 128], P('prompt', 'resp'), may hold values from -6 to 6
- v_prefix: bfloat16 [16, 1024, 128], P('prompt', 'resp'), may hold values from -6 to 6
- k_resp: bfloat16 [16, 4, 1024, 128], P('prompt', None, 'resp'), may hold values from -6 to 6
- v_resp: bfloat16 [16, 4, 1024, 128], P('prompt', None, 'resp'), may hold values from -6 to 6
- dout_prefix: bfloat16 [16, 1024, 1024], P('prompt', 'resp'), may hold values from -144 to 144
- dout_resp: bfloat16 [16, 4, 1024, 1024], P('prompt', None, 'resp'), may hold values from -144 to 144
- lengths: int32 [16, 4], P('prompt'), may hold values from 1 to 1024, as said below
Outputs:
- dq_prefix: bfloat16 [16, 1024, 1024], P('prompt', 'resp')
- dq_resp: bfloat16 [16, 4, 1024, 1024], P('prompt', None, 'resp')
- dk_prefix: float32 [16, 1024, 128], P('prompt', 'resp')
- dv_prefix: float32 [16, 1024, 128], P('prompt', 'resp')
- dk_resp: float32 [16, 4, 1024, 128], P('prompt', None, 'resp')
- dv_resp: float32 [16, 4, 1024, 128], P('prompt', None, 'resp')
Inputs may be any that keep to these rules, and one draw needn't show every extreme that they name: `lengths`: some response has exactly 1024 tokens.
All inputs are finite; a program needn't handle non-finite values.
Results may differ from a plain program's by a relative error of at most 0.019.
Values may be sent and summed in bfloat16 or wider, within the bound.
No kernel may reach another device: no remote copies, remote signals or barrier semaphores. Data moves between devices by JAX's collectives and lax.ppermute only.
A program may use at most 64 MiB of HBM per device.

v0:
```python
import jax
import jax.numpy as jnp
from jax import lax
from jax.experimental import pallas as pl
from jax.experimental.pallas import tpu as pltpu
from jax.sharding import PartitionSpec as P

HD = 128
HEADS = 8
ROWS = 64
CHUNK = ROWS * HEADS
ZN = 8
PROMPTS = 16
RESPS = 4
TOKENS = 65536.0
NEG = -1e30
SCALE = HD**-0.5
LOG2E = 1.4426950408889634
TILE_BLOCKS = 4
TILE = TILE_BLOCKS * ROWS
BIG = 24
VMEM = pl.BlockSpec(memory_space=pltpu.VMEM)
SMEM = pl.BlockSpec(memory_space=pltpu.SMEM)
F32 = jnp.float32
BF16 = jnp.bfloat16


def dot_nt(a, b):
    return lax.dot_general(a, b, (((1,), (1,)), ((), ())), preferred_element_type=F32)


def dot_tn(a, b):
    return lax.dot_general(a, b, (((0,), (0,)), ((), ())), preferred_element_type=F32)


def dot_nn(a, b):
    return lax.dot_general(a, b, (((1,), (0,)), ((), ())), preferred_element_type=F32)


def stack_heads(rows):
    return jnp.concatenate([rows[:, h * HD : (h + 1) * HD] for h in range(HEADS)], axis=0)


def unstack_heads(rows):
    return jnp.concatenate([rows[h * ROWS : (h + 1) * ROWS] for h in range(HEADS)], axis=1)


def place():
    me = lax.axis_index("resp")
    return me >> 3, me & (ZN - 1)


def dealt(lengths):
    size = [lengths[0, i] for i in range(RESPS)]
    rank = []
    for i in range(RESPS):
        before = [
            ((size[j] >= size[i]) if j < i else (size[j] > size[i])).astype(jnp.int32)
            for j in range(RESPS)
            if j != i
        ]
        rank.append(before[0] + before[1] + before[2])
    at = [
        sum(jnp.where(rank[i] == k, i, 0) for i in range(1, RESPS)) for k in range(RESPS)
    ]
    return (at[0], at[3]), (at[1], at[2])


def of_half(both, half):
    return tuple(jnp.where(half == 0, a, b) for a, b in zip(*both))


def keep_mask(key_first, row_first, tile):
    key_pos = key_first + lax.broadcasted_iota(jnp.int32, (tile, CHUNK), 0)
    row_pos = row_first + (lax.broadcasted_iota(jnp.int32, (tile, CHUNK), 1) & (ROWS - 1))
    return key_pos <= row_pos


def stats_step(stats, q, d, kt, vt, keep):
    top, total, mixed = stats
    s = dot_nt(kt, q) * (SCALE * LOG2E)
    g = dot_nt(vt, d)
    if keep is not None:
        s = jnp.where(keep, s, NEG)
    new_top = jnp.maximum(top, jnp.max(s, axis=0, keepdims=True))
    e = jnp.exp2(s - new_top)
    fix = jnp.exp2(top - new_top)
    total = total * fix + jnp.sum(e, axis=0, keepdims=True)
    mixed = mixed * fix + jnp.sum(e * g, axis=0, keepdims=True)
    return new_top, total, mixed


def grads_step(q, d, kt, vt, log_sum, delta, keep):
    s = dot_nt(kt, q) * (SCALE * LOG2E)
    g = dot_nt(vt, d)
    w = jnp.exp2(s - log_sum)
    if keep is not None:
        w = jnp.where(keep, w, 0.0)
    grad_s = (w * (g - delta)).astype(BF16)
    dv = dot_nn(w.astype(BF16), d)
    dk = dot_nn(grad_s, q)
    dq = dot_tn(grad_s, kt)
    return dq, dk, dv


def empty_stats():
    return (
        jnp.full((1, CHUNK), NEG, F32),
        jnp.zeros((1, CHUNK), F32),
        jnp.zeros((1, CHUNK), F32),
    )


def finish(stats):
    top, total, mixed = stats
    return top + jnp.log2(total), mixed / total


def chunk_first(chunk):
    half, z = place()
    return ((half ^ (chunk & 1)) * ZN + z) * ROWS


def chunk_length(lengths, chunk):
    first, second = of_half(dealt(lengths), place()[0])
    return lengths[0, jnp.where(chunk < 2, first, second)]


def live_chunks(lengths, body):
    def one(chunk, carried):
        @pl.when(chunk_first(chunk) < chunk_length(lengths, chunk))
        def _():
            body(chunk)

        return carried

    lax.fori_loop(0, 2 * 2, one, 0)


def keys_kernel(lengths, kr, vr, kp, vp, sent, prefix):
    half, _ = place()
    for slot, resp in enumerate(of_half(dealt(lengths), 1 - half)):
        sent[0, slot] = kr[0, resp]
        sent[1, slot] = vr[0, resp]
    for step in range(ZN):
        prefix[step, 0] = kp[0]
        prefix[step, 1] = vp[0]


def pick_kernel(lengths, rows, sent):
    half, _ = place()
    for slot, resp in enumerate(of_half(dealt(lengths), 1 - half)):
        sent[slot] = rows[0, resp]


def block_kernel(lengths, kr, vr, got, _, block, count):
    half, _ = place()
    for slot, resp in enumerate(of_half(dealt(lengths), half)):
        for step in range(ZN):
            block[step, 0, 0, slot] = kr[0, resp]
            block[step, 0, 1, slot] = vr[0, resp]
            block[step, 1, 0, slot] = got[0, slot]
            block[step, 1, 1, slot] = got[1, slot]
    total = lengths[0, 0] + lengths[0, 1] + lengths[0, 2] + lengths[0, 3]
    count[...] = jnp.full(count.shape, total, jnp.int32).astype(F32)


def prefix_kernel(
    lengths, qr, dr, q_got, d_got, qp, dp, kv_own, kv_pair,
    q_st, d_st, stats_out, dq_out, acc, kv, q1, d1, dq_acc,
):
    half, z = place()
    kv[half] = kv_own[...]
    kv[1 - half] = kv_pair[...]
    acc[...] = jnp.zeros_like(acc)
    q1[...] = stack_heads(qp[0])
    d1[...] = stack_heads(dp[0])
    dq_acc[...] = jnp.zeros_like(dq_acc)
    block = half * ZN + z
    tiles = block // TILE_BLOCKS + 1

    def load(tile):
        lead = tile >> 1
        first = (tile & 1) * TILE_BLOCKS
        keys, values = (
            kv[lead, pl.ds(first, TILE_BLOCKS), kind].reshape(TILE, HD) for kind in range(2)
        )
        return lead, first, keys, values, keep_mask(tile * TILE, block * ROWS, TILE)

    def first_pass(tile, stats):
        _, _, keys, values, keep = load(tile)
        return stats_step(stats, q1[...], d1[...], keys, values, keep)

    log_sum, delta = finish(lax.fori_loop(0, tiles, first_pass, empty_stats()))

    def second_pass(tile, carried):
        lead, first, keys, values, keep = load(tile)
        dq, dk, dv = grads_step(q1[...], d1[...], keys, values, log_sum, delta, keep)
        dq_acc[...] += dq
        acc[lead, pl.ds(first, TILE_BLOCKS), 0] += dk.reshape(TILE_BLOCKS, ROWS, HD)
        acc[lead, pl.ds(first, TILE_BLOCKS), 1] += dv.reshape(TILE_BLOCKS, ROWS, HD)
        return carried

    lax.fori_loop(0, tiles, second_pass, 0)
    dq_out[...] = unstack_heads(dq_acc[...])
    responses = of_half(dealt(lengths), half)
    for chunk in range(4):
        slot = chunk >> 1
        if chunk & 1:
            queries, douts = q_got[slot], d_got[slot]
        else:
            queries, douts = qr[0, responses[slot]], dr[0, responses[slot]]
        pos = chunk_first(chunk) + lax.broadcasted_iota(jnp.int32, douts.shape, 0)
        douts = jnp.where(pos < lengths[0, responses[slot]], douts.astype(F32), 0.0).astype(BF16)
        q_st[chunk] = stack_heads(queries)
        d_st[chunk] = stack_heads(douts)

    def body(chunk):
        stats = empty_stats()
        for lead in range(2):
            for first in range(0, ZN, TILE_BLOCKS):
                keys, values = (
                    kv[lead, first : first + TILE_BLOCKS, kind].reshape(TILE, HD)
                    for kind in range(2)
                )
                stats = stats_step(stats, q_st[chunk], d_st[chunk], keys, values, None)
        for row in range(3):
            stats_out[chunk, row : row + 1] = stats[row]

    live_chunks(lengths, body)


def resp_tile(kv, slot, tile):
    half, _ = place()
    which = (tile >> 1) ^ half
    at = pl.ds((tile & 1) * TILE_BLOCKS, TILE_BLOCKS)
    return (kv[at, which, kind, slot].reshape(TILE, HD) for kind in range(2))


def half_prefix(chunk, q_st, d_st, log_sum, delta, kv, dq_acc, acc):
    for first in range(0, ZN, TILE_BLOCKS):
        at = slice(first, first + TILE_BLOCKS)
        keys, values = (kv[at, kind].reshape(TILE, HD) for kind in range(2))
        dq, dk, dv = grads_step(q_st[chunk], d_st[chunk], keys, values, log_sum, delta, None)
        dq_acc[chunk] += dq
        acc[at, 0] += dk.reshape(TILE_BLOCKS, ROWS, HD)
        acc[at, 1] += dv.reshape(TILE_BLOCKS, ROWS, HD)


def resp_kernel(
    lengths, total, q_st, d_st, stats_in, kv, factor_out, log_out, dq_out, grads, acc
):
    factor_out[...] = TOKENS / (2.0 * total[...])
    acc[...] = jnp.zeros_like(acc)
    dq_out[...] = jnp.zeros_like(dq_out)

    def body(chunk):
        row_first = chunk_first(chunk)
        last = row_first // TILE
        slot = chunk >> 1

        def first(tile, stats, keep):
            keys, values = resp_tile(kv, slot, tile)
            return stats_step(stats, q_st[chunk], d_st[chunk], keys, values, keep)

        keep = keep_mask(last * TILE, row_first, TILE)
        stats = tuple(stats_in[chunk, row : row + 1] for row in range(3))
        stats = lax.fori_loop(0, last, lambda tile, now: first(tile, now, None), stats)
        log_sum, delta = finish(first(last, stats, keep))
        log_out[chunk, 0:1] = log_sum
        log_out[chunk, 1:2] = delta

        def second(tile, keep):
            keys, values = resp_tile(kv, slot, tile)
            dq, dk, dv = grads_step(q_st[chunk], d_st[chunk], keys, values, log_sum, delta, keep)
            dq_out[chunk] += dq
            at = pl.ds(tile * TILE_BLOCKS, TILE_BLOCKS)
            acc[at, 0, slot] += dk.reshape(TILE_BLOCKS, ROWS, HD)
            acc[at, 1, slot] += dv.reshape(TILE_BLOCKS, ROWS, HD)

        def plain(tile, carried):
            second(tile, None)
            return carried

        lax.fori_loop(0, last, plain, 0)
        second(last, keep)

    live_chunks(lengths, body)
    grads[...] = acc[...].astype(BF16)


def pair_kernel(lengths, q_st, d_st, logs, dq_in, kv, acc_in, dq_out, g_pair, acc):
    acc[...] = acc_in[1 - place()[0]]
    dq_out[...] = dq_in[...]

    def body(chunk):
        half_prefix(chunk, q_st, d_st, logs[chunk, 0:1], logs[chunk, 1:2], kv, dq_out, acc)

    live_chunks(lengths, body)
    g_pair[...] = acc[...].astype(BF16)


def own_kernel(
    lengths, scale, q_st, d_st, logs, dq_in, dqp_in, kv, acc_in,
    dqp_out, dq_own, dq_pair, g_own, dq_acc,
):
    factor = scale[0:1] * SCALE
    wide = jnp.concatenate([factor] * HEADS, axis=1)
    dqp_out[0] = (dqp_in[...] * wide).astype(BF16)
    g_own[...] = acc_in[place()[0]]
    dq_acc[...] = dq_in[...]

    def body(chunk):
        half_prefix(chunk, q_st, d_st, logs[chunk, 0:1], logs[chunk, 1:2], kv, dq_acc, g_own)

    live_chunks(lengths, body)
    for slot in range(2):
        dq_own[slot] = unstack_heads((dq_acc[2 * slot] * factor).astype(BF16))
        dq_pair[slot] = unstack_heads((dq_acc[2 * slot + 1] * factor).astype(BF16))


def join_kernel(g_own, g_got, *outs):
    _, z = place()
    for step in range(ZN):
        at = (z + step) & (ZN - 1)
        outs[step][...] = (g_own[at] + g_got[at].astype(F32)).astype(outs[step].dtype)


def rows_kernel(lengths, own, got, out):
    half, _ = place()
    both = dealt(lengths)
    for slot, resp in enumerate(of_half(both, half)):
        out[0, resp] = own[slot]
    for slot, resp in enumerate(of_half(both, 1 - half)):
        out[0, resp] = got[slot]


def sums_kernel(lengths, scale, terms, own, *rest):
    others, (dkp, dvp, dkr, dvr) = rest[: ZN - 1], rest[ZN - 1 :]
    factor = scale[0:1]
    for kind, out, by in ((0, dkp, factor * SCALE), (1, dvp, factor)):
        value = own[kind]
        for other in others:
            value = value + other[kind].astype(F32)
        out[0] = value * by
    for half, responses in enumerate(dealt(lengths)):
        for slot, resp in enumerate(responses):
            for kind, out, by in ((0, dkr, factor * SCALE), (1, dvr, factor)):
                value = terms[half * ZN, kind, slot].astype(F32)
                for step in range(1, ZN):
                    value = value + terms[half * ZN + step, kind, slot].astype(F32)
                out[0, resp] = value * by


def shape(dims, dtype):
    return jax.ShapeDtypeStruct(dims, dtype)


def call(kernel, kinds, outs, scratch=(), flops=1 << 20, name=None, vmem=8):
    spec = {"s": SMEM, "v": VMEM, "a": pl.BlockSpec(memory_space=pl.ANY)}
    return pl.pallas_call(
        kernel,
        out_shape=outs,
        in_specs=[spec[kind] for kind in kinds],
        out_specs=[VMEM] * len(outs),
        scratch_shapes=list(scratch),
        name=name,
        cost_estimate=pl.CostEstimate(flops=flops, bytes_accessed=2 << 20, transcendentals=0),
        compiler_params=pltpu.CompilerParams(vmem_limit_bytes=vmem << 20),
    )


def per_device(
    q_prefix, q_resp, k_prefix, v_prefix, k_resp, v_resp, dout_prefix, dout_resp, lengths
):
    pair = [(i, (i + ZN) % (2 * ZN)) for i in range(2 * ZN)]
    columns = [list(range(ZN)), list(range(ZN, 2 * ZN))]

    def swap(value):
        return lax.ppermute(value, "resp", pair)

    def spread(value):
        return lax.all_to_all(value, "resp", 0, 0, axis_index_groups=columns)

    half_f32 = shape((ZN, 2, ROWS, HD), F32)
    half_bf16 = shape((ZN, 2, ROWS, HD), BF16)
    rows_bf16 = shape((2, ROWS, HEADS * HD), BF16)
    st = shape((4, CHUNK, HD), BF16)
    part = shape((4, CHUNK, HD), F32)
    logs_f32 = shape((4, 8, CHUNK), F32)

    kv_sent, prefix = call(
        keys_kernel, "svvvv", [shape((2, 2, ROWS, HD), BF16), half_bf16], name="keys"
    )(lengths, k_resp, v_resp, k_prefix, v_prefix)
    kv_got = swap(kv_sent)
    (q_sent,) = call(pick_kernel, "sv", [rows_bf16], name="queries")(lengths, q_resp)
    q_got = swap(q_sent)
    (d_sent,) = call(pick_kernel, "sv", [rows_bf16], name="douts")(lengths, dout_resp)
    d_got = swap(d_sent)
    kvp_own = spread(prefix)
    kvp_pair = swap(kvp_own)
    block, total = call(
        block_kernel, "svvva",
        [shape((ZN, 2, 2, 2, ROWS, HD), BF16), shape((8, HD), F32)], name="block",
    )(lengths, k_resp, v_resp, kv_got, q_got)
    kvr = spread(block)
    for step in (1, 2, 4, 8):
        total = total + lax.ppermute(total, "prompt", [(i, i ^ step) for i in range(PROMPTS)])

    q_st, d_st, stats, dqp, acc_p = call(
        prefix_kernel, "svvvvvvvv",
        [st, st, logs_f32, shape((ROWS, HEADS * HD), F32), shape((2, ZN, 2, ROWS, HD), F32)],
        [pltpu.VMEM((2, ZN, 2, ROWS, HD), BF16), pltpu.VMEM((CHUNK, HD), BF16),
         pltpu.VMEM((CHUNK, HD), BF16), pltpu.VMEM((CHUNK, HD), F32)],
        5 << 30, "prefix", BIG,
    )(lengths, q_resp, dout_resp, q_got, d_got, q_prefix, dout_prefix, kvp_own, kvp_pair)
    scale, logs, dq_part, grads_r = call(
        resp_kernel, "svvvvv",
        [shape((8, HD), F32), logs_f32, part, shape((2 * ZN, 2, 2, ROWS, HD), BF16)],
        [pltpu.VMEM((2 * ZN, 2, 2, ROWS, HD), F32)], 4 << 30, "resp", BIG,
    )(lengths, total, q_st, d_st, stats, kvr)
    terms_r = lax.all_to_all(grads_r, "resp", 0, 0)
    dq_part, g_pair = call(
        pair_kernel, "svvvvvv", [part, half_bf16],
        [pltpu.VMEM((ZN, 2, ROWS, HD), F32)], 4 << 30, "pair", BIG,
    )(lengths, q_st, d_st, logs, dq_part, kvp_pair, acc_p)
    g_got = swap(g_pair)
    dqp_out, dq_own, dq_pair, g_own = call(
        own_kernel, "svvvvvvvv",
        [shape((1, ROWS, HEADS * HD), BF16), rows_bf16, rows_bf16, half_f32],
        [pltpu.VMEM((4, CHUNK, HD), F32)], 4 << 30, "own", BIG,
    )(lengths, scale, q_st, d_st, logs, dq_part, dqp, kvp_own, acc_p)
    own, *blocks = call(
        join_kernel, "vv",
        [shape((2, ROWS, HD), F32)] + [shape((2, ROWS, HD), BF16)] * (ZN - 1), name="join",
    )(g_own, g_got)
    dq_got = swap(dq_pair)
    others = []
    for step, value in enumerate(blocks, 1):
        moves = [(c + i, c + (i + step) % ZN) for c in (0, ZN) for i in range(ZN)]
        others.append(lax.ppermute(value, "resp", moves))
    (dq_all,) = call(
        rows_kernel, "svv", [shape((1, RESPS, ROWS, HEADS * HD), BF16)], name="rows"
    )(lengths, dq_own, dq_got)
    prefix_out = shape((1, ROWS, HD), F32)
    resp_out = shape((1, RESPS, ROWS, HD), F32)
    dkp, dvp, dkr, dvr = call(
        sums_kernel, "s" + "v" * (ZN + 2), [prefix_out, prefix_out, resp_out, resp_out],
        name="sums",
    )(lengths, scale, terms_r, own, *others)
    return dqp_out, dq_all, dkp, dvp, dkr, dvr


def solution(mesh):
    rows = P("prompt", "resp", None)
    resp_rows = P("prompt", None, "resp", None)
    return jax.shard_map(
        per_device,
        mesh=mesh,
        in_specs=(
            rows, resp_rows, rows, rows, resp_rows, resp_rows, rows, resp_rows, P("prompt", None),
        ),
        out_specs=(rows, resp_rows, rows, rows, resp_rows, resp_rows),
        check_vma=False,
    )
```

profile of v0, /device:TPU:16, one launch (start us, length us, event | category | flops | bytes accessed | tf_op | source)
XLA Modules:
  0.0 120.0 jit_solution(4432412321170211335)
XLA Ops:
  0.6 0.0 copy-start.2
  0.7 0.9 copy-done.2
  1.5 0.8 copy-done.4
  2.4 0.7 copy-done.6
  3.0 0.7 copy-done.8
  3.8 0.7 copy-done.9
  4.5 1.3 %keys.1 = (bf16[2,2,64,128]{3,2,1,0:T(8,128)(2,1)S(1)}, bf16[8,2,64,128]{3,2,1,0:T(8,128)(2,1)}) custom-call(s32[1,4]{1,0:T(1,128)S(1)} %copy-done.6, bf16[1,4,64,128]{3,2,1,0:T(8,128)(2,1)S(1)} %copy-done.2, bf16[1,4,64,128]{3,2,1,0:T(8,128)(2,1)S(1)} %copy-done.4, bf16[1,64,128]{2,1,0:T(8,128)(2,1)S(1)} %copy-done.8, bf16[1,64,128]{2,1,0:T(8,128)(2,1)S(1)} %copy-done.9), custom_call_target="tpu_custom_call" | custom-call | flops 1048576 | bytes 2097152 | tf_op jit(solution)/shard_map/keys/pallas_call | solution.py:392
  5.8 8.6 %all-to-all-start = ((bf16[8,2,64,128]{3,2,1,0:T(8,128)(2,1)}), bf16[8,2,64,128]{3,2,1,0:T(8,128)(2,1)S(1)}, u32[]{:S(2)}, u32[]{:S(2)}) async-start(bf16[8,2,64,128]{3,2,1,0:T(8,128)(2,1)} %get-tuple-element.39), calls=%async_computation | async-start | bytes 524288 | tf_op jit(solution)/shard_map/all_to_all | solution.py:383
  14.4 0.0 copy-start.3
  14.4 0.0 copy-start.5
  14.4 0.6 queries.1
  15.0 1.6 %collective-permute-start.1 = (bf16[2,64,1024]{2,1,0:T(8,128)(2,1)S(1)}, bf16[2,64,1024]{2,1,0:T(8,128)(2,1)S(1)}, u32[]{:S(2)}, u32[]{:S(2)}) collective-permute-start(bf16[2,64,1024]{2,1,0:T(8,128)(2,1)S(1)} %queries.1), channel_id=1, source_target_pairs={{0,8},{1,9},{2,10},{3,11},{4,12},{5,13},{6,14},{7,15},{8,0},{9,1},... | collective-permute-start | bytes 786440 | tf_op jit(solution)/shard_map/ppermute | solution.py:380
  16.6 0.5 collective-permute-start
  17.1 7.1 %collective-permute-done.got = bf16[2,2,64,128]{3,2,1,0:T(8,128)(2,1)S(1)} collective-permute-done((bf16[2,2,64,128]{3,2,1,0:T(8,128)(2,1)S(1)}, bf16[2,2,64,128]{3,2,1,0:T(8,128)(2,1)S(1)}, u32[]{:S(2)}, u32[]{:S(2)}) %collective-permute-start) | collective-permute-done | bytes 65568 | tf_op jit(solution)/shard_map/ppermute | solution.py:380
  24.2 0.0 collective-permute-done.1._.q_got
  24.3 1.7 %block.1 = (bf16[8,2,2,2,64,128]{5,4,3,2,1,0:T(8,128)(2,1)}, f32[8,128]{1,0:T(8,128)S(1)}) custom-call(s32[1,4]{1,0:T(1,128)S(1)} %copy-done.7, bf16[1,4,64,128]{3,2,1,0:T(8,128)(2,1)S(1)} %copy-done.3, bf16[1,4,64,128]{3,2,1,0:T(8,128)(2,1)S(1)} %copy-done.5, bf16[2,2,64,128]{3,2,1,0:T(8,128)(2,1)S(1)} %collective-permute-done.got, ...), custom_call_target="tpu_custom_call" | custom-call | flops 1048576 | bytes 2097152 | tf_op jit(solution)/shard_map/block/pallas_call | solution.py:402
  25.9 0.3 all-to-all-done.kv_own.kv
  26.2 6.7 %all-to-all-start.1 = ((bf16[8,2,2,2,64,128]{5,4,3,2,1,0:T(8,128)(2,1)}), bf16[8,2,2,2,64,128]{5,4,3,2,1,0:T(8,128)(2,1)S(1)}, u32[]{:S(2)}, u32[]{:S(2)}) async-start(bf16[8,2,2,2,64,128]{5,4,3,2,1,0:T(8,128)(2,1)} %get-tuple-element.43), calls=%async_computation.1 | async-start | bytes 2097152 | tf_op jit(solution)/shard_map/all_to_all | solution.py:383
  33.0 0.0 copy-start.10
  33.0 0.0 copy-start.11
  33.0 0.6 douts.1
  33.6 1.6 %collective-permute-start.6 = (bf16[2,64,1024]{2,1,0:T(8,128)(2,1)S(1)}, bf16[2,64,1024]{2,1,0:T(8,128)(2,1)S(1)}, u32[]{:S(2)}, u32[]{:S(2)}) collective-permute-start(bf16[2,64,1024]{2,1,0:T(8,128)(2,1)S(1)} %douts.1), channel_id=1, source_target_pairs={{0,8},{1,9},{2,10},{3,11},{4,12},{5,13},{6,14},{7,15},{8,0},{9,1},... | collective-permute-start | bytes 786440 | tf_op jit(solution)/shard_map/ppermute | solution.py:380
  35.2 0.5 collective-permute-start.7
  35.7 0.0 collective-permute-start.2
  35.7 1.2 collective-permute-done.2
  36.9 3.0 %collective-permute-start.3 = (f32[8,128]{1,0:T(8,128)S(1)}, f32[8,128]{1,0:T(8,128)S(1)}, u32[]{:S(2)}, u32[]{:S(2)}) collective-permute-start(f32[8,128]{1,0:T(8,128)S(1)} %add.12), channel_id=1, source_target_pairs={{0,32},{16,48},{32,0},{48,16},{64,96},{80,112},{96,64},{112,80},{1... | collective-permute-start | bytes 12296 | tf_op jit(solution)/shard_map/ppermute | solution.py:408
  39.9 8.0 %collective-permute-done.3 = f32[8,128]{1,0:T(8,128)S(1)} collective-permute-done((f32[8,128]{1,0:T(8,128)S(1)}, f32[8,128]{1,0:T(8,128)S(1)}, u32[]{:S(2)}, u32[]{:S(2)}) %collective-permute-start.3) | collective-permute-done | bytes 4128 | tf_op jit(solution)/shard_map/ppermute | solution.py:408
  47.9 1.3 %collective-permute-start.4 = (f32[8,128]{1,0:T(8,128)S(1)}, f32[8,128]{1,0:T(8,128)S(1)}, u32[]{:S(2)}, u32[]{:S(2)}) collective-permute-start(f32[8,128]{1,0:T(8,128)S(1)} %add.13), channel_id=1, source_target_pairs={{0,64},{16,80},{32,96},{48,112},{64,0},{80,16},{96,32},{112,48},{1... | collective-permute-start | bytes 12296 | tf_op jit(solution)/shard_map/ppermute | solution.py:408
  49.1 2.3 %collective-permute-done.4 = f32[8,128]{1,0:T(8,128)S(1)} collective-permute-done((f32[8,128]{1,0:T(8,128)S(1)}, f32[8,128]{1,0:T(8,128)S(1)}, u32[]{:S(2)}, u32[]{:S(2)}) %collective-permute-start.4) | collective-permute-done | bytes 4128 | tf_op jit(solution)/shard_map/ppermute | solution.py:408
  51.5 0.3 collective-permute-start.5
  51.8 4.8 %collective-permute-done.5 = f32[8,128]{1,0:T(8,128)S(1)} collective-permute-done((f32[8,128]{1,0:T(8,128)S(1)}, f32[8,128]{1,0:T(8,128)S(1)}, u32[]{:S(2)}, u32[]{:S(2)}) %collective-permute-start.5) | collective-permute-done | bytes 4128 | tf_op jit(solution)/shard_map/ppermute | solution.py:408
  56.6 0.0 collective-permute-done.6.d_got
  56.6 0.0 collective-permute-done.7.kv_pair.kv
  56.6 4.6 %prefix.1 = (bf16[4,512,128]{2,1,0:T(8,128)(2,1)S(1)}, bf16[4,512,128]{2,1,0:T(8,128)(2,1)S(1)}, f32[4,8,512]{2,1,0:T(8,128)S(1)}, f32[64,1024]{1,0:T(8,128)S(1)}, f32[2,8,2,64,128]{4,3,2,1,0:T(8,128)S(1)}) custom-call(s32[1,4]{1,0:T(1,128)S(1)} %copy-done.7, bf16[1,4,64,1024]{3,2,1,0:T(8,128)(2,1)S(1)} %copy-done, bf16[1,4,64,1024]{3,2,1,0:T(8,128)(2,1)S(1)} %copy-done.1, ...), custom_call_target="tpu_custom_call" | custom-call | flops 5368709120 | bytes 2097152 | tf_op jit(solution)/shard_map/prefix/pallas_call | solution.py:410
  61.2 1.0 copy-done.12
  62.2 0.8 copy-done.17
  63.0 0.7 copy-done.20
  63.7 0.0 all-to-all-done.1.kv
  63.7 1.0 copy-done.18
  64.7 6.8 %resp.1 = (f32[8,128]{1,0:T(8,128)S(1)}, f32[4,8,512]{2,1,0:T(8,128)S(1)}, f32[4,512,128]{2,1,0:T(8,128)S(1)}, bf16[16,2,2,64,128]{4,3,2,1,0:T(8,128)(2,1)}) custom-call(s32[1,4]{1,0:T(1,128)S(1)} %copy-done.7, f32[8,128]{1,0:T(8,128)S(1)} %add.15.total, bf16[4,512,128]{2,1,0:T(8,128)(2,1)S(1)} %get-tuple-element.40.q_st, ...), custom_call_target="tpu_custom_call" | custom-call | flops 4294967296 | bytes 2097152 | tf_op jit(solution)/shard_map/resp/pallas_call | solution.py:417
  71.6 1.0 copy-done.15
  72.5 7.8 %all-to-all-start.2 = ((bf16[16,2,2,64,128]{4,3,2,1,0:T(8,128)(2,1)}), bf16[16,2,2,64,128]{4,3,2,1,0:T(8,128)(2,1)S(1)}, u32[]{:S(2)}, u32[]{:S(2)}) async-start(bf16[16,2,2,64,128]{4,3,2,1,0:T(8,128)(2,1)} %get-tuple-element.53), calls=%async_computation.2 | async-start | bytes 2097152 | tf_op jit(solution)/shard_map/all_to_all | solution.py:422
  80.4 1.2 %copy-done.13 = f32[2,8,2,64,128]{4,3,2,1,0:T(8,128)S(1)} copy-done((f32[2,8,2,64,128]{4,3,2,1,0:T(8,128)S(1)}, f32[2,8,2,64,128]{4,3,2,1,0:T(8,128)}, u32[]{:S(2)}) %copy-start.13) | copy-done | bytes 1048600
  81.6 1.2 %copy-done.16 = f32[4,512,128]{2,1,0:T(8,128)S(1)} copy-done((f32[4,512,128]{2,1,0:T(8,128)S(1)}, f32[4,512,128]{2,1,0:T(8,128)}, u32[]{:S(2)}) %copy-start.16) | copy-done | bytes 1048600
  82.8 3.7 %pair.1 = (f32[4,512,128]{2,1,0:T(8,128)S(1)}, bf16[8,2,64,128]{3,2,1,0:T(8,128)(2,1)S(1)}) custom-call(s32[1,4]{1,0:T(1,128)S(1)} %copy-done.7, bf16[4,512,128]{2,1,0:T(8,128)(2,1)S(1)} %get-tuple-element.40.q_st, bf16[4,512,128]{2,1,0:T(8,128)(2,1)S(1)} %copy-done.19, f32[4,8,512]{2,1,0:T(8,128)S(1)} %get-tuple-element.45.logs, ...), custom_call_target="tpu_custom_call" | custom-call | flops 4294967296 | bytes 2097152 | tf_op jit(solution)/shard_map/pair/pallas_call | solution.py:423
  86.5 2.2 %collective-permute-start.9 = (bf16[8,2,64,128]{3,2,1,0:T(8,128)(2,1)S(1)}, bf16[8,2,64,128]{3,2,1,0:T(8,128)(2,1)S(1)}, u32[]{:S(2)}, u32[]{:S(2)}) collective-permute-start(bf16[8,2,64,128]{3,2,1,0:T(8,128)(2,1)S(1)} %get-tuple-element.55), channel_id=1, source_target_pairs={{0,8},{1,9},{2,10},{3,11},{4,12},{5,13},{6,14},{7,15},{8,0},{9,1},... | collective-permute-start | bytes 786440 | tf_op jit(solution)/shard_map/ppermute | solution.py:380
  88.7 4.3 %own.1 = (bf16[1,64,1024]{2,1,0:T(8,128)(2,1)}, bf16[2,64,1024]{2,1,0:T(8,128)(2,1)S(1)}, bf16[2,64,1024]{2,1,0:T(8,128)(2,1)S(1)}, f32[8,2,64,128]{3,2,1,0:T(8,128)S(1)}) custom-call(s32[1,4]{1,0:T(1,128)S(1)} %copy-done.7, f32[8,128]{1,0:T(8,128)S(1)} %get-tuple-element.44.scale, bf16[4,512,128]{2,1,0:T(8,128)(2,1)S(1)} %get-tuple-element.40.q_st, ...), custom_call_target="tpu_custom_call" | custom-call | flops 4294967296 | bytes 2097152 | tf_op jit(solution)/shard_map/own/pallas_call | solution.py:428
  93.1 0.1 collective-permute-start.8
  93.2 7.0 %collective-permute-done.9.g_got = bf16[8,2,64,128]{3,2,1,0:T(8,128)(2,1)S(1)} collective-permute-done((bf16[8,2,64,128]{3,2,1,0:T(8,128)(2,1)S(1)}, bf16[8,2,64,128]{3,2,1,0:T(8,128)(2,1)S(1)}, u32[]{:S(2)}, u32[]{:S(2)}) %collective-permute-start.9) | collective-permute-done | bytes 262176 | tf_op jit(solution)/shard_map/ppermute | solution.py:380
  100.3 1.9 %collective-permute-start.10 = (bf16[2,64,128]{2,1,0:T(8,128)(2,1)S(1)}, bf16[2,64,128]{2,1,0:T(8,128)(2,1)S(1)}, u32[]{:S(2)}, u32[]{:S(2)}) collective-permute-start(bf16[2,64,128]{2,1,0:T(8,128)(2,1)S(1)} %get-tuple-element.57), channel_id=1, source_target_pairs={{0,1},{1,2},{2,3},{3,4},{4,5},{5,6},{6,7},{7,0},{8,9},{9,10},{10,1... | collective-permute-start | bytes 98312 | tf_op jit(solution)/shard_map/ppermute | solution.py:441
  102.2 1.4 %collective-permute-start.11 = (bf16[2,64,128]{2,1,0:T(8,128)(2,1)S(1)}, bf16[2,64,128]{2,1,0:T(8,128)(2,1)S(1)}, u32[]{:S(2)}, u32[]{:S(2)}) collective-permute-start(bf16[2,64,128]{2,1,0:T(8,128)(2,1)S(1)} %get-tuple-element.58), channel_id=1, source_target_pairs={{0,2},{1,3},{2,4},{3,5},{4,6},{5,7},{6,0},{7,1},{8,10},{9,11},{10,... | collective-permute-start | bytes 98312 | tf_op jit(solution)/shard_map/ppermute | solution.py:441
  103.6 2.0 %collective-permute-start.12 = (bf16[2,64,128]{2,1,0:T(8,128)(2,1)S(1)}, bf16[2,64,128]{2,1,0:T(8,128)(2,1)S(1)}, u32[]{:S(2)}, u32[]{:S(2)}) collective-permute-start(bf16[2,64,128]{2,1,0:T(8,128)(2,1)S(1)} %get-tuple-element.59), channel_id=1, source_target_pairs={{0,3},{1,4},{2,5},{3,6},{4,7},{5,0},{6,1},{7,2},{8,11},{9,12},{10,... | collective-permute-start | bytes 98312 | tf_op jit(solution)/shard_map/ppermute | solution.py:441
  105.6 2.6 %collective-permute-start.13 = (bf16[2,64,128]{2,1,0:T(8,128)(2,1)S(1)}, bf16[2,64,128]{2,1,0:T(8,128)(2,1)S(1)}, u32[]{:S(2)}, u32[]{:S(2)}) collective-permute-start(bf16[2,64,128]{2,1,0:T(8,128)(2,1)S(1)} %get-tuple-element.60), channel_id=1, source_target_pairs={{0,4},{1,5},{2,6},{3,7},{4,0},{5,1},{6,2},{7,3},{8,12},{9,13},{10,... | collective-permute-start | bytes 98312 | tf_op jit(solution)/shard_map/ppermute | solution.py:441
  108.2 2.3 %collective-permute-start.14 = (bf16[2,64,128]{2,1,0:T(8,128)(2,1)S(1)}, bf16[2,64,128]{2,1,0:T(8,128)(2,1)S(1)}, u32[]{:S(2)}, u32[]{:S(2)}) collective-permute-start(bf16[2,64,128]{2,1,0:T(8,128)(2,1)S(1)} %get-tuple-element.61), channel_id=1, source_target_pairs={{0,5},{1,6},{2,7},{3,0},{4,1},{5,2},{6,3},{7,4},{8,13},{9,14},{10,... | collective-permute-start | bytes 98312 | tf_op jit(solution)/shard_map/ppermute | solution.py:441
  110.5 0.0 collective-permute-done.10.rest_0_
  110.5 4.1 %collective-permute-start.15 = (bf16[2,64,128]{2,1,0:T(8,128)(2,1)S(1)}, bf16[2,64,128]{2,1,0:T(8,128)(2,1)S(1)}, u32[]{:S(2)}, u32[]{:S(2)}) collective-permute-start(bf16[2,64,128]{2,1,0:T(8,128)(2,1)S(1)} %get-tuple-element.62), channel_id=1, source_target_pairs={{0,6},{1,7},{2,0},{3,1},{4,2},{5,3},{6,4},{7,5},{8,14},{9,15},{10,... | collective-permute-start | bytes 98312 | tf_op jit(solution)/shard_map/ppermute | solution.py:441
  114.7 0.0 collective-permute-done.11.rest_1_
  114.7 0.5 collective-permute-start.16
  115.2 1.4 %rows.5 = bf16[1,4,64,1024]{3,2,1,0:T(8,128)(2,1)} custom-call(s32[1,4]{1,0:T(1,128)S(1)} %copy-done.7, bf16[2,64,1024]{2,1,0:T(8,128)(2,1)S(1)} %get-tuple-element.51.own, bf16[2,64,1024]{2,1,0:T(8,128)(2,1)S(1)} %collective-permute-done.8.got), custom_call_target="tpu_custom_call" | custom-call | flops 1048576 | bytes 2097152 | tf_op jit(solution)/shard_map/rows/pallas_call | solution.py:442
  116.6 0.0 collective-permute-done.12.rest_2_
  116.6 0.0 collective-permute-done.13.rest_3_
  116.6 0.0 collective-permute-done.15.rest_5_
  116.6 2.0 %collective-permute-done.16.rest_6_ = bf16[2,64,128]{2,1,0:T(8,128)(2,1)S(1)} collective-permute-done((bf16[2,64,128]{2,1,0:T(8,128)(2,1)S(1)}, bf16[2,64,128]{2,1,0:T(8,128)(2,1)S(1)}, u32[]{:S(2)}, u32[]{:S(2)}) %collective-permute-start.16) | collective-permute-done | bytes 32800 | tf_op jit(solution)/shard_map/ppermute | solution.py:441
  118.6 1.4 %sums.1 = (f32[1,64,128]{2,1,0:T(8,128)}, f32[1,64,128]{2,1,0:T(8,128)}, f32[1,4,64,128]{3,2,1,0:T(8,128)}, f32[1,4,64,128]{3,2,1,0:T(8,128)}) custom-call(s32[1,4]{1,0:T(1,128)S(1)} %copy-done.7, f32[8,128]{1,0:T(8,128)S(1)} %get-tuple-element.44.scale, bf16[16,2,2,64,128]{4,3,2,1,0:T(8,128)(2,1)S(1)} %all-to-all-done.2.terms, ...), custom_call_target="tpu_custom_call" | custom-call | flops 1048576 | bytes 2097152 | tf_op jit(solution)/shard_map/sums/pallas_call | solution.py:447
  (35 shorter events, 0.1 us)
Async XLA Ops:
  0.6 13.7 %copy-start = (bf16[1,4,64,1024]{3,2,1,0:T(8,128)(2,1)S(1)}, bf16[1,4,64,1024]{3,2,1,0:T(8,128)(2,1)}, u32[]{:S(2)}) copy-start(bf16[1,4,64,1024]{3,2,1,0:T(8,128)(2,1)} %qr.1) | copy-start | bytes 1572868
  0.6 0.9 copy-start.2
  1.5 0.8 copy-start.4
  2.4 0.7 copy-start.6
  3.0 0.7 copy-start.8
  3.8 0.7 copy-start.9
  5.8 8.6 %copy-start.7 = (s32[1,4]{1,0:T(1,128)S(1)}, s32[1,4]{1,0:T(1,128)}, u32[]{:S(2)}) copy-start(s32[1,4]{1,0:T(1,128)} %lengths.19) | copy-start | bytes 52
  5.8 20.5 %all-to-all-start = ((bf16[8,2,64,128]{3,2,1,0:T(8,128)(2,1)}), bf16[8,2,64,128]{3,2,1,0:T(8,128)(2,1)S(1)}, u32[]{:S(2)}, u32[]{:S(2)}) async-start(bf16[8,2,64,128]{3,2,1,0:T(8,128)(2,1)} %get-tuple-element.39), calls=%async_computation | async-start | bytes 524288 | tf_op jit(solution)/shard_map/all_to_all | solution.py:383
  14.4 9.9 %copy-start.3 = (bf16[1,4,64,128]{3,2,1,0:T(8,128)(2,1)S(1)}, bf16[1,4,64,128]{3,2,1,0:T(8,128)(2,1)}, u32[]{:S(2)}) copy-start(bf16[1,4,64,128]{3,2,1,0:T(8,128)(2,1)} %kr.3) | copy-start | bytes 196612
  14.4 9.9 %copy-start.5 = (bf16[1,4,64,128]{3,2,1,0:T(8,128)(2,1)S(1)}, bf16[1,4,64,128]{3,2,1,0:T(8,128)(2,1)}, u32[]{:S(2)}) copy-start(bf16[1,4,64,128]{3,2,1,0:T(8,128)(2,1)} %vr.3) | copy-start | bytes 196612
  15.0 9.3 %collective-permute-start.1 = (bf16[2,64,1024]{2,1,0:T(8,128)(2,1)S(1)}, bf16[2,64,1024]{2,1,0:T(8,128)(2,1)S(1)}, u32[]{:S(2)}, u32[]{:S(2)}) collective-permute-start(bf16[2,64,1024]{2,1,0:T(8,128)(2,1)S(1)} %queries.1), channel_id=1, source_target_pairs={{0,8},{1,9},{2,10},{3,11},{4,12},{5,13},{6,14},{7,15},{8,0},{9,1},... | collective-permute-start | bytes 786440 | tf_op jit(solution)/shard_map/ppermute | solution.py:380
  16.6 7.7 %collective-permute-start = (bf16[2,2,64,128]{3,2,1,0:T(8,128)(2,1)S(1)}, bf16[2,2,64,128]{3,2,1,0:T(8,128)(2,1)S(1)}, u32[]{:S(2)}, u32[]{:S(2)}) collective-permute-start(bf16[2,2,64,128]{3,2,1,0:T(8,128)(2,1)S(1)} %get-tuple-element.37), channel_id=1, source_target_pairs={{0,8},{1,9},{2,10},{3,11},{4,12},{5,13},{6,14},{7,15},{8,0},{9,1},... | collective-permute-start | bytes 196616 | tf_op jit(solution)/shard_map/ppermute | solution.py:380
  26.2 6.7 %copy-start.1 = (bf16[1,4,64,1024]{3,2,1,0:T(8,128)(2,1)S(1)}, bf16[1,4,64,1024]{3,2,1,0:T(8,128)(2,1)}, u32[]{:S(2)}) copy-start(bf16[1,4,64,1024]{3,2,1,0:T(8,128)(2,1)} %dr.1) | copy-start | bytes 1572868
  26.2 37.5 %all-to-all-start.1 = ((bf16[8,2,2,2,64,128]{5,4,3,2,1,0:T(8,128)(2,1)}), bf16[8,2,2,2,64,128]{5,4,3,2,1,0:T(8,128)(2,1)S(1)}, u32[]{:S(2)}, u32[]{:S(2)}) async-start(bf16[8,2,2,2,64,128]{5,4,3,2,1,0:T(8,128)(2,1)} %get-tuple-element.43), calls=%async_computation.1 | async-start | bytes 2097152 | tf_op jit(solution)/shard_map/all_to_all | solution.py:383
  33.0 23.6 %copy-start.10 = (bf16[1,64,1024]{2,1,0:T(8,128)(2,1)S(1)}, bf16[1,64,1024]{2,1,0:T(8,128)(2,1)}, u32[]{:S(2)}) copy-start(bf16[1,64,1024]{2,1,0:T(8,128)(2,1)} %qp.1) | copy-start | bytes 393220
  33.0 23.6 %copy-start.11 = (bf16[1,64,1024]{2,1,0:T(8,128)(2,1)S(1)}, bf16[1,64,1024]{2,1,0:T(8,128)(2,1)}, u32[]{:S(2)}) copy-start(bf16[1,64,1024]{2,1,0:T(8,128)(2,1)} %dp.1) | copy-start | bytes 393220
  33.6 23.0 %collective-permute-start.6 = (bf16[2,64,1024]{2,1,0:T(8,128)(2,1)S(1)}, bf16[2,64,1024]{2,1,0:T(8,128)(2,1)S(1)}, u32[]{:S(2)}, u32[]{:S(2)}) collective-permute-start(bf16[2,64,1024]{2,1,0:T(8,128)(2,1)S(1)} %douts.1), channel_id=1, source_target_pairs={{0,8},{1,9},{2,10},{3,11},{4,12},{5,13},{6,14},{7,15},{8,0},{9,1},... | collective-permute-start | bytes 786440 | tf_op jit(solution)/shard_map/ppermute | solution.py:380
  35.2 21.4 %collective-permute-start.7 = (bf16[8,2,64,128]{3,2,1,0:T(8,128)(2,1)S(1)}, bf16[8,2,64,128]{3,2,1,0:T(8,128)(2,1)S(1)}, u32[]{:S(2)}, u32[]{:S(2)}) collective-permute-start(bf16[8,2,64,128]{3,2,1,0:T(8,128)(2,1)S(1)} %all-to-all-done.kv_own.kv), channel_id=1, source_target_pairs={{0,8},{1,9},{2,10},{3,11},{4,12},{5,13},{6,14},{7,15},{8,0},{9,1},... | collective-permute-start | bytes 786440 | tf_op jit(solution)/shard_map/ppermute | solution.py:380
  35.7 1.2 collective-permute-start.2
  36.9 11.0 %collective-permute-start.3 = (f32[8,128]{1,0:T(8,128)S(1)}, f32[8,128]{1,0:T(8,128)S(1)}, u32[]{:S(2)}, u32[]{:S(2)}) collective-permute-start(f32[8,128]{1,0:T(8,128)S(1)} %add.12), channel_id=1, source_target_pairs={{0,32},{16,48},{32,0},{48,16},{64,96},{80,112},{96,64},{112,80},{1... | collective-permute-start | bytes 12296 | tf_op jit(solution)/shard_map/ppermute | solution.py:408
  47.9 3.6 %collective-permute-start.4 = (f32[8,128]{1,0:T(8,128)S(1)}, f32[8,128]{1,0:T(8,128)S(1)}, u32[]{:S(2)}, u32[]{:S(2)}) collective-permute-start(f32[8,128]{1,0:T(8,128)S(1)} %add.13), channel_id=1, source_target_pairs={{0,64},{16,80},{32,96},{48,112},{64,0},{80,16},{96,32},{112,48},{1... | collective-permute-start | bytes 12296 | tf_op jit(solution)/shard_map/ppermute | solution.py:408
  51.5 5.1 %collective-permute-start.5 = (f32[8,128]{1,0:T(8,128)S(1)}, f32[8,128]{1,0:T(8,128)S(1)}, u32[]{:S(2)}, u32[]{:S(2)}) collective-permute-start(f32[8,128]{1,0:T(8,128)S(1)} %add.14), channel_id=1, source_target_pairs={{0,128},{16,144},{32,160},{48,176},{64,192},{80,208},{96,224},{112... | collective-permute-start | bytes 12296 | tf_op jit(solution)/shard_map/ppermute | solution.py:408
  61.2 1.0 copy-start.12
  62.2 0.8 copy-start.17
  63.0 0.7 copy-start.20
  63.7 1.0 copy-start.18
  71.6 1.0 copy-start.15
  72.5 7.8 %copy-start.19 = (bf16[4,512,128]{2,1,0:T(8,128)(2,1)S(1)}, bf16[4,512,128]{2,1,0:T(8,128)(2,1)}, u32[]{:S(2)}) copy-start(bf16[4,512,128]{2,1,0:T(8,128)(2,1)} %copy-done.17) | copy-start | bytes 1572868
  72.5 46.0 %all-to-all-start.2 = ((bf16[16,2,2,64,128]{4,3,2,1,0:T(8,128)(2,1)}), bf16[16,2,2,64,128]{4,3,2,1,0:T(8,128)(2,1)S(1)}, u32[]{:S(2)}, u32[]{:S(2)}) async-start(bf16[16,2,2,64,128]{4,3,2,1,0:T(8,128)(2,1)} %get-tuple-element.53), calls=%async_computation.2 | async-start | bytes 2097152 | tf_op jit(solution)/shard_map/all_to_all | solution.py:422
  80.4 1.2 %copy-start.13 = (f32[2,8,2,64,128]{4,3,2,1,0:T(8,128)S(1)}, f32[2,8,2,64,128]{4,3,2,1,0:T(8,128)}, u32[]{:S(2)}) copy-start(f32[2,8,2,64,128]{4,3,2,1,0:T(8,128)} %copy-done.12) | copy-start | bytes 3145732
  81.6 1.2 %copy-start.16 = (f32[4,512,128]{2,1,0:T(8,128)S(1)}, f32[4,512,128]{2,1,0:T(8,128)}, u32[]{:S(2)}) copy-start(f32[4,512,128]{2,1,0:T(8,128)} %copy-done.15) | copy-start | bytes 3145732
  82.8 5.9 %copy-start.14 = (f32[2,8,2,64,128]{4,3,2,1,0:T(8,128)S(1)}, f32[2,8,2,64,128]{4,3,2,1,0:T(8,128)}, u32[]{:S(2)}) copy-start(f32[2,8,2,64,128]{4,3,2,1,0:T(8,128)} %copy-done.12) | copy-start | bytes 3145732
  82.8 5.9 %copy-start.21 = (f32[64,1024]{1,0:T(8,128)S(1)}, f32[64,1024]{1,0:T(8,128)}, u32[]{:S(2)}) copy-start(f32[64,1024]{1,0:T(8,128)} %copy-done.20) | copy-start | bytes 786436
  86.5 13.7 %collective-permute-start.9 = (bf16[8,2,64,128]{3,2,1,0:T(8,128)(2,1)S(1)}, bf16[8,2,64,128]{3,2,1,0:T(8,128)(2,1)S(1)}, u32[]{:S(2)}, u32[]{:S(2)}) collective-permute-start(bf16[8,2,64,128]{3,2,1,0:T(8,128)(2,1)S(1)} %get-tuple-element.55), channel_id=1, source_target_pairs={{0,8},{1,9},{2,10},{3,11},{4,12},{5,13},{6,14},{7,15},{8,0},{9,1},... | collective-permute-start | bytes 786440 | tf_op jit(solution)/shard_map/ppermute | solution.py:380
  93.1 15.1 %collective-permute-start.8 = (bf16[2,64,1024]{2,1,0:T(8,128)(2,1)S(1)}, bf16[2,64,1024]{2,1,0:T(8,128)(2,1)S(1)}, u32[]{:S(2)}, u32[]{:S(2)}) collective-permute-start(bf16[2,64,1024]{2,1,0:T(8,128)(2,1)S(1)} %get-tuple-element.52), channel_id=1, source_target_pairs={{0,8},{1,9},{2,10},{3,11},{4,12},{5,13},{6,14},{7,15},{8,0},{9,1},... | collective-permute-start | bytes 786440 | tf_op jit(solution)/shard_map/ppermute | solution.py:380
  100.3 10.3 %collective-permute-start.10 = (bf16[2,64,128]{2,1,0:T(8,128)(2,1)S(1)}, bf16[2,64,128]{2,1,0:T(8,128)(2,1)S(1)}, u32[]{:S(2)}, u32[]{:S(2)}) collective-permute-start(bf16[2,64,128]{2,1,0:T(8,128)(2,1)S(1)} %get-tuple-element.57), channel_id=1, source_target_pairs={{0,1},{1,2},{2,3},{3,4},{4,5},{5,6},{6,7},{7,0},{8,9},{9,10},{10,1... | collective-permute-start | bytes 98312 | tf_op jit(solution)/shard_map/ppermute | solution.py:441
  102.2 12.5 %collective-permute-start.11 = (bf16[2,64,128]{2,1,0:T(8,128)(2,1)S(1)}, bf16[2,64,128]{2,1,0:T(8,128)(2,1)S(1)}, u32[]{:S(2)}, u32[]{:S(2)}) collective-permute-start(bf16[2,64,128]{2,1,0:T(8,128)(2,1)S(1)} %get-tuple-element.58), channel_id=1, source_target_pairs={{0,2},{1,3},{2,4},{3,5},{4,6},{5,7},{6,0},{7,1},{8,10},{9,11},{10,... | collective-permute-start | bytes 98312 | tf_op jit(solution)/shard_map/ppermute | solution.py:441
  103.6 13.0 %collective-permute-start.12 = (bf16[2,64,128]{2,1,0:T(8,128)(2,1)S(1)}, bf16[2,64,128]{2,1,0:T(8,128)(2,1)S(1)}, u32[]{:S(2)}, u32[]{:S(2)}) collective-permute-start(bf16[2,64,128]{2,1,0:T(8,128)(2,1)S(1)} %get-tuple-element.59), channel_id=1, source_target_pairs={{0,3},{1,4},{2,5},{3,6},{4,7},{5,0},{6,1},{7,2},{8,11},{9,12},{10,... | collective-permute-start | bytes 98312 | tf_op jit(solution)/shard_map/ppermute | solution.py:441
  105.6 11.0 %collective-permute-start.13 = (bf16[2,64,128]{2,1,0:T(8,128)(2,1)S(1)}, bf16[2,64,128]{2,1,0:T(8,128)(2,1)S(1)}, u32[]{:S(2)}, u32[]{:S(2)}) collective-permute-start(bf16[2,64,128]{2,1,0:T(8,128)(2,1)S(1)} %get-tuple-element.60), channel_id=1, source_target_pairs={{0,4},{1,5},{2,6},{3,7},{4,0},{5,1},{6,2},{7,3},{8,12},{9,13},{10,... | collective-permute-start | bytes 98312 | tf_op jit(solution)/shard_map/ppermute | solution.py:441
  108.2 8.4 %collective-permute-start.14 = (bf16[2,64,128]{2,1,0:T(8,128)(2,1)S(1)}, bf16[2,64,128]{2,1,0:T(8,128)(2,1)S(1)}, u32[]{:S(2)}, u32[]{:S(2)}) collective-permute-start(bf16[2,64,128]{2,1,0:T(8,128)(2,1)S(1)} %get-tuple-element.61), channel_id=1, source_target_pairs={{0,5},{1,6},{2,7},{3,0},{4,1},{5,2},{6,3},{7,4},{8,13},{9,14},{10,... | collective-permute-start | bytes 98312 | tf_op jit(solution)/shard_map/ppermute | solution.py:441
  110.5 6.1 %collective-permute-start.15 = (bf16[2,64,128]{2,1,0:T(8,128)(2,1)S(1)}, bf16[2,64,128]{2,1,0:T(8,128)(2,1)S(1)}, u32[]{:S(2)}, u32[]{:S(2)}) collective-permute-start(bf16[2,64,128]{2,1,0:T(8,128)(2,1)S(1)} %get-tuple-element.62), channel_id=1, source_target_pairs={{0,6},{1,7},{2,0},{3,1},{4,2},{5,3},{6,4},{7,5},{8,14},{9,15},{10,... | collective-permute-start | bytes 98312 | tf_op jit(solution)/shard_map/ppermute | solution.py:441
  114.7 3.9 %collective-permute-start.16 = (bf16[2,64,128]{2,1,0:T(8,128)(2,1)S(1)}, bf16[2,64,128]{2,1,0:T(8,128)(2,1)S(1)}, u32[]{:S(2)}, u32[]{:S(2)}) collective-permute-start(bf16[2,64,128]{2,1,0:T(8,128)(2,1)S(1)} %get-tuple-element.63), channel_id=1, source_target_pairs={{0,7},{1,0},{2,1},{3,2},{4,3},{5,4},{6,5},{7,6},{8,15},{9,8},{10,9... | collective-permute-start | bytes 98312 | tf_op jit(solution)/shard_map/ppermute | solution.py:441
where the time goes:
time: 121 us; the launch traced here: 120 us
  starting transfers between devices  49.2 us (41%)
  waiting for transfers between devices  32.7 us (27%)
  Pallas kernels  26.4 us (22%)
  local copies, waits for them, and re-layouts  10.8 us (9%)
    ppermute x4, waiting for transfers between devices, per_device(): lax.ppermute(total, 'prompt', [(i, i ^ step) for i in range(PROMPTS)])  16.2 us
    all_to_all x2, starting transfers between devices, spread(): return lax.all_to_all(value, 'resp', 0, 0, axis_index_groups=columns)  15.3 us
    ppermute x7, starting transfers between devices, per_device(): others.append(lax.ppermute(value, 'resp', moves))  14.9 us
    ppermute x6, waiting for transfers between devices, swap(): return lax.ppermute(value, 'resp', pair)  14.2 us
    unnamed x44, local copies, waits for them, and re-layouts  10.8 us
    all_to_all x1, starting transfers between devices, per_device(): terms_r = lax.all_to_all(grads_r, 'resp', 0, 0)  7.83 us
    pallas_call x1, Pallas kernels, per_device(): call(resp_kernel, 'svvvvv', [shape((8, HD), F32), logs_f32, part, shape((...  6.84 us
    ppermute x6, starting transfers between devices, swap(): return lax.ppermute(value, 'resp', pair)  6.52 us
  transfers between devices with their start and end apart: 20, of which 8 were waited for; matrix products, arithmetic and copies ran while one was open for 0% of the time, Pallas kernels for 14%

commit v1 on v0

v1 whole, which is shorter than its diff:
```python
import jax
import jax.numpy as jnp
from jax import lax
from jax.experimental import pallas as pl
from jax.experimental.pallas import tpu as pltpu
from jax.sharding import PartitionSpec as P

HD = 128
HEADS = 8
ROWS = 64
CHUNK = ROWS * HEADS
ZN = 8
PROMPTS = 16
RESPS = 4
TOKENS = 65536.0
NEG = -1e30
SCALE = HD**-0.5
LOG2E = 1.4426950408889634
TILE_BLOCKS = 4
TILE = TILE_BLOCKS * ROWS
BIG = 24
HALF_ROWS = 6 * ROWS
COUNT_ROWS = 16
VMEM = pl.BlockSpec(memory_space=pltpu.VMEM)
SMEM = pl.BlockSpec(memory_space=pltpu.SMEM)
F32 = jnp.float32
BF16 = jnp.bfloat16


def dot_nt(a, b):
    return lax.dot_general(a, b, (((1,), (1,)), ((), ())), preferred_element_type=F32)


def dot_tn(a, b):
    return lax.dot_general(a, b, (((0,), (0,)), ((), ())), preferred_element_type=F32)


def dot_nn(a, b):
    return lax.dot_general(a, b, (((1,), (0,)), ((), ())), preferred_element_type=F32)


def stack_heads(rows):
    return jnp.concatenate([rows[:, h * HD : (h + 1) * HD] for h in range(HEADS)], axis=0)


def unstack_heads(rows):
    return jnp.concatenate([rows[h * ROWS : (h + 1) * ROWS] for h in range(HEADS)], axis=1)


def place():
    me = lax.axis_index("resp")
    return me >> 3, me & (ZN - 1)


def dealt(lengths):
    size = [lengths[0, i] for i in range(RESPS)]
    rank = []
    for i in range(RESPS):
        before = [
            ((size[j] >= size[i]) if j < i else (size[j] > size[i])).astype(jnp.int32)
            for j in range(RESPS)
            if j != i
        ]
        rank.append(before[0] + before[1] + before[2])
    at = [
        sum(jnp.where(rank[i] == k, i, 0) for i in range(1, RESPS)) for k in range(RESPS)
    ]
    return (at[0], at[3]), (at[1], at[2])


def of_half(both, half):
    return tuple(jnp.where(half == 0, a, b) for a, b in zip(*both))


def keep_mask(key_first, row_first, tile):
    key_pos = key_first + lax.broadcasted_iota(jnp.int32, (tile, CHUNK), 0)
    row_pos = row_first + (lax.broadcasted_iota(jnp.int32, (tile, CHUNK), 1) & (ROWS - 1))
    return key_pos <= row_pos


def stats_step(stats, q, d, kt, vt, keep):
    top, total, mixed = stats
    s = dot_nt(kt, q) * (SCALE * LOG2E)
    g = dot_nt(vt, d)
    if keep is not None:
        s = jnp.where(keep, s, NEG)
    new_top = jnp.maximum(top, jnp.max(s, axis=0, keepdims=True))
    e = jnp.exp2(s - new_top)
    fix = jnp.exp2(top - new_top)
    total = total * fix + jnp.sum(e, axis=0, keepdims=True)
    mixed = mixed * fix + jnp.sum(e * g, axis=0, keepdims=True)
    return new_top, total, mixed


def grads_step(q, d, kt, vt, log_sum, delta, keep):
    s = dot_nt(kt, q) * (SCALE * LOG2E)
    g = dot_nt(vt, d)
    w = jnp.exp2(s - log_sum)
    if keep is not None:
        w = jnp.where(keep, w, 0.0)
    grad_s = (w * (g - delta)).astype(BF16)
    dv = dot_nn(w.astype(BF16), d)
    dk = dot_nn(grad_s, q)
    dq = dot_tn(grad_s, kt)
    return dq, dk, dv


def empty_stats():
    return (
        jnp.full((1, CHUNK), NEG, F32),
        jnp.zeros((1, CHUNK), F32),
        jnp.zeros((1, CHUNK), F32),
    )


def finish(stats):
    top, total, mixed = stats
    return top + jnp.log2(total), mixed / total


def keys_kernel(lengths, kr, vr, kp, vp, mine, sent, digits):
    half, _ = place()
    both = dealt(lengths)
    for out, responses in ((mine, of_half(both, half)), (sent, of_half(both, 1 - half))):
        rows = [kp[0], vp[0]]
        for resp in responses:
            rows += [kr[0, resp], vr[0, resp]]
        for at, value in enumerate(rows):
            out[at * ROWS : (at + 1) * ROWS] = value
    total = lengths[0, 0] + lengths[0, 1] + lengths[0, 2] + lengths[0, 3]
    upper = lax.broadcasted_iota(jnp.int32, digits.shape, 0) < COUNT_ROWS // 2
    digits[...] = jnp.where(upper, total >> 6, total & 63).astype(F32).astype(BF16)


def block_kernel(mine, got, count_a, count_b, block):
    block[:HALF_ROWS] = mine[...]
    block[HALF_ROWS : 2 * HALF_ROWS] = got[...]
    block[2 * HALF_ROWS :] = (count_a[...].astype(F32) + count_b[...].astype(F32)).astype(BF16)


def queries_kernel(lengths, qr, dr, sent):
    half, _ = place()
    for slot, resp in enumerate(of_half(dealt(lengths), 1 - half)):
        sent[0, slot] = qr[0, resp]
        sent[1, slot] = dr[0, resp]


def tile_at(kv, part, tile):
    at = pl.ds(tile * TILE_BLOCKS, TILE_BLOCKS)
    return [kv[at, part, kind].reshape(TILE, HD) for kind in range(2)]


def main_kernel(lengths, qr, dr, got, qp, dp, *rest):
    blocks, rest = rest[:ZN], rest[ZN:]
    factor_out, dqp_out, dq_own, dq_pair, grads, kv, acc, q1, d1, dq1 = rest
    half, z = place()
    digits = jnp.zeros((COUNT_ROWS, HD), F32)
    for step, block in enumerate(blocks):
        digits = digits + block[2 * HALF_ROWS :].astype(F32)
        for which in range(2):
            at = (half ^ which) * ZN + ((z - step) & (ZN - 1))
            rows = block[which * HALF_ROWS : (which + 1) * HALF_ROWS]
            kv[at] = rows.reshape(3, 2, ROWS, HD)
    total = digits[: COUNT_ROWS // 2] * 64.0 + digits[COUNT_ROWS // 2 :]
    factor = TOKENS / (2.0 * total)
    factor_out[...] = factor
    factor = factor[0:1] * SCALE
    acc[...] = jnp.zeros_like(acc)

    def add(part, tile, keys, values, log_sum, delta, keep):
        dq, dk, dv = grads_step(q1[...], d1[...], keys, values, log_sum, delta, keep)
        dq1[...] += dq
        at = pl.ds(tile * TILE_BLOCKS, TILE_BLOCKS)
        acc[at, part, 0] += dk.reshape(TILE_BLOCKS, ROWS, HD)
        acc[at, part, 1] += dv.reshape(TILE_BLOCKS, ROWS, HD)

    def causal(row_first, part, stats):
        last = row_first // TILE
        keep = keep_mask(last * TILE, row_first, TILE)

        def first(tile, now, keep):
            return stats_step(now, q1[...], d1[...], *tile_at(kv, part, tile), keep)

        stats = lax.fori_loop(0, last, lambda tile, now: first(tile, now, None), stats)
        log_sum, delta = finish(first(last, stats, keep))

        def plain(tile, carried):
            add(part, tile, *tile_at(kv, part, tile), log_sum, delta, None)
            return carried

        lax.fori_loop(0, last, plain, 0)
        add(part, last, *tile_at(kv, part, last), log_sum, delta, keep)
        return log_sum, delta

    q1[...] = stack_heads(qp[0])
    d1[...] = stack_heads(dp[0])
    dq1[...] = jnp.zeros_like(dq1)
    causal((half * ZN + z) * ROWS, 0, empty_stats())
    dqp_out[0] = unstack_heads((dq1[...] * factor).astype(BF16))

    responses = of_half(dealt(lengths), half)
    for slot, resp in enumerate(responses):
        length = lengths[0, resp]
        for which in range(2):
            row_first = ((half ^ which) * ZN + z) * ROWS
            queries, douts = ((qr.at[0, resp], dr.at[0, resp]), (got.at[0, slot], got.at[1, slot]))[which]
            out = (dq_own, dq_pair)[which].at[slot]

            @pl.when(row_first >= length)
            def _():
                out[...] = jnp.zeros_like(out)

            @pl.when(row_first < length)
            def _():
                pos = row_first + lax.broadcasted_iota(jnp.int32, douts.shape, 0)
                live = jnp.where(pos < length, douts[...].astype(F32), 0.0).astype(BF16)
                q1[...] = stack_heads(queries[...])
                d1[...] = stack_heads(live)
                dq1[...] = jnp.zeros_like(dq1)
                stats = empty_stats()
                for tile in range(2 * ZN // TILE_BLOCKS):
                    stats = stats_step(stats, q1[...], d1[...], *tile_at(kv, 0, tile), None)
                log_sum, delta = causal(row_first, 1 + slot, stats)
                for tile in range(2 * ZN // TILE_BLOCKS):
                    add(0, tile, *tile_at(kv, 0, tile), log_sum, delta, None)
                out[...] = unstack_heads((dq1[...] * factor).astype(BF16))

    grads[...] = acc[...].astype(BF16)


def rows_kernel(lengths, own, got, out):
    half, _ = place()
    both = dealt(lengths)
    for slot, resp in enumerate(of_half(both, half)):
        out[0, resp] = own[slot]
    for slot, resp in enumerate(of_half(both, 1 - half)):
        out[0, resp] = got[slot]


def sums_kernel(lengths, scale, terms, dkp, dvp, dkr, dvr):
    def summed(sources, part, kind):
        value = terms[sources[0], part, kind].astype(F32)
        for source in sources[1:]:
            value = value + terms[source, part, kind].astype(F32)
        return value

    factor = scale[0:1]
    for kind, out, by in ((0, dkp, factor * SCALE), (1, dvp, factor)):
        out[0] = summed(range(2 * ZN), 0, kind) * by
    for half, responses in enumerate(dealt(lengths)):
        sources = range(half * ZN, (half + 1) * ZN)
        for slot, resp in enumerate(responses):
            for kind, out, by in ((0, dkr, factor * SCALE), (1, dvr, factor)):
                out[0, resp] = summed(sources, 1 + slot, kind) * by


def shape(dims, dtype):
    return jax.ShapeDtypeStruct(dims, dtype)


def call(kernel, kinds, outs, scratch=(), flops=1 << 20, name=None, vmem=8):
    spec = {"s": SMEM, "v": VMEM, "a": pl.BlockSpec(memory_space=pl.ANY)}
    return pl.pallas_call(
        kernel,
        out_shape=outs,
        in_specs=[spec[kind] for kind in kinds],
        out_specs=[VMEM] * len(outs),
        scratch_shapes=list(scratch),
        name=name,
        cost_estimate=pl.CostEstimate(flops=flops, bytes_accessed=2 << 20, transcendentals=0),
        compiler_params=pltpu.CompilerParams(vmem_limit_bytes=vmem << 20),
    )


def per_device(
    q_prefix, q_resp, k_prefix, v_prefix, k_resp, v_resp, dout_prefix, dout_resp, lengths
):
    pair = [(i, (i + ZN) % (2 * ZN)) for i in range(2 * ZN)]

    def swap(value):
        return lax.ppermute(value, "resp", pair)

    def shift(value, by):
        moves = [(c + i, c + (i + by) % ZN) for c in (0, ZN) for i in range(ZN)]
        return lax.ppermute(value, "resp", moves)

    rows_bf16 = shape((2, ROWS, HEADS * HD), BF16)
    half_keys = shape((HALF_ROWS, HD), BF16)
    mine, sent, digits = call(
        keys_kernel, "svvvv", [half_keys, half_keys, shape((COUNT_ROWS, HD), BF16)],
        name="keys", vmem=60,
    )(lengths, k_resp, v_resp, k_prefix, v_prefix)
    kv_got = swap(sent)
    counts = []
    for ahead in (0, ZN):
        moves = [
            (p * 2 * ZN + i, ((p - i % ZN - ahead) % PROMPTS) * 2 * ZN + i)
            for p in range(PROMPTS)
            for i in range(2 * ZN)
        ]
        counts.append(lax.ppermute(digits, ("prompt", "resp"), moves))
    (q_sent,) = call(
        queries_kernel, "svv", [shape((2, 2, ROWS, HEADS * HD), BF16)], name="queries", vmem=60
    )(lengths, q_resp, dout_resp)
    got = swap(q_sent)
    (block,) = call(
        block_kernel, "vvvv", [shape((2 * HALF_ROWS + COUNT_ROWS, HD), BF16)], name="block"
    )(mine, kv_got, *counts)
    blocks = [block] * ZN
    for step in range(1, ZN // 2 + 1):
        blocks[step] = shift(blocks[step - 1], 1)
        if step < ZN // 2:
            blocks[ZN - step] = shift(blocks[(ZN - step + 1) % ZN], -1)

    terms = shape((2 * ZN, 3, 2, ROWS, HD), BF16)
    scale, dqp_out, dq_own, dq_pair, grads = call(
        main_kernel, "s" + "v" * (ZN + 5),
        [shape((8, HD), F32), shape((1, ROWS, HEADS * HD), BF16), rows_bf16, rows_bf16, terms],
        [pltpu.VMEM((2 * ZN, 3, 2, ROWS, HD), BF16), pltpu.VMEM((2 * ZN, 3, 2, ROWS, HD), F32),
         pltpu.VMEM((CHUNK, HD), BF16), pltpu.VMEM((CHUNK, HD), BF16),
         pltpu.VMEM((CHUNK, HD), F32)],
        9 << 30, "main", BIG,
    )(lengths, q_resp, dout_resp, got, q_prefix, dout_prefix, *blocks)
    terms = lax.all_to_all(grads, "resp", 0, 0)
    dq_got = swap(dq_pair)
    (dq_all,) = call(
        rows_kernel, "svv", [shape((1, RESPS, ROWS, HEADS * HD), BF16)], name="rows"
    )(lengths, dq_own, dq_got)
    prefix_out = shape((1, ROWS, HD), F32)
    resp_out = shape((1, RESPS, ROWS, HD), F32)
    dkp, dvp, dkr, dvr = call(
        sums_kernel, "svv", [prefix_out, prefix_out, resp_out, resp_out],
        name="sums",
    )(lengths, scale, terms)
    return dqp_out, dq_all, dkp, dvp, dkr, dvr


def solution(mesh):
    rows = P("prompt", "resp", None)
    resp_rows = P("prompt", None, "resp", None)
    return jax.shard_map(
        per_device,
        mesh=mesh,
        in_specs=(
            rows, resp_rows, rows, rows, resp_rows, resp_rows, rows, resp_rows, P("prompt", None),
        ),
        out_specs=(rows, resp_rows, rows, rows, resp_rows, resp_rows),
        check_vma=False,
    )
```

time: 121 us -> 104 us (0.86)
  the two profiles are of different devices: /device:TPU:16 before, /device:TPU:24 now
where the time goes in v1:
time: 104 us; the launch traced here: 105 us
  waiting for transfers between devices  54.8 us (53%)
  starting transfers between devices  26.3 us (25%)
  Pallas kernels  21.8 us (21%)
    all_to_all x1, waiting for transfers between devices, per_device(): terms = lax.all_to_all(grads, 'resp', 0, 0)  22.3 us
    ppermute x7, waiting for transfers between devices, shift(): return lax.ppermute(value, 'resp', moves)  18.3 us
    ppermute x7, starting transfers between devices, shift(): return lax.ppermute(value, 'resp', moves)  16.4 us
    pallas_call x1, Pallas kernels, per_device(): call(main_kernel, 's' + 'v' * (ZN + 5), [shape((8, HD), F32), shape((1, R...  15.3 us
    ppermute x3, waiting for transfers between devices, swap(): return lax.ppermute(value, 'resp', pair)  11.4 us
    all_to_all x1, starting transfers between devices, per_device(): terms = lax.all_to_all(grads, 'resp', 0, 0)  3.71 us
    ppermute x3, starting transfers between devices, swap(): return lax.ppermute(value, 'resp', pair)  3.66 us
    ppermute x2, waiting for transfers between devices, per_device(): counts.append(lax.ppermute(digits, ('prompt', 'resp'), moves))  2.75 us
  transfers between devices with their start and end apart: 13, of which 10 were waited for; matrix products, arithmetic and copies ran while one was open for 0% of the time, Pallas kernels for 3%

profile of v1, /device:TPU:24, one launch (start us, length us, event | category | flops | bytes accessed | tf_op | source)
XLA Modules:
  0.0 104.6 jit_solution(8628897123087708704)
XLA Ops:
  0.6 0.0 copy-start.1
  0.6 0.0 copy-start
  0.7 1.7 %keys.1 = (bf16[384,128]{1,0:T(8,128)(2,1)}, bf16[384,128]{1,0:T(8,128)(2,1)}, bf16[16,128]{1,0:T(8,128)(2,1)}) custom-call(s32[1,4]{1,0:T(1,128)} %lengths.9, bf16[1,4,64,128]{3,2,1,0:T(8,128)(2,1)} %kr.1, bf16[1,4,64,128]{3,2,1,0:T(8,128)(2,1)} %vr.1, bf16[1,64,128]{2,1,0:T(8,128)(2,1)} %kp.1, bf16[1,64,128]{2,1,0:T(8,128)(2,1)} %vp.1), custom_call_target="tpu_custom_call" | custom-call | flops 1048576 | bytes 2097152 | tf_op jit(solution)/shard_map/keys/pallas_call | solution.py:289
  2.3 1.5 %collective-permute-start.1 = (bf16[384,128]{1,0:T(8,128)(2,1)}, bf16[384,128]{1,0:T(8,128)(2,1)S(1)}, u32[]{:S(2)}, u32[]{:S(2)}) collective-permute-start(bf16[384,128]{1,0:T(8,128)(2,1)} %get-tuple-element.19), channel_id=1, source_target_pairs={{0,8},{1,9},{2,10},{3,11},{4,12},{5,13},{6,14},{7,15},{8,0},{9,1},... | collective-permute-start | bytes 294920 | tf_op jit(solution)/shard_map/ppermute | solution.py:281
  3.8 1.2 %collective-permute-start.3 = (bf16[16,128]{1,0:T(8,128)(2,1)}, bf16[16,128]{1,0:T(8,128)(2,1)S(1)}, u32[]{:S(2)}, u32[]{:S(2)}) collective-permute-start(bf16[16,128]{1,0:T(8,128)(2,1)} %get-tuple-element.20), channel_id=1, source_target_pairs={{0,128},{1,113},{2,98},{3,83},{4,68},{5,53},{6,38},{7,23},{8,136},... | collective-permute-start | bytes 12296 | tf_op jit(solution)/shard_map/ppermute | solution.py:301
  5.1 1.3 %collective-permute-start.2 = (bf16[16,128]{1,0:T(8,128)(2,1)}, bf16[16,128]{1,0:T(8,128)(2,1)S(1)}, u32[]{:S(2)}, u32[]{:S(2)}) collective-permute-start(bf16[16,128]{1,0:T(8,128)(2,1)} %get-tuple-element.20), channel_id=1, source_target_pairs={{0,0},{1,241},{2,226},{3,211},{4,196},{5,181},{6,166},{7,151},{8,8... | collective-permute-start | bytes 12296 | tf_op jit(solution)/shard_map/ppermute | solution.py:301
  6.4 2.8 %collective-permute-done.3.count_b = bf16[16,128]{1,0:T(8,128)(2,1)S(1)} collective-permute-done((bf16[16,128]{1,0:T(8,128)(2,1)}, bf16[16,128]{1,0:T(8,128)(2,1)S(1)}, u32[]{:S(2)}, u32[]{:S(2)}) %collective-permute-start.3) | collective-permute-done | bytes 4128 | tf_op jit(solution)/shard_map/ppermute | solution.py:301
  9.2 0.0 collective-permute-done.2.count_a
  9.2 0.0 collective-permute-done.1.got
  9.2 0.0 copy-start.2
  9.2 0.9 copy-done.2
  10.1 0.0 copy-start.3
  10.1 0.0 copy-start.4
  10.1 0.0 copy-start.5
  10.1 3.1 %collective-permute-start.4 = (bf16[784,128]{1,0:T(8,128)(2,1)S(1)}, bf16[784,128]{1,0:T(8,128)(2,1)S(1)}, u32[]{:S(2)}, u32[]{:S(2)}) collective-permute-start(bf16[784,128]{1,0:T(8,128)(2,1)S(1)} %block.1.rest_0_), channel_id=1, source_target_pairs={{0,1},{1,2},{2,3},{3,4},{4,5},{5,6},{6,7},{7,0},{8,9},{9,10},{10,1... | collective-permute-start | bytes 602120 | tf_op jit(solution)/shard_map/ppermute | solution.py:285
  13.1 6.4 %collective-permute-start.8 = (bf16[784,128]{1,0:T(8,128)(2,1)S(1)}, bf16[784,128]{1,0:T(8,128)(2,1)S(1)}, u32[]{:S(2)}, u32[]{:S(2)}) collective-permute-start(bf16[784,128]{1,0:T(8,128)(2,1)S(1)} %block.1.rest_0_), channel_id=1, source_target_pairs={{0,7},{1,0},{2,1},{3,2},{4,3},{5,4},{6,5},{7,6},{8,15},{9,8},{10,9... | collective-permute-start | bytes 602120 | tf_op jit(solution)/shard_map/ppermute | solution.py:285
  19.5 5.7 %collective-permute-done.4.rest_1_ = bf16[784,128]{1,0:T(8,128)(2,1)S(1)} collective-permute-done((bf16[784,128]{1,0:T(8,128)(2,1)S(1)}, bf16[784,128]{1,0:T(8,128)(2,1)S(1)}, u32[]{:S(2)}, u32[]{:S(2)}) %collective-permute-start.4) | collective-permute-done | bytes 200736 | tf_op jit(solution)/shard_map/ppermute | solution.py:285
  25.2 0.0 collective-permute-start.5
  25.2 2.1 %queries.1 = bf16[2,2,64,1024]{3,2,1,0:T(8,128)(2,1)} custom-call(s32[1,4]{1,0:T(1,128)} %lengths.9, bf16[1,4,64,1024]{3,2,1,0:T(8,128)(2,1)} %qr.3, bf16[1,4,64,1024]{3,2,1,0:T(8,128)(2,1)} %dr.3), custom_call_target="tpu_custom_call" | custom-call | flops 1048576 | bytes 2097152 | tf_op jit(solution)/shard_map/queries/pallas_call | solution.py:302
  27.3 0.3 collective-permute-start
  27.6 0.0 collective-permute-done.8.rest_7_
  27.6 3.2 %collective-permute-start.9 = (bf16[784,128]{1,0:T(8,128)(2,1)S(1)}, bf16[784,128]{1,0:T(8,128)(2,1)S(1)}, u32[]{:S(2)}, u32[]{:S(2)}) collective-permute-start(bf16[784,128]{1,0:T(8,128)(2,1)S(1)} %collective-permute-done.8.rest_7_), channel_id=1, source_target_pairs={{0,7},{1,0},{2,1},{3,2},{4,3},{5,4},{6,5},{7,6},{8,15},{9,8},{10,9... | collective-permute-start | bytes 602120 | tf_op jit(solution)/shard_map/ppermute | solution.py:285
  30.8 2.6 %collective-permute-done.5.rest_2_ = bf16[784,128]{1,0:T(8,128)(2,1)S(1)} collective-permute-done((bf16[784,128]{1,0:T(8,128)(2,1)S(1)}, bf16[784,128]{1,0:T(8,128)(2,1)S(1)}, u32[]{:S(2)}, u32[]{:S(2)}) %collective-permute-start.5) | collective-permute-done | bytes 200736 | tf_op jit(solution)/shard_map/ppermute | solution.py:285
  33.5 0.0 collective-permute-start.6
  33.5 1.4 %collective-permute-done.9.rest_6_ = bf16[784,128]{1,0:T(8,128)(2,1)S(1)} collective-permute-done((bf16[784,128]{1,0:T(8,128)(2,1)S(1)}, bf16[784,128]{1,0:T(8,128)(2,1)S(1)}, u32[]{:S(2)}, u32[]{:S(2)}) %collective-permute-start.9) | collective-permute-done | bytes 200736 | tf_op jit(solution)/shard_map/ppermute | solution.py:285
  34.9 3.7 %collective-permute-start.10 = (bf16[784,128]{1,0:T(8,128)(2,1)S(1)}, bf16[784,128]{1,0:T(8,128)(2,1)S(1)}, u32[]{:S(2)}, u32[]{:S(2)}) collective-permute-start(bf16[784,128]{1,0:T(8,128)(2,1)S(1)} %collective-permute-done.9.rest_6_), channel_id=1, source_target_pairs={{0,7},{1,0},{2,1},{3,2},{4,3},{5,4},{6,5},{7,6},{8,15},{9,8},{10,9... | collective-permute-start | bytes 602120 | tf_op jit(solution)/shard_map/ppermute | solution.py:285
  38.6 2.3 %collective-permute-done.6.rest_3_ = bf16[784,128]{1,0:T(8,128)(2,1)S(1)} collective-permute-done((bf16[784,128]{1,0:T(8,128)(2,1)S(1)}, bf16[784,128]{1,0:T(8,128)(2,1)S(1)}, u32[]{:S(2)}, u32[]{:S(2)}) %collective-permute-start.6) | collective-permute-done | bytes 200736 | tf_op jit(solution)/shard_map/ppermute | solution.py:285
  40.8 0.0 collective-permute-start.7
  40.8 0.6 collective-permute-done.got
  41.5 0.3 collective-permute-done.10.rest_5_
  41.8 6.0 %collective-permute-done.7.rest_4_ = bf16[784,128]{1,0:T(8,128)(2,1)S(1)} collective-permute-done((bf16[784,128]{1,0:T(8,128)(2,1)S(1)}, bf16[784,128]{1,0:T(8,128)(2,1)S(1)}, u32[]{:S(2)}, u32[]{:S(2)}) %collective-permute-start.7) | collective-permute-done | bytes 200736 | tf_op jit(solution)/shard_map/ppermute | solution.py:285
  47.8 0.0 copy-done.1
  47.8 0.0 copy-done
  47.8 0.0 copy-done.3
  47.8 0.0 copy-done.4
  47.8 0.0 copy-done.5
  47.8 15.3 %main.1 = (f32[8,128]{1,0:T(8,128)S(1)}, bf16[1,64,1024]{2,1,0:T(8,128)(2,1)}, bf16[2,64,1024]{2,1,0:T(8,128)(2,1)S(1)}, bf16[2,64,1024]{2,1,0:T(8,128)(2,1)S(1)}, bf16[16,3,2,64,128]{4,3,2,1,0:T(8,128)(2,1)}) custom-call(s32[1,4]{1,0:T(1,128)S(1)} %copy-done.3, bf16[1,4,64,1024]{3,2,1,0:T(8,128)(2,1)S(1)} %copy-done, ...), custom_call_target="tpu_custom_call" | custom-call | flops 9663676416 | bytes 2097152 | tf_op jit(solution)/shard_map/main/pallas_call | solution.py:316
  63.1 3.7 %all-to-all-start = ((bf16[16,3,2,64,128]{4,3,2,1,0:T(8,128)(2,1)}), bf16[16,3,2,64,128]{4,3,2,1,0:T(8,128)(2,1)S(1)}, u32[]{:S(2)}, u32[]{:S(2)}) async-start(bf16[16,3,2,64,128]{4,3,2,1,0:T(8,128)(2,1)} %get-tuple-element.25), calls=%async_computation | async-start | bytes 3145728 | tf_op jit(solution)/shard_map/all_to_all | solution.py:324
  66.8 1.9 %collective-permute-start.11 = (bf16[2,64,1024]{2,1,0:T(8,128)(2,1)S(1)}, bf16[2,64,1024]{2,1,0:T(8,128)(2,1)S(1)}, u32[]{:S(2)}, u32[]{:S(2)}) collective-permute-start(bf16[2,64,1024]{2,1,0:T(8,128)(2,1)S(1)} %get-tuple-element.23), channel_id=1, source_target_pairs={{0,8},{1,9},{2,10},{3,11},{4,12},{5,13},{6,14},{7,15},{8,0},{9,1},... | collective-permute-start | bytes 786440 | tf_op jit(solution)/shard_map/ppermute | solution.py:281
  68.6 10.8 %collective-permute-done.11.got = bf16[2,64,1024]{2,1,0:T(8,128)(2,1)S(1)} collective-permute-done((bf16[2,64,1024]{2,1,0:T(8,128)(2,1)S(1)}, bf16[2,64,1024]{2,1,0:T(8,128)(2,1)S(1)}, u32[]{:S(2)}, u32[]{:S(2)}) %collective-permute-start.11) | collective-permute-done | bytes 262176 | tf_op jit(solution)/shard_map/ppermute | solution.py:281
  79.4 1.4 %rows.1 = bf16[1,4,64,1024]{3,2,1,0:T(8,128)(2,1)} custom-call(s32[1,4]{1,0:T(1,128)S(1)} %copy-done.3, bf16[2,64,1024]{2,1,0:T(8,128)(2,1)S(1)} %get-tuple-element.22.own, bf16[2,64,1024]{2,1,0:T(8,128)(2,1)S(1)} %collective-permute-done.11.got), custom_call_target="tpu_custom_call" | custom-call | flops 1048576 | bytes 2097152 | tf_op jit(solution)/shard_map/rows/pallas_call | solution.py:326
  80.8 22.3 %all-to-all-done.terms = bf16[16,3,2,64,128]{4,3,2,1,0:T(8,128)(2,1)S(1)} async-done(((bf16[16,3,2,64,128]{4,3,2,1,0:T(8,128)(2,1)}), bf16[16,3,2,64,128]{4,3,2,1,0:T(8,128)(2,1)S(1)}, u32[]{:S(2)}, u32[]{:S(2)}) %all-to-all-start) | async-done | bytes 1572896 | tf_op jit(solution)/shard_map/all_to_all | solution.py:324
  103.1 1.4 %sums.1 = (f32[1,64,128]{2,1,0:T(8,128)}, f32[1,64,128]{2,1,0:T(8,128)}, f32[1,4,64,128]{3,2,1,0:T(8,128)}, f32[1,4,64,128]{3,2,1,0:T(8,128)}) custom-call(s32[1,4]{1,0:T(1,128)S(1)} %copy-done.3, f32[8,128]{1,0:T(8,128)S(1)} %get-tuple-element.24.scale, bf16[16,3,2,64,128]{4,3,2,1,0:T(8,128)(2,1)S(1)} %all-to-all-done.terms), custom_call_target="tpu_custom_call" | custom-call | flops 1048576 | bytes 2097152 | tf_op jit(solution)/shard_map/sums/pallas_call | solution.py:331
  (1 shorter events, 0.0 us)
Async XLA Ops:
  0.6 47.1 %copy-start.1 = (bf16[1,4,64,1024]{3,2,1,0:T(8,128)(2,1)S(1)}, bf16[1,4,64,1024]{3,2,1,0:T(8,128)(2,1)}, u32[]{:S(2)}) copy-start(bf16[1,4,64,1024]{3,2,1,0:T(8,128)(2,1)} %dr.3) | copy-start | bytes 1572868
  0.6 47.1 %copy-start = (bf16[1,4,64,1024]{3,2,1,0:T(8,128)(2,1)S(1)}, bf16[1,4,64,1024]{3,2,1,0:T(8,128)(2,1)}, u32[]{:S(2)}) copy-start(bf16[1,4,64,1024]{3,2,1,0:T(8,128)(2,1)} %qr.3) | copy-start | bytes 1572868
  2.3 6.8 %collective-permute-start.1 = (bf16[384,128]{1,0:T(8,128)(2,1)}, bf16[384,128]{1,0:T(8,128)(2,1)S(1)}, u32[]{:S(2)}, u32[]{:S(2)}) collective-permute-start(bf16[384,128]{1,0:T(8,128)(2,1)} %get-tuple-element.19), channel_id=1, source_target_pairs={{0,8},{1,9},{2,10},{3,11},{4,12},{5,13},{6,14},{7,15},{8,0},{9,1},... | collective-permute-start | bytes 294920 | tf_op jit(solution)/shard_map/ppermute | solution.py:281
  3.8 5.3 %collective-permute-start.3 = (bf16[16,128]{1,0:T(8,128)(2,1)}, bf16[16,128]{1,0:T(8,128)(2,1)S(1)}, u32[]{:S(2)}, u32[]{:S(2)}) collective-permute-start(bf16[16,128]{1,0:T(8,128)(2,1)} %get-tuple-element.20), channel_id=1, source_target_pairs={{0,128},{1,113},{2,98},{3,83},{4,68},{5,53},{6,38},{7,23},{8,136},... | collective-permute-start | bytes 12296 | tf_op jit(solution)/shard_map/ppermute | solution.py:301
  5.1 4.1 %collective-permute-start.2 = (bf16[16,128]{1,0:T(8,128)(2,1)}, bf16[16,128]{1,0:T(8,128)(2,1)S(1)}, u32[]{:S(2)}, u32[]{:S(2)}) collective-permute-start(bf16[16,128]{1,0:T(8,128)(2,1)} %get-tuple-element.20), channel_id=1, source_target_pairs={{0,0},{1,241},{2,226},{3,211},{4,196},{5,181},{6,166},{7,151},{8,8... | collective-permute-start | bytes 12296 | tf_op jit(solution)/shard_map/ppermute | solution.py:301
  9.2 0.9 copy-start.2
  10.1 37.7 %copy-start.3 = (s32[1,4]{1,0:T(1,128)S(1)}, s32[1,4]{1,0:T(1,128)}, u32[]{:S(2)}) copy-start(s32[1,4]{1,0:T(1,128)} %lengths.9) | copy-start | bytes 52
  10.1 37.7 %copy-start.4 = (bf16[1,64,1024]{2,1,0:T(8,128)(2,1)S(1)}, bf16[1,64,1024]{2,1,0:T(8,128)(2,1)}, u32[]{:S(2)}) copy-start(bf16[1,64,1024]{2,1,0:T(8,128)(2,1)} %qp.1) | copy-start | bytes 393220
  10.1 37.7 %copy-start.5 = (bf16[1,64,1024]{2,1,0:T(8,128)(2,1)S(1)}, bf16[1,64,1024]{2,1,0:T(8,128)(2,1)}, u32[]{:S(2)}) copy-start(bf16[1,64,1024]{2,1,0:T(8,128)(2,1)} %dp.1) | copy-start | bytes 393220
  10.1 15.1 %collective-permute-start.4 = (bf16[784,128]{1,0:T(8,128)(2,1)S(1)}, bf16[784,128]{1,0:T(8,128)(2,1)S(1)}, u32[]{:S(2)}, u32[]{:S(2)}) collective-permute-start(bf16[784,128]{1,0:T(8,128)(2,1)S(1)} %block.1.rest_0_), channel_id=1, source_target_pairs={{0,1},{1,2},{2,3},{3,4},{4,5},{5,6},{6,7},{7,0},{8,9},{9,10},{10,1... | collective-permute-start | bytes 602120 | tf_op jit(solution)/shard_map/ppermute | solution.py:285
  13.1 14.5 %collective-permute-start.8 = (bf16[784,128]{1,0:T(8,128)(2,1)S(1)}, bf16[784,128]{1,0:T(8,128)(2,1)S(1)}, u32[]{:S(2)}, u32[]{:S(2)}) collective-permute-start(bf16[784,128]{1,0:T(8,128)(2,1)S(1)} %block.1.rest_0_), channel_id=1, source_target_pairs={{0,7},{1,0},{2,1},{3,2},{4,3},{5,4},{6,5},{7,6},{8,15},{9,8},{10,9... | collective-permute-start | bytes 602120 | tf_op jit(solution)/shard_map/ppermute | solution.py:285
  25.2 8.2 %collective-permute-start.5 = (bf16[784,128]{1,0:T(8,128)(2,1)S(1)}, bf16[784,128]{1,0:T(8,128)(2,1)S(1)}, u32[]{:S(2)}, u32[]{:S(2)}) collective-permute-start(bf16[784,128]{1,0:T(8,128)(2,1)S(1)} %collective-permute-done.4.rest_1_), channel_id=1, source_target_pairs={{0,1},{1,2},{2,3},{3,4},{4,5},{5,6},{6,7},{7,0},{8,9},{9,10},{10,1... | collective-permute-start | bytes 602120 | tf_op jit(solution)/shard_map/ppermute | solution.py:285
  27.3 14.2 %collective-permute-start = (bf16[2,2,64,1024]{3,2,1,0:T(8,128)(2,1)}, bf16[2,2,64,1024]{3,2,1,0:T(8,128)(2,1)S(1)}, u32[]{:S(2)}, u32[]{:S(2)}) collective-permute-start(bf16[2,2,64,1024]{3,2,1,0:T(8,128)(2,1)} %queries.1), channel_id=1, source_target_pairs={{0,8},{1,9},{2,10},{3,11},{4,12},{5,13},{6,14},{7,15},{8,0},{9,1},... | collective-permute-start | bytes 1572872 | tf_op jit(solution)/shard_map/ppermute | solution.py:281
  27.6 7.2 %collective-permute-start.9 = (bf16[784,128]{1,0:T(8,128)(2,1)S(1)}, bf16[784,128]{1,0:T(8,128)(2,1)S(1)}, u32[]{:S(2)}, u32[]{:S(2)}) collective-permute-start(bf16[784,128]{1,0:T(8,128)(2,1)S(1)} %collective-permute-done.8.rest_7_), channel_id=1, source_target_pairs={{0,7},{1,0},{2,1},{3,2},{4,3},{5,4},{6,5},{7,6},{8,15},{9,8},{10,9... | collective-permute-start | bytes 602120 | tf_op jit(solution)/shard_map/ppermute | solution.py:285
  33.5 7.4 %collective-permute-start.6 = (bf16[784,128]{1,0:T(8,128)(2,1)S(1)}, bf16[784,128]{1,0:T(8,128)(2,1)S(1)}, u32[]{:S(2)}, u32[]{:S(2)}) collective-permute-start(bf16[784,128]{1,0:T(8,128)(2,1)S(1)} %collective-permute-done.5.rest_2_), channel_id=1, source_target_pairs={{0,1},{1,2},{2,3},{3,4},{4,5},{5,6},{6,7},{7,0},{8,9},{9,10},{10,1... | collective-permute-start | bytes 602120 | tf_op jit(solution)/shard_map/ppermute | solution.py:285
  34.9 6.9 %collective-permute-start.10 = (bf16[784,128]{1,0:T(8,128)(2,1)S(1)}, bf16[784,128]{1,0:T(8,128)(2,1)S(1)}, u32[]{:S(2)}, u32[]{:S(2)}) collective-permute-start(bf16[784,128]{1,0:T(8,128)(2,1)S(1)} %collective-permute-done.9.rest_6_), channel_id=1, source_target_pairs={{0,7},{1,0},{2,1},{3,2},{4,3},{5,4},{6,5},{7,6},{8,15},{9,8},{10,9... | collective-permute-start | bytes 602120 | tf_op jit(solution)/shard_map/ppermute | solution.py:285
  40.8 6.9 %collective-permute-start.7 = (bf16[784,128]{1,0:T(8,128)(2,1)S(1)}, bf16[784,128]{1,0:T(8,128)(2,1)S(1)}, u32[]{:S(2)}, u32[]{:S(2)}) collective-permute-start(bf16[784,128]{1,0:T(8,128)(2,1)S(1)} %collective-permute-done.6.rest_3_), channel_id=1, source_target_pairs={{0,1},{1,2},{2,3},{3,4},{4,5},{5,6},{6,7},{7,0},{8,9},{9,10},{10,1... | collective-permute-start | bytes 602120 | tf_op jit(solution)/shard_map/ppermute | solution.py:285
  63.1 40.1 %all-to-all-start = ((bf16[16,3,2,64,128]{4,3,2,1,0:T(8,128)(2,1)}), bf16[16,3,2,64,128]{4,3,2,1,0:T(8,128)(2,1)S(1)}, u32[]{:S(2)}, u32[]{:S(2)}) async-start(bf16[16,3,2,64,128]{4,3,2,1,0:T(8,128)(2,1)} %get-tuple-element.25), calls=%async_computation | async-start | bytes 3145728 | tf_op jit(solution)/shard_map/all_to_all | solution.py:324
  66.8 12.7 %collective-permute-start.11 = (bf16[2,64,1024]{2,1,0:T(8,128)(2,1)S(1)}, bf16[2,64,1024]{2,1,0:T(8,128)(2,1)S(1)}, u32[]{:S(2)}, u32[]{:S(2)}) collective-permute-start(bf16[2,64,1024]{2,1,0:T(8,128)(2,1)S(1)} %get-tuple-element.23), channel_id=1, source_target_pairs={{0,8},{1,9},{2,10},{3,11},{4,12},{5,13},{6,14},{7,15},{8,0},{9,1},... | collective-permute-start | bytes 786440 | tf_op jit(solution)/shard_map/ppermute | solution.py:281

commit v2 on v1

v2 whole, which is shorter than its diff:
```python
import jax
import jax.numpy as jnp
from jax import lax
from jax.experimental import pallas as pl
from jax.experimental.pallas import tpu as pltpu
from jax.sharding import PartitionSpec as P

HD = 128
HEADS = 8
ROWS = 64
CHUNK = ROWS * HEADS
ZN = 8
PROMPTS = 16
RESPS = 4
TOKENS = 65536.0
NEG = -1e30
SCALE = HD**-0.5
LOG2E = 1.4426950408889634
TILE_BLOCKS = 8
TILE = TILE_BLOCKS * ROWS
BIG = 30
HALF_ROWS = 6 * ROWS
VMEM = pl.BlockSpec(memory_space=pltpu.VMEM)
SMEM = pl.BlockSpec(memory_space=pltpu.SMEM)
F32 = jnp.float32
BF16 = jnp.bfloat16


def dot_nt(a, b):
    return lax.dot_general(a, b, (((1,), (1,)), ((), ())), preferred_element_type=F32)


def dot_tn(a, b):
    return lax.dot_general(a, b, (((0,), (0,)), ((), ())), preferred_element_type=F32)


def dot_nn(a, b):
    return lax.dot_general(a, b, (((1,), (0,)), ((), ())), preferred_element_type=F32)


def stack_heads(rows):
    return jnp.concatenate([rows[:, h * HD : (h + 1) * HD] for h in range(HEADS)], axis=0)


def unstack_heads(rows):
    return jnp.concatenate([rows[h * ROWS : (h + 1) * ROWS] for h in range(HEADS)], axis=1)


def place():
    me = lax.axis_index("resp")
    return me >> 3, me & (ZN - 1)


def dealt(lengths):
    size = [lengths[0, i] for i in range(RESPS)]
    rank = []
    for i in range(RESPS):
        before = [
            ((size[j] >= size[i]) if j < i else (size[j] > size[i])).astype(jnp.int32)
            for j in range(RESPS)
            if j != i
        ]
        rank.append(before[0] + before[1] + before[2])
    at = [
        sum(jnp.where(rank[i] == k, i, 0) for i in range(1, RESPS)) for k in range(RESPS)
    ]
    return (at[1], at[2]), (at[0], at[3])


def of_half(both, half):
    return tuple(jnp.where(half == 0, a, b) for a, b in zip(*both))


def fold(value):
    return value.reshape(value.shape[0] // 8, 8, CHUNK)


def half_rows(out, kr, vr, kp, vp, responses):
    rows = [kp[0], vp[0]]
    for resp in responses:
        rows += [kr[0, resp], vr[0, resp]]
    for at, value in enumerate(rows):
        out[at * ROWS : (at + 1) * ROWS] = value


def keys_kernel(lengths, kr, vr, kp, vp, sent, count):
    half, _ = place()
    half_rows(sent, kr, vr, kp, vp, of_half(dealt(lengths), 1 - half))
    total = lengths[0, 0] + lengths[0, 1] + lengths[0, 2] + lengths[0, 3]
    count[...] = jnp.full(count.shape, total, jnp.int32).astype(F32)


def queries_kernel(lengths, qr, dr, qp, dp, own, sent, done):
    half, z = place()
    both = dealt(lengths)
    pos = (half * ZN + z) * ROWS + lax.broadcasted_iota(jnp.int32, (ROWS, HEADS * HD), 0)
    for out, responses in ((own, of_half(both, half)), (sent, of_half(both, 1 - half))):
        for slot, resp in enumerate(responses):
            live = jnp.where(pos < lengths[0, resp], dr[0, resp].astype(F32), 0.0)
            out[0, slot] = stack_heads(qr[0, resp])
            out[1, slot] = stack_heads(live.astype(BF16))
    own[0, 2] = stack_heads(qp[0])
    own[1, 2] = stack_heads(dp[0])
    done[...] = jnp.zeros_like(done)


def block_kernel(lengths, kr, vr, kp, vp, got, _, block):
    half_rows(block, kr, vr, kp, vp, of_half(dealt(lengths), place()[0]))
    block[HALF_ROWS:] = got[...]


def tile_at(kv, part, tile, size=TILE):
    at = pl.ds(tile * TILE_BLOCKS, size // ROWS)
    return [kv[at, part, kind].reshape(size, HD) for kind in range(2)]


def token_factor(total):
    return TOKENS / (2.0 * total[0:1])


def attend(
    tail, z, kv, q_ref, d_ref, part, high, shared, acc, factor,
    dq_out, dq1, kept_s, kept_g,
):
    q, d = q_ref[...], d_ref[...]
    tiles = [(0, 0), (0, 1)] if shared else []
    base = len(tiles)

    def rows_of(place, size):
        return pl.ds(pl.multiple_of(place * TILE, TILE), size)

    def over_tiles(body, now):
        for own, tile in tiles:
            now = body(now, own, tile, tile, TILE, False)
        now = lax.fori_loop(0, high, lambda tile, now: body(now, part, tile, base + tile, TILE, False), now)
        return body(now, part, high, base + high, tail, True)

    def scores(top, part, tile, place, size, masked):
        keys, _ = tile_at(kv, part, tile, size)
        s = dot_nt(keys, q) * (SCALE * LOG2E)
        if masked:
            ahead = lax.broadcasted_iota(jnp.int32, s.shape, 0) - (
                lax.broadcasted_iota(jnp.int32, s.shape, 1) & (ROWS - 1)
            )
            s = jnp.where(ahead <= z * ROWS, s, NEG)
        kept_s[rows_of(place, size)] = s
        return jnp.maximum(top, jnp.max(fold(s), axis=0))

    top = over_tiles(scores, jnp.full((8, CHUNK), NEG, F32))
    top = jnp.max(top, axis=0, keepdims=True)

    def sums(now, part, tile, place, size, masked):
        _, values = tile_at(kv, part, tile, size)
        at = rows_of(place, size)
        g = dot_nt(values, d)
        e = jnp.exp2(kept_s[at] - top)
        kept_s[at] = e
        kept_g[at] = g
        return now[0] + jnp.sum(fold(e), axis=0), now[1] + jnp.sum(fold(e * g), axis=0)

    now = over_tiles(sums, (jnp.zeros((8, CHUNK), F32), jnp.zeros((8, CHUNK), F32)))
    total, mixed = (jnp.sum(value, axis=0, keepdims=True) for value in now)
    inverse = 1.0 / total
    delta = mixed * inverse

    def grads(now, part, tile, place, size, masked):
        keys, _ = tile_at(kv, part, tile, size)
        at = rows_of(place, size)
        w = kept_s[at] * inverse
        grad_s = (w * (kept_g[at] - delta)).astype(BF16)
        dv = dot_nn(w.astype(BF16), d)
        dk = dot_nn(grad_s, q)
        dq1[...] += dot_tn(keys, grad_s)
        at = pl.ds(tile * TILE_BLOCKS, size // ROWS)
        acc[at, part, 0] += dk.reshape(size // ROWS, ROWS, HD)
        acc[at, part, 1] += dv.reshape(size // ROWS, ROWS, HD)
        return now

    dq1[...] = jnp.zeros_like(dq1)
    over_tiles(grads, 0)
    dq_out[...] = (jnp.transpose(dq1[...]) * factor).astype(BF16)


def main_kernel(lengths, total, own, got, *rest):
    blocks, rest = rest[:ZN], rest[ZN:]
    dqp_out, dq_own, dq_pair, rest = rest[0], rest[1], rest[2], rest[3:]
    terms, (kv, acc, q_st, d_st, dq_st, *work) = rest[:ZN], rest[ZN:]
    half, z = place()
    factor = token_factor(total) * SCALE
    for step, block in enumerate(blocks):
        for which in range(2):
            at = (half ^ which) * ZN + ((z - step) & (ZN - 1))
            rows = block[which * HALF_ROWS : (which + 1) * HALF_ROWS]
            kv[at] = rows.reshape(3, 2, ROWS, HD)
    acc[...] = jnp.zeros_like(acc)
    dq_st[...] = jnp.zeros_like(dq_st)
    for slot in range(2):
        for kind, ref in enumerate((q_st, d_st)):
            ref[2 * slot] = own[kind, slot]
            ref[2 * slot + 1] = got[kind, slot]
    first, second = of_half(dealt(lengths), half)

    def all_rows(tail):
        attend(
            tail, z, kv, own.at[0, 2], own.at[1, 2], 0, half, False, acc, factor, dqp_out, *work
        )

        def one(chunk, carried):
            slot = chunk >> 1
            high = half ^ (chunk & 1)

            @pl.when((high * ZN + z) * ROWS < lengths[0, jnp.where(slot == 0, first, second)])
            def _():
                attend(
                    tail, z, kv, q_st.at[chunk], d_st.at[chunk], 1 + slot, high, True, acc,
                    factor, dq_st.at[chunk], *work,
                )

            return carried

        lax.fori_loop(0, 4, one, 0)

    pl.when(z < ZN // 2)(lambda: all_rows(TILE // 2))
    pl.when(z >= ZN // 2)(lambda: all_rows(TILE))
    for slot in range(2):
        dq_own[slot] = dq_st[2 * slot]
        dq_pair[slot] = dq_st[2 * slot + 1]
    for step, out in enumerate(terms):
        for which in range(2):
            at = (half ^ which) * ZN + ((z + step) & (ZN - 1))
            out[which * HALF_ROWS : (which + 1) * HALF_ROWS] = (
                acc[at].reshape(HALF_ROWS, HD).astype(BF16)
            )


def add_kernel(got, term, out):
    out[...] = (got[...].astype(F32) + term[...].astype(F32)).astype(BF16)


def column_kernel(own, up, down, mine, sent):
    total = own[...].astype(F32) + up[...].astype(F32) + down[...].astype(F32)
    mine[...] = total[:HALF_ROWS]
    sent[...] = total[HALF_ROWS:].astype(BF16)


def rows_kernel(lengths, prefix, own, got, prefix_out, out):
    prefix_out[0] = unstack_heads(prefix[...])
    half, _ = place()
    both = dealt(lengths)
    for slot, resp in enumerate(of_half(both, half)):
        out[0, resp] = unstack_heads(own[slot])
    for slot, resp in enumerate(of_half(both, 1 - half)):
        out[0, resp] = unstack_heads(got[slot])


def sums_kernel(lengths, total, mine, got, dkp, dvp, dkr, dvr):
    half, _ = place()
    both = dealt(lengths)
    factor = token_factor(total)
    for kind, outs, by in ((0, (dkp, dkr), factor * SCALE), (1, (dvp, dvr), factor)):
        outs[0][0] = (mine[kind * ROWS : (kind + 1) * ROWS] + got[kind * ROWS : (kind + 1) * ROWS].astype(F32)) * by
        for source, responses in ((mine, of_half(both, half)), (got, of_half(both, 1 - half))):
            for slot, resp in enumerate(responses):
                at = ((1 + slot) * 2 + kind) * ROWS
                outs[1][0, resp] = source[at : at + ROWS].astype(F32) * by


def shape(dims, dtype):
    return jax.ShapeDtypeStruct(dims, dtype)


def call(kernel, kinds, outs, scratch=(), flops=1 << 20, name=None, vmem=8):
    spec = {"s": SMEM, "v": VMEM}
    return pl.pallas_call(
        kernel,
        out_shape=outs,
        in_specs=[spec[kind] for kind in kinds],
        out_specs=[VMEM] * len(outs),
        scratch_shapes=list(scratch),
        name=name,
        cost_estimate=pl.CostEstimate(flops=flops, bytes_accessed=2 << 20, transcendentals=0),
        compiler_params=pltpu.CompilerParams(vmem_limit_bytes=vmem << 20),
    )


def per_device(
    q_prefix, q_resp, k_prefix, v_prefix, k_resp, v_resp, dout_prefix, dout_resp, lengths
):
    pair = [(i, (i + ZN) % (2 * ZN)) for i in range(2 * ZN)]

    def swap(value):
        return lax.ppermute(value, "resp", pair)

    def shift(value, by):
        moves = [(c + i, c + (i + by) % ZN) for c in (0, ZN) for i in range(ZN)]
        return lax.ppermute(value, "resp", moves)

    def add_count(value, step):
        return lax.ppermute(value, "prompt", [(i, i ^ step) for i in range(PROMPTS)])

    count = shape((8, HD), F32)
    half_keys = shape((HALF_ROWS, HD), BF16)
    sent, total = call(
        keys_kernel, "svvvv", [half_keys, count], name="keys", vmem=60
    )(lengths, k_resp, v_resp, k_prefix, v_prefix)
    kv_got = swap(sent)
    own, q_sent, built = call(
        queries_kernel, "svvvv",
        [shape((2, 3, CHUNK, HD), BF16), shape((2, 2, CHUNK, HD), BF16), count],
        name="queries", vmem=24,
    )(lengths, q_resp, dout_resp, q_prefix, dout_prefix)
    got = swap(q_sent)
    (block,) = call(
        block_kernel, "svvvvvv", [shape((2 * HALF_ROWS, HD), BF16)], name="block"
    )(lengths, k_resp, v_resp, k_prefix, v_prefix, kv_got, built)
    blocks = [block] * ZN
    for step in range(1, ZN // 2 + 1):
        before = blocks[step - 1]
        if step > 1:
            total = total + add_count(total, (2, 1, 4)[step - 2])
            before, total = lax.optimization_barrier((before, total))
        blocks[step] = shift(before, 1)
        if step < ZN // 2:
            blocks[ZN - step] = shift(blocks[(ZN - step + 1) % ZN], -1)
    total = total + add_count(total, 8)
    rows = shape((2, CHUNK, HD), BF16)
    dqp, dq_own, dq_pair, *terms = call(
        main_kernel, "s" + "v" * (ZN + 3),
        [shape((CHUNK, HD), BF16), rows, rows] + [shape((2 * HALF_ROWS, HD), BF16)] * ZN,
        [pltpu.VMEM((2 * ZN, 3, 2, ROWS, HD), BF16), pltpu.VMEM((2 * ZN, 3, 2, ROWS, HD), F32),
         pltpu.VMEM((4, CHUNK, HD), BF16), pltpu.VMEM((4, CHUNK, HD), BF16),
         pltpu.VMEM((4, CHUNK, HD), BF16), pltpu.VMEM((HD, CHUNK), F32),
         pltpu.VMEM((4 * TILE, CHUNK), F32), pltpu.VMEM((4 * TILE, CHUNK), F32)],
        9 << 30, "main", BIG,
    )(lengths, total, own, got, *blocks)

    def add(got, term):
        return call(add_kernel, "vv", [shape((2 * HALF_ROWS, HD), BF16)], name="add")(got, term)[0]

    up, down = terms[ZN // 2], terms[ZN // 2 + 1]
    for step in range(ZN // 2 - 1, 0, -1):
        up = add(shift(up, 1), terms[step])
        if step > 1:
            down = add(shift(down, -1), terms[ZN - step + 1])
    mine, sent = call(column_kernel, "vvv", [shape((HALF_ROWS, HD), F32), half_keys], name="column")(
        terms[0], shift(up, 1), shift(down, -1)
    )
    terms_got = swap(sent)
    dq_got = swap(dq_pair)
    dqp_out, dq_all = call(
        rows_kernel, "svvv",
        [shape((1, ROWS, HEADS * HD), BF16), shape((1, RESPS, ROWS, HEADS * HD), BF16)],
        name="rows",
    )(lengths, dqp, dq_own, dq_got)
    prefix_out = shape((1, ROWS, HD), F32)
    resp_out = shape((1, RESPS, ROWS, HD), F32)
    dkp, dvp, dkr, dvr = call(
        sums_kernel, "svvv", [prefix_out, prefix_out, resp_out, resp_out],
        name="sums",
    )(lengths, total, mine, terms_got)
    return dqp_out, dq_all, dkp, dvp, dkr, dvr


def solution(mesh):
    rows = P("prompt", "resp", None)
    resp_rows = P("prompt", None, "resp", None)
    return jax.shard_map(
        per_device,
        mesh=mesh,
        in_specs=(
            rows, resp_rows, rows, rows, resp_rows, resp_rows, rows, resp_rows, P("prompt", None),
        ),
        out_specs=(rows, resp_rows, rows, rows, resp_rows, resp_rows),
        check_vma=False,
    )
```

time: 104 us -> 92.2 us (0.89)
  the two profiles are of different devices: /device:TPU:24 before, /device:TPU:16 now
where the time goes in v2:
time: 92.2 us; the launch traced here: 92.5 us
  starting transfers between devices  35 us (38%)
  waiting for transfers between devices  32.9 us (36%)
  Pallas kernels  20.7 us (22%)
  local copies, waits for them, and re-layouts  3.12 us (3%)
    ppermute x14, waiting for transfers between devices, shift(): return lax.ppermute(value, 'resp', moves)  24.6 us
    ppermute x14, starting transfers between devices, shift(): return lax.ppermute(value, 'resp', moves)  23.7 us
    pallas_call x1, Pallas kernels, per_device(): call(main_kernel, 's' + 'v' * (ZN + 3), [shape((CHUNK, HD), BF16), rows,...  14.7 us
    ppermute x4, waiting for transfers between devices, add_count(): lax.ppermute(value, 'prompt', [(i, i ^ step) for i in range(PROMPTS)])  7.16 us
    ppermute x4, starting transfers between devices, swap(): return lax.ppermute(value, 'resp', pair)  6.76 us
    ppermute x4, starting transfers between devices, add_count(): lax.ppermute(value, 'prompt', [(i, i ^ step) for i in range(PROMPTS)])  4.53 us
    unnamed x20, local copies, waits for them, and re-layouts  3.12 us
  transfers between devices with their start and end apart: 22, of which 11 were waited for; matrix products, arithmetic and copies ran while one was open for 0% of the time, Pallas kernels for 3%

profile of v2, /device:TPU:16, one launch (start us, length us, event | category | flops | bytes accessed | tf_op | source)
XLA Modules:
  0.0 92.5 jit_solution(5742763251601941663)
XLA Ops:
  0.6 0.0 copy-start.4
  0.6 1.6 %keys.1 = (bf16[384,128]{1,0:T(8,128)(2,1)}, f32[8,128]{1,0:T(8,128)}) custom-call(s32[1,4]{1,0:T(1,128)} %lengths.11, bf16[1,4,64,128]{3,2,1,0:T(8,128)(2,1)} %kr.3, bf16[1,4,64,128]{3,2,1,0:T(8,128)(2,1)} %vr.3, bf16[1,64,128]{2,1,0:T(8,128)(2,1)} %kp.3, bf16[1,64,128]{2,1,0:T(8,128)(2,1)} %vp.3), custom_call_target="tpu_custom_call" | custom-call | flops 1048576 | bytes 2097152 | tf_op jit(solution)/shard_map/keys/pallas_call | solution.py:303
  2.2 0.0 copy-start.8
  2.2 1.5 %collective-permute-start = (bf16[384,128]{1,0:T(8,128)(2,1)}, bf16[384,128]{1,0:T(8,128)(2,1)S(1)}, u32[]{:S(2)}, u32[]{:S(2)}) collective-permute-start(bf16[384,128]{1,0:T(8,128)(2,1)} %get-tuple-element.36), channel_id=1, source_target_pairs={{0,8},{1,9},{2,10},{3,11},{4,12},{5,13},{6,14},{7,15},{8,0},{9,1},... | collective-permute-start | bytes 294920 | tf_op jit(solution)/shard_map/ppermute | solution.py:292
  3.7 0.0 copy-done.4
  3.7 0.0 copy-done.8
  3.7 1.0 %copy-done = bf16[1,4,64,1024]{3,2,1,0:T(8,128)(2,1)S(1)} copy-done((bf16[1,4,64,1024]{3,2,1,0:T(8,128)(2,1)S(1)}, bf16[1,4,64,1024]{3,2,1,0:T(8,128)(2,1)}, u32[]{:S(2)}) %copy-start) | copy-done | bytes 524312
  4.8 1.0 %copy-done.1 = bf16[1,4,64,1024]{3,2,1,0:T(8,128)(2,1)S(1)} copy-done((bf16[1,4,64,1024]{3,2,1,0:T(8,128)(2,1)S(1)}, bf16[1,4,64,1024]{3,2,1,0:T(8,128)(2,1)}, u32[]{:S(2)}) %copy-start.1) | copy-done | bytes 524312
  5.8 0.9 copy-done.5
  6.7 0.7 queries.1
  7.5 0.0 collective-permute-done.got
  7.5 0.1 copy-done.2
  7.6 0.0 copy-done.3
  7.6 0.0 copy-done.6
  7.6 0.0 copy-done.7
  7.6 0.6 block.1.rest_0_
  8.2 2.0 %collective-permute-start.1 = (bf16[768,128]{1,0:T(8,128)(2,1)S(1)}, bf16[768,128]{1,0:T(8,128)(2,1)S(1)}, u32[]{:S(2)}, u32[]{:S(2)}) collective-permute-start(bf16[768,128]{1,0:T(8,128)(2,1)S(1)} %block.1.rest_0_), channel_id=1, source_target_pairs={{0,1},{1,2},{2,3},{3,4},{4,5},{5,6},{6,7},{7,0},{8,9},{9,10},{10,1... | collective-permute-start | bytes 589832 | tf_op jit(solution)/shard_map/ppermute | solution.py:296
  10.2 0.0 copy-done.9
  10.2 2.7 %collective-permute-start.2 = (f32[8,128]{1,0:T(8,128)S(1)}, f32[8,128]{1,0:T(8,128)S(1)}, u32[]{:S(2)}, u32[]{:S(2)}) collective-permute-start(f32[8,128]{1,0:T(8,128)S(1)} %copy-done.9), channel_id=1, source_target_pairs={{0,32},{16,48},{32,0},{48,16},{64,96},{80,112},{96,64},{112,80},{1... | collective-permute-start | bytes 12296 | tf_op jit(solution)/shard_map/ppermute | solution.py:299
  12.9 2.4 %collective-permute-done.2 = f32[8,128]{1,0:T(8,128)S(1)} collective-permute-done((f32[8,128]{1,0:T(8,128)S(1)}, f32[8,128]{1,0:T(8,128)S(1)}, u32[]{:S(2)}, u32[]{:S(2)}) %collective-permute-start.2) | collective-permute-done | bytes 4128 | tf_op jit(solution)/shard_map/ppermute | solution.py:299
  15.3 4.0 %collective-permute-start.10 = (bf16[768,128]{1,0:T(8,128)(2,1)S(1)}, bf16[768,128]{1,0:T(8,128)(2,1)S(1)}, u32[]{:S(2)}, u32[]{:S(2)}) collective-permute-start(bf16[768,128]{1,0:T(8,128)(2,1)S(1)} %block.1.rest_0_), channel_id=1, source_target_pairs={{0,7},{1,0},{2,1},{3,2},{4,3},{5,4},{6,5},{7,6},{8,15},{9,8},{10,9... | collective-permute-start | bytes 589832 | tf_op jit(solution)/shard_map/ppermute | solution.py:296
  19.3 0.0 collective-permute-done.1.rest_1_
  19.4 0.0 collective-permute-start.3
  19.4 1.0 %collective-permute-start.8 = (bf16[2,2,512,128]{3,2,1,0:T(8,128)(2,1)S(1)}, bf16[2,2,512,128]{3,2,1,0:T(8,128)(2,1)S(1)}, u32[]{:S(2)}, u32[]{:S(2)}) collective-permute-start(bf16[2,2,512,128]{3,2,1,0:T(8,128)(2,1)S(1)} %get-tuple-element.45), channel_id=1, source_target_pairs={{0,8},{1,9},{2,10},{3,11},{4,12},{5,13},{6,14},{7,15},{8,0},{9,1},... | collective-permute-start | bytes 1572872 | tf_op jit(solution)/shard_map/ppermute | solution.py:292
  20.3 0.0 collective-permute-start.4
  20.3 2.2 %collective-permute-done.10.rest_7_ = bf16[768,128]{1,0:T(8,128)(2,1)S(1)} collective-permute-done((bf16[768,128]{1,0:T(8,128)(2,1)S(1)}, bf16[768,128]{1,0:T(8,128)(2,1)S(1)}, u32[]{:S(2)}, u32[]{:S(2)}) %collective-permute-start.10) | collective-permute-done | bytes 196640 | tf_op jit(solution)/shard_map/ppermute | solution.py:296
  22.5 3.7 %collective-permute-start.11 = (bf16[768,128]{1,0:T(8,128)(2,1)S(1)}, bf16[768,128]{1,0:T(8,128)(2,1)S(1)}, u32[]{:S(2)}, u32[]{:S(2)}) collective-permute-start(bf16[768,128]{1,0:T(8,128)(2,1)S(1)} %collective-permute-done.10.rest_7_), channel_id=1, source_target_pairs={{0,7},{1,0},{2,1},{3,2},{4,3},{5,4},{6,5},{7,6},{8,15},{9,8},{10,9... | collective-permute-start | bytes 589832 | tf_op jit(solution)/shard_map/ppermute | solution.py:296
  26.2 0.0 collective-permute-done.4
  26.2 0.0 collective-permute-done.3.rest_2_
  26.2 0.1 collective-permute-start.5
  26.3 1.4 %collective-permute-start.6 = (f32[8,128]{1,0:T(8,128)S(1)}, f32[8,128]{1,0:T(8,128)S(1)}, u32[]{:S(2)}, u32[]{:S(2)}) collective-permute-start(f32[8,128]{1,0:T(8,128)S(1)} %add.18), channel_id=1, source_target_pairs={{0,64},{16,80},{32,96},{48,112},{64,0},{80,16},{96,32},{112,48},{1... | collective-permute-start | bytes 12296 | tf_op jit(solution)/shard_map/ppermute | solution.py:299
  27.7 1.7 %collective-permute-done.11.rest_6_ = bf16[768,128]{1,0:T(8,128)(2,1)S(1)} collective-permute-done((bf16[768,128]{1,0:T(8,128)(2,1)S(1)}, bf16[768,128]{1,0:T(8,128)(2,1)S(1)}, u32[]{:S(2)}, u32[]{:S(2)}) %collective-permute-start.11) | collective-permute-done | bytes 196640 | tf_op jit(solution)/shard_map/ppermute | solution.py:296
  29.4 3.7 %collective-permute-start.12 = (bf16[768,128]{1,0:T(8,128)(2,1)S(1)}, bf16[768,128]{1,0:T(8,128)(2,1)S(1)}, u32[]{:S(2)}, u32[]{:S(2)}) collective-permute-start(bf16[768,128]{1,0:T(8,128)(2,1)S(1)} %collective-permute-done.11.rest_6_), channel_id=1, source_target_pairs={{0,7},{1,0},{2,1},{3,2},{4,3},{5,4},{6,5},{7,6},{8,15},{9,8},{10,9... | collective-permute-start | bytes 589832 | tf_op jit(solution)/shard_map/ppermute | solution.py:296
  33.1 0.0 collective-permute-done.6
  33.1 0.1 collective-permute-done.5.rest_3_
  33.2 0.0 collective-permute-start.9
  33.2 0.4 collective-permute-start.7
  33.6 4.8 %collective-permute-done.7 = f32[8,128]{1,0:T(8,128)S(1)} collective-permute-done((f32[8,128]{1,0:T(8,128)S(1)}, f32[8,128]{1,0:T(8,128)S(1)}, u32[]{:S(2)}, u32[]{:S(2)}) %collective-permute-start.7) | collective-permute-done | bytes 4128 | tf_op jit(solution)/shard_map/ppermute | solution.py:299
  38.4 0.0 collective-permute-done.8.got
  38.4 0.0 collective-permute-done.12.rest_5_
  38.4 1.7 %collective-permute-done.9.rest_4_ = bf16[768,128]{1,0:T(8,128)(2,1)S(1)} collective-permute-done((bf16[768,128]{1,0:T(8,128)(2,1)S(1)}, bf16[768,128]{1,0:T(8,128)(2,1)S(1)}, u32[]{:S(2)}, u32[]{:S(2)}) %collective-permute-start.9) | collective-permute-done | bytes 196640 | tf_op jit(solution)/shard_map/ppermute | solution.py:296
  40.1 14.7 %main.1 = (bf16[512,128]{1,0:T(8,128)(2,1)S(1)}, bf16[2,512,128]{2,1,0:T(8,128)(2,1)S(1)}, bf16[2,512,128]{2,1,0:T(8,128)(2,1)S(1)}, bf16[768,128]{1,0:T(8,128)(...) custom-call(s32[1,4]{1,0:T(1,128)S(1)} %copy-done.8, ...), custom_call_target="tpu_custom_call" | custom-call | flops 9663676416 | bytes 2097152 | tf_op jit(solution)/shard_map/main/pallas_call | solution.py:327
  54.8 0.1 collective-permute-start.14
  54.9 3.2 %collective-permute-start.18 = (bf16[768,128]{1,0:T(8,128)(2,1)S(1)}, bf16[768,128]{1,0:T(8,128)(2,1)S(1)}, u32[]{:S(2)}, u32[]{:S(2)}) collective-permute-start(bf16[768,128]{1,0:T(8,128)(2,1)S(1)} %get-tuple-element.57), channel_id=1, source_target_pairs={{0,7},{1,0},{2,1},{3,2},{4,3},{5,4},{6,5},{7,6},{8,15},{9,8},{10,9... | collective-permute-start | bytes 589832 | tf_op jit(solution)/shard_map/ppermute | solution.py:296
  58.1 5.6 %collective-permute-done.14.got = bf16[768,128]{1,0:T(8,128)(2,1)S(1)} collective-permute-done((bf16[768,128]{1,0:T(8,128)(2,1)S(1)}, bf16[768,128]{1,0:T(8,128)(2,1)S(1)}, u32[]{:S(2)}, u32[]{:S(2)}) %collective-permute-start.14) | collective-permute-done | bytes 196640 | tf_op jit(solution)/shard_map/ppermute | solution.py:296
  63.8 0.1 collective-permute-start.15
  63.9 0.0 collective-permute-done.18.got
  63.9 3.3 %collective-permute-start.19 = (bf16[768,128]{1,0:T(8,128)(2,1)S(1)}, bf16[768,128]{1,0:T(8,128)(2,1)S(1)}, u32[]{:S(2)}, u32[]{:S(2)}) collective-permute-start(bf16[768,128]{1,0:T(8,128)(2,1)S(1)} %add.24), channel_id=1, source_target_pairs={{0,7},{1,0},{2,1},{3,2},{4,3},{5,4},{6,5},{7,6},{8,15},{9,8},{10,9... | collective-permute-start | bytes 589832 | tf_op jit(solution)/shard_map/ppermute | solution.py:296
  67.2 4.7 %collective-permute-done.15.got = bf16[768,128]{1,0:T(8,128)(2,1)S(1)} collective-permute-done((bf16[768,128]{1,0:T(8,128)(2,1)S(1)}, bf16[768,128]{1,0:T(8,128)(2,1)S(1)}, u32[]{:S(2)}, u32[]{:S(2)}) %collective-permute-start.15) | collective-permute-done | bytes 196640 | tf_op jit(solution)/shard_map/ppermute | solution.py:296
  72.0 0.1 collective-permute-start.16
  72.1 0.0 collective-permute-done.19.got
  72.2 3.3 %collective-permute-start.20 = (bf16[768,128]{1,0:T(8,128)(2,1)S(1)}, bf16[768,128]{1,0:T(8,128)(2,1)S(1)}, u32[]{:S(2)}, u32[]{:S(2)}) collective-permute-start(bf16[768,128]{1,0:T(8,128)(2,1)S(1)} %add.25), channel_id=1, source_target_pairs={{0,7},{1,0},{2,1},{3,2},{4,3},{5,4},{6,5},{7,6},{8,15},{9,8},{10,9... | collective-permute-start | bytes 589832 | tf_op jit(solution)/shard_map/ppermute | solution.py:296
  75.5 3.9 %collective-permute-done.16.got = bf16[768,128]{1,0:T(8,128)(2,1)S(1)} collective-permute-done((bf16[768,128]{1,0:T(8,128)(2,1)S(1)}, bf16[768,128]{1,0:T(8,128)(2,1)S(1)}, u32[]{:S(2)}, u32[]{:S(2)}) %collective-permute-start.16) | collective-permute-done | bytes 196640 | tf_op jit(solution)/shard_map/ppermute | solution.py:296
  79.4 0.1 add.23
  79.5 0.1 collective-permute-start.17
  79.6 2.1 %collective-permute-start.13 = (bf16[2,512,128]{2,1,0:T(8,128)(2,1)S(1)}, bf16[2,512,128]{2,1,0:T(8,128)(2,1)S(1)}, u32[]{:S(2)}, u32[]{:S(2)}) collective-permute-start(bf16[2,512,128]{2,1,0:T(8,128)(2,1)S(1)} %get-tuple-element.49), channel_id=1, source_target_pairs={{0,8},{1,9},{2,10},{3,11},{4,12},{5,13},{6,14},{7,15},{8,0},{9,1},... | collective-permute-start | bytes 786440 | tf_op jit(solution)/shard_map/ppermute | solution.py:292
  81.7 0.0 collective-permute-done.20.down
  81.7 4.7 %collective-permute-done.17.up = bf16[768,128]{1,0:T(8,128)(2,1)S(1)} collective-permute-done((bf16[768,128]{1,0:T(8,128)(2,1)S(1)}, bf16[768,128]{1,0:T(8,128)(2,1)S(1)}, u32[]{:S(2)}, u32[]{:S(2)}) %collective-permute-start.17) | collective-permute-done | bytes 196640 | tf_op jit(solution)/shard_map/ppermute | solution.py:296
  86.4 0.1 column.1
  86.5 2.1 %collective-permute-start.21 = (bf16[384,128]{1,0:T(8,128)(2,1)S(1)}, bf16[384,128]{1,0:T(8,128)(2,1)S(1)}, u32[]{:S(2)}, u32[]{:S(2)}) collective-permute-start(bf16[384,128]{1,0:T(8,128)(2,1)S(1)} %get-tuple-element.61), channel_id=1, source_target_pairs={{0,8},{1,9},{2,10},{3,11},{4,12},{5,13},{6,14},{7,15},{8,0},{9,1},... | collective-permute-start | bytes 294920 | tf_op jit(solution)/shard_map/ppermute | solution.py:292
  88.6 0.0 collective-permute-done.13.got
  88.6 1.5 %rows.1 = (bf16[1,64,1024]{2,1,0:T(8,128)(2,1)}, bf16[1,4,64,1024]{3,2,1,0:T(8,128)(2,1)}) custom-call(s32[1,4]{1,0:T(1,128)S(1)} %copy-done.8, bf16[512,128]{1,0:T(8,128)(2,1)S(1)} %get-tuple-element.47.prefix, bf16[2,512,128]{2,1,0:T(8,128)(2,1)S(1)} %get-tuple-element.48.own, bf16[2,512,128]{2,1,0:T(8,128)(2,1)S(1)} %collective-permute-done.13.got), custom_call_target="tpu_custom_call" | custom-call | flops 1048576 | bytes 2097152 | tf_op jit(solution)/shard_map/rows/pallas_call | solution.py:350
  90.1 1.1 %collective-permute-done.21.got = bf16[384,128]{1,0:T(8,128)(2,1)S(1)} collective-permute-done((bf16[384,128]{1,0:T(8,128)(2,1)S(1)}, bf16[384,128]{1,0:T(8,128)(2,1)S(1)}, u32[]{:S(2)}, u32[]{:S(2)}) %collective-permute-start.21) | collective-permute-done | bytes 98336 | tf_op jit(solution)/shard_map/ppermute | solution.py:292
  91.2 1.3 %sums.1 = (f32[1,64,128]{2,1,0:T(8,128)}, f32[1,64,128]{2,1,0:T(8,128)}, f32[1,4,64,128]{3,2,1,0:T(8,128)}, f32[1,4,64,128]{3,2,1,0:T(8,128)}) custom-call(s32[1,4]{1,0:T(1,128)S(1)} %copy-done.8, f32[8,128]{1,0:T(8,128)S(1)} %add.20.total, f32[384,128]{1,0:T(8,128)S(1)} %get-tuple-element.60.mine, bf16[384,128]{1,0:T(8,128)(2,1)S(1)} %collective-permute-done.21.got), custom_call_target="tpu_custom_call" | custom-call | flops 1048576 | bytes 2097152 | tf_op jit(solution)/shard_map/sums/pallas_call | solution.py:357
  (16 shorter events, 0.2 us)
Async XLA Ops:
  0.6 3.1 %copy-start.4 = (bf16[1,64,1024]{2,1,0:T(8,128)(2,1)S(1)}, bf16[1,64,1024]{2,1,0:T(8,128)(2,1)}, u32[]{:S(2)}) copy-start(bf16[1,64,1024]{2,1,0:T(8,128)(2,1)} %qp.1) | copy-start | bytes 393220
  2.2 1.5 %copy-start.8 = (s32[1,4]{1,0:T(1,128)S(1)}, s32[1,4]{1,0:T(1,128)}, u32[]{:S(2)}) copy-start(s32[1,4]{1,0:T(1,128)} %lengths.11) | copy-start | bytes 52
  2.2 5.2 %collective-permute-start = (bf16[384,128]{1,0:T(8,128)(2,1)}, bf16[384,128]{1,0:T(8,128)(2,1)S(1)}, u32[]{:S(2)}, u32[]{:S(2)}) collective-permute-start(bf16[384,128]{1,0:T(8,128)(2,1)} %get-tuple-element.36), channel_id=1, source_target_pairs={{0,8},{1,9},{2,10},{3,11},{4,12},{5,13},{6,14},{7,15},{8,0},{9,1},... | collective-permute-start | bytes 294920 | tf_op jit(solution)/shard_map/ppermute | solution.py:292
  3.7 1.0 %copy-start = (bf16[1,4,64,1024]{3,2,1,0:T(8,128)(2,1)S(1)}, bf16[1,4,64,1024]{3,2,1,0:T(8,128)(2,1)}, u32[]{:S(2)}) copy-start(bf16[1,4,64,1024]{3,2,1,0:T(8,128)(2,1)} %qr.1) | copy-start | bytes 1572868
  4.8 1.0 %copy-start.1 = (bf16[1,4,64,1024]{3,2,1,0:T(8,128)(2,1)S(1)}, bf16[1,4,64,1024]{3,2,1,0:T(8,128)(2,1)}, u32[]{:S(2)}) copy-start(bf16[1,4,64,1024]{3,2,1,0:T(8,128)(2,1)} %dr.1) | copy-start | bytes 1572868
  5.8 0.9 copy-start.5
  6.7 0.8 copy-start.2
  6.7 0.9 copy-start.3
  6.7 0.9 copy-start.6
  6.7 0.9 copy-start.7
  7.6 2.6 %copy-start.9 = (f32[8,128]{1,0:T(8,128)S(1)}, f32[8,128]{1,0:T(8,128)}, u32[]{:S(2)}) copy-start(f32[8,128]{1,0:T(8,128)} %get-tuple-element.38) | copy-start | bytes 12292
  8.2 11.2 %collective-permute-start.1 = (bf16[768,128]{1,0:T(8,128)(2,1)S(1)}, bf16[768,128]{1,0:T(8,128)(2,1)S(1)}, u32[]{:S(2)}, u32[]{:S(2)}) collective-permute-start(bf16[768,128]{1,0:T(8,128)(2,1)S(1)} %block.1.rest_0_), channel_id=1, source_target_pairs={{0,1},{1,2},{2,3},{3,4},{4,5},{5,6},{6,7},{7,0},{8,9},{9,10},{10,1... | collective-permute-start | bytes 589832 | tf_op jit(solution)/shard_map/ppermute | solution.py:296
  10.2 5.1 %collective-permute-start.2 = (f32[8,128]{1,0:T(8,128)S(1)}, f32[8,128]{1,0:T(8,128)S(1)}, u32[]{:S(2)}, u32[]{:S(2)}) collective-permute-start(f32[8,128]{1,0:T(8,128)S(1)} %copy-done.9), channel_id=1, source_target_pairs={{0,32},{16,48},{32,0},{48,16},{64,96},{80,112},{96,64},{112,80},{1... | collective-permute-start | bytes 12296 | tf_op jit(solution)/shard_map/ppermute | solution.py:299
  15.3 7.2 %collective-permute-start.10 = (bf16[768,128]{1,0:T(8,128)(2,1)S(1)}, bf16[768,128]{1,0:T(8,128)(2,1)S(1)}, u32[]{:S(2)}, u32[]{:S(2)}) collective-permute-start(bf16[768,128]{1,0:T(8,128)(2,1)S(1)} %block.1.rest_0_), channel_id=1, source_target_pairs={{0,7},{1,0},{2,1},{3,2},{4,3},{5,4},{6,5},{7,6},{8,15},{9,8},{10,9... | collective-permute-start | bytes 589832 | tf_op jit(solution)/shard_map/ppermute | solution.py:296
  19.4 6.9 %collective-permute-start.3 = (bf16[768,128]{1,0:T(8,128)(2,1)S(1)}, bf16[768,128]{1,0:T(8,128)(2,1)S(1)}, u32[]{:S(2)}, u32[]{:S(2)}) collective-permute-start(bf16[768,128]{1,0:T(8,128)(2,1)S(1)} %collective-permute-done.1.rest_1_), channel_id=1, source_target_pairs={{0,1},{1,2},{2,3},{3,4},{4,5},{5,6},{6,7},{7,0},{8,9},{9,10},{10,1... | collective-permute-start | bytes 589832 | tf_op jit(solution)/shard_map/ppermute | solution.py:296
  19.4 19.1 %collective-permute-start.8 = (bf16[2,2,512,128]{3,2,1,0:T(8,128)(2,1)S(1)}, bf16[2,2,512,128]{3,2,1,0:T(8,128)(2,1)S(1)}, u32[]{:S(2)}, u32[]{:S(2)}) collective-permute-start(bf16[2,2,512,128]{3,2,1,0:T(8,128)(2,1)S(1)} %get-tuple-element.45), channel_id=1, source_target_pairs={{0,8},{1,9},{2,10},{3,11},{4,12},{5,13},{6,14},{7,15},{8,0},{9,1},... | collective-permute-start | bytes 1572872 | tf_op jit(solution)/shard_map/ppermute | solution.py:292
  20.3 5.9 %collective-permute-start.4 = (f32[8,128]{1,0:T(8,128)S(1)}, f32[8,128]{1,0:T(8,128)S(1)}, u32[]{:S(2)}, u32[]{:S(2)}) collective-permute-start(f32[8,128]{1,0:T(8,128)S(1)} %add.17), channel_id=1, source_target_pairs={{0,16},{16,0},{32,48},{48,32},{64,80},{80,64},{96,112},{112,96},{1... | collective-permute-start | bytes 12296 | tf_op jit(solution)/shard_map/ppermute | solution.py:299
  22.5 6.9 %collective-permute-start.11 = (bf16[768,128]{1,0:T(8,128)(2,1)S(1)}, bf16[768,128]{1,0:T(8,128)(2,1)S(1)}, u32[]{:S(2)}, u32[]{:S(2)}) collective-permute-start(bf16[768,128]{1,0:T(8,128)(2,1)S(1)} %collective-permute-done.10.rest_7_), channel_id=1, source_target_pairs={{0,7},{1,0},{2,1},{3,2},{4,3},{5,4},{6,5},{7,6},{8,15},{9,8},{10,9... | collective-permute-start | bytes 589832 | tf_op jit(solution)/shard_map/ppermute | solution.py:296
  26.2 7.0 %collective-permute-start.5 = (bf16[768,128]{1,0:T(8,128)(2,1)S(1)}, bf16[768,128]{1,0:T(8,128)(2,1)S(1)}, u32[]{:S(2)}, u32[]{:S(2)}) collective-permute-start(bf16[768,128]{1,0:T(8,128)(2,1)S(1)} %collective-permute-done.3.rest_2_), channel_id=1, source_target_pairs={{0,1},{1,2},{2,3},{3,4},{4,5},{5,6},{6,7},{7,0},{8,9},{9,10},{10,1... | collective-permute-start | bytes 589832 | tf_op jit(solution)/shard_map/ppermute | solution.py:296
  26.3 6.8 %collective-permute-start.6 = (f32[8,128]{1,0:T(8,128)S(1)}, f32[8,128]{1,0:T(8,128)S(1)}, u32[]{:S(2)}, u32[]{:S(2)}) collective-permute-start(f32[8,128]{1,0:T(8,128)S(1)} %add.18), channel_id=1, source_target_pairs={{0,64},{16,80},{32,96},{48,112},{64,0},{80,16},{96,32},{112,48},{1... | collective-permute-start | bytes 12296 | tf_op jit(solution)/shard_map/ppermute | solution.py:299
  29.4 9.0 %collective-permute-start.12 = (bf16[768,128]{1,0:T(8,128)(2,1)S(1)}, bf16[768,128]{1,0:T(8,128)(2,1)S(1)}, u32[]{:S(2)}, u32[]{:S(2)}) collective-permute-start(bf16[768,128]{1,0:T(8,128)(2,1)S(1)} %collective-permute-done.11.rest_6_), channel_id=1, source_target_pairs={{0,7},{1,0},{2,1},{3,2},{4,3},{5,4},{6,5},{7,6},{8,15},{9,8},{10,9... | collective-permute-start | bytes 589832 | tf_op jit(solution)/shard_map/ppermute | solution.py:296
  33.2 6.9 %collective-permute-start.9 = (bf16[768,128]{1,0:T(8,128)(2,1)S(1)}, bf16[768,128]{1,0:T(8,128)(2,1)S(1)}, u32[]{:S(2)}, u32[]{:S(2)}) collective-permute-start(bf16[768,128]{1,0:T(8,128)(2,1)S(1)} %collective-permute-done.5.rest_3_), channel_id=1, source_target_pairs={{0,1},{1,2},{2,3},{3,4},{4,5},{5,6},{6,7},{7,0},{8,9},{9,10},{10,1... | collective-permute-start | bytes 589832 | tf_op jit(solution)/shard_map/ppermute | solution.py:296
  33.2 5.2 %collective-permute-start.7 = (f32[8,128]{1,0:T(8,128)S(1)}, f32[8,128]{1,0:T(8,128)S(1)}, u32[]{:S(2)}, u32[]{:S(2)}) collective-permute-start(f32[8,128]{1,0:T(8,128)S(1)} %add.19), channel_id=1, source_target_pairs={{0,128},{16,144},{32,160},{48,176},{64,192},{80,208},{96,224},{112... | collective-permute-start | bytes 12296 | tf_op jit(solution)/shard_map/ppermute | solution.py:299
  54.8 8.9 %collective-permute-start.14 = (bf16[768,128]{1,0:T(8,128)(2,1)S(1)}, bf16[768,128]{1,0:T(8,128)(2,1)S(1)}, u32[]{:S(2)}, u32[]{:S(2)}) collective-permute-start(bf16[768,128]{1,0:T(8,128)(2,1)S(1)} %get-tuple-element.53), channel_id=1, source_target_pairs={{0,1},{1,2},{2,3},{3,4},{4,5},{5,6},{6,7},{7,0},{8,9},{9,10},{10,1... | collective-permute-start | bytes 589832 | tf_op jit(solution)/shard_map/ppermute | solution.py:296
  54.9 9.0 %collective-permute-start.18 = (bf16[768,128]{1,0:T(8,128)(2,1)S(1)}, bf16[768,128]{1,0:T(8,128)(2,1)S(1)}, u32[]{:S(2)}, u32[]{:S(2)}) collective-permute-start(bf16[768,128]{1,0:T(8,128)(2,1)S(1)} %get-tuple-element.57), channel_id=1, source_target_pairs={{0,7},{1,0},{2,1},{3,2},{4,3},{5,4},{6,5},{7,6},{8,15},{9,8},{10,9... | collective-permute-start | bytes 589832 | tf_op jit(solution)/shard_map/ppermute | solution.py:296
  63.8 8.2 %collective-permute-start.15 = (bf16[768,128]{1,0:T(8,128)(2,1)S(1)}, bf16[768,128]{1,0:T(8,128)(2,1)S(1)}, u32[]{:S(2)}, u32[]{:S(2)}) collective-permute-start(bf16[768,128]{1,0:T(8,128)(2,1)S(1)} %add.21), channel_id=1, source_target_pairs={{0,1},{1,2},{2,3},{3,4},{4,5},{5,6},{6,7},{7,0},{8,9},{9,10},{10,1... | collective-permute-start | bytes 589832 | tf_op jit(solution)/shard_map/ppermute | solution.py:296
  63.9 8.2 %collective-permute-start.19 = (bf16[768,128]{1,0:T(8,128)(2,1)S(1)}, bf16[768,128]{1,0:T(8,128)(2,1)S(1)}, u32[]{:S(2)}, u32[]{:S(2)}) collective-permute-start(bf16[768,128]{1,0:T(8,128)(2,1)S(1)} %add.24), channel_id=1, source_target_pairs={{0,7},{1,0},{2,1},{3,2},{4,3},{5,4},{6,5},{7,6},{8,15},{9,8},{10,9... | collective-permute-start | bytes 589832 | tf_op jit(solution)/shard_map/ppermute | solution.py:296
  72.0 7.4 %collective-permute-start.16 = (bf16[768,128]{1,0:T(8,128)(2,1)S(1)}, bf16[768,128]{1,0:T(8,128)(2,1)S(1)}, u32[]{:S(2)}, u32[]{:S(2)}) collective-permute-start(bf16[768,128]{1,0:T(8,128)(2,1)S(1)} %add.22), channel_id=1, source_target_pairs={{0,1},{1,2},{2,3},{3,4},{4,5},{5,6},{6,7},{7,0},{8,9},{9,10},{10,1... | collective-permute-start | bytes 589832 | tf_op jit(solution)/shard_map/ppermute | solution.py:296
  72.2 9.5 %collective-permute-start.20 = (bf16[768,128]{1,0:T(8,128)(2,1)S(1)}, bf16[768,128]{1,0:T(8,128)(2,1)S(1)}, u32[]{:S(2)}, u32[]{:S(2)}) collective-permute-start(bf16[768,128]{1,0:T(8,128)(2,1)S(1)} %add.25), channel_id=1, source_target_pairs={{0,7},{1,0},{2,1},{3,2},{4,3},{5,4},{6,5},{7,6},{8,15},{9,8},{10,9... | collective-permute-start | bytes 589832 | tf_op jit(solution)/shard_map/ppermute | solution.py:296
  79.5 7.0 %collective-permute-start.17 = (bf16[768,128]{1,0:T(8,128)(2,1)S(1)}, bf16[768,128]{1,0:T(8,128)(2,1)S(1)}, u32[]{:S(2)}, u32[]{:S(2)}) collective-permute-start(bf16[768,128]{1,0:T(8,128)(2,1)S(1)} %add.23), channel_id=1, source_target_pairs={{0,1},{1,2},{2,3},{3,4},{4,5},{5,6},{6,7},{7,0},{8,9},{9,10},{10,1... | collective-permute-start | bytes 589832 | tf_op jit(solution)/shard_map/ppermute | solution.py:296
  79.6 9.1 %collective-permute-start.13 = (bf16[2,512,128]{2,1,0:T(8,128)(2,1)S(1)}, bf16[2,512,128]{2,1,0:T(8,128)(2,1)S(1)}, u32[]{:S(2)}, u32[]{:S(2)}) collective-permute-start(bf16[2,512,128]{2,1,0:T(8,128)(2,1)S(1)} %get-tuple-element.49), channel_id=1, source_target_pairs={{0,8},{1,9},{2,10},{3,11},{4,12},{5,13},{6,14},{7,15},{8,0},{9,1},... | collective-permute-start | bytes 786440 | tf_op jit(solution)/shard_map/ppermute | solution.py:292
  86.5 4.7 %collective-permute-start.21 = (bf16[384,128]{1,0:T(8,128)(2,1)S(1)}, bf16[384,128]{1,0:T(8,128)(2,1)S(1)}, u32[]{:S(2)}, u32[]{:S(2)}) collective-permute-start(bf16[384,128]{1,0:T(8,128)(2,1)S(1)} %get-tuple-element.61), channel_id=1, source_target_pairs={{0,8},{1,9},{2,10},{3,11},{4,12},{5,13},{6,14},{7,15},{8,0},{9,1},... | collective-permute-start | bytes 294920 | tf_op jit(solution)/shard_map/ppermute | solution.py:292

commit v3 on v2

--- a/solution.py
+++ b/solution.py
@@ -1,3 +1,5 @@
+import functools
+
 import jax
 import jax.numpy as jnp
 from jax import lax
@@ -184,7 +186,7 @@
 def main_kernel(lengths, total, own, got, *rest):
     blocks, rest = rest[:ZN], rest[ZN:]
     dqp_out, dq_own, dq_pair, rest = rest[0], rest[1], rest[2], rest[3:]
-    terms, (kv, acc, q_st, d_st, dq_st, *work) = rest[:ZN], rest[ZN:]
+    terms, (far, kv, acc, q_st, d_st, dq_st, *work) = rest[:ZN], rest[ZN:]
     half, z = place()
     factor = token_factor(total) * SCALE
     for step, block in enumerate(blocks):
@@ -228,13 +230,18 @@
     for step, out in enumerate(terms):
         for which in range(2):
             at = (half ^ which) * ZN + ((z + step) & (ZN - 1))
-            out[which * HALF_ROWS : (which + 1) * HALF_ROWS] = (
-                acc[at].reshape(HALF_ROWS, HD).astype(BF16)
-            )
-
-
-def add_kernel(got, term, out):
-    out[...] = (got[...].astype(F32) + term[...].astype(F32)).astype(BF16)
+            rows = acc[at].reshape(HALF_ROWS, HD).astype(BF16)
+            if step == ZN // 2:
+                (out, far)[which][...] = rows
+            else:
+                out[which * HALF_ROWS : (which + 1) * HALF_ROWS] = rows
+
+
+def add_kernel(first, got, term, out):
+    rows = slice(first, first + got.shape[0])
+    if got.shape != term.shape:
+        out[...] = term[...]
+    out[rows] = (got[...].astype(F32) + term[rows].astype(F32)).astype(BF16)
 
 
 def column_kernel(own, up, down, mine, sent):
@@ -324,9 +331,11 @@
             blocks[ZN - step] = shift(blocks[(ZN - step + 1) % ZN], -1)
     total = total + add_count(total, 8)
     rows = shape((2, CHUNK, HD), BF16)
-    dqp, dq_own, dq_pair, *terms = call(
+    whole_keys = shape((2 * HALF_ROWS, HD), BF16)
+    dqp, dq_own, dq_pair, *terms, down = call(
         main_kernel, "s" + "v" * (ZN + 3),
-        [shape((CHUNK, HD), BF16), rows, rows] + [shape((2 * HALF_ROWS, HD), BF16)] * ZN,
+        [shape((CHUNK, HD), BF16), rows, rows]
+        + [whole_keys] * (ZN // 2) + [half_keys] + [whole_keys] * (ZN // 2 - 1) + [half_keys],
         [pltpu.VMEM((2 * ZN, 3, 2, ROWS, HD), BF16), pltpu.VMEM((2 * ZN, 3, 2, ROWS, HD), F32),
          pltpu.VMEM((4, CHUNK, HD), BF16), pltpu.VMEM((4, CHUNK, HD), BF16),
          pltpu.VMEM((4, CHUNK, HD), BF16), pltpu.VMEM((HD, CHUNK), F32),
@@ -334,14 +343,14 @@
         9 << 30, "main", BIG,
     )(lengths, total, own, got, *blocks)
 
-    def add(got, term):
-        return call(add_kernel, "vv", [shape((2 * HALF_ROWS, HD), BF16)], name="add")(got, term)[0]
-
-    up, down = terms[ZN // 2], terms[ZN // 2 + 1]
+    def add(got, term, first=0):
+        body = functools.partial(add_kernel, first)
+        return call(body, "vv", [whole_keys], name="add")(got, term)[0]
+
+    up = terms[ZN // 2]
     for step in range(ZN // 2 - 1, 0, -1):
         up = add(shift(up, 1), terms[step])
-        if step > 1:
-            down = add(shift(down, -1), terms[ZN - step + 1])
+        down = add(shift(down, -1), terms[ZN - step], HALF_ROWS if step == ZN // 2 - 1 else 0)
     mine, sent = call(column_kernel, "vvv", [shape((HALF_ROWS, HD), F32), half_keys], name="column")(
         terms[0], shift(up, 1), shift(down, -1)
     )

time: 92.2 us -> 88.8 us (0.963); the launches traced: 92.5 us -> 87.2 us
  starting transfers between devices: 35 us -> 46.7 us
  waiting for transfers between devices: 32.9 us -> 23 us
  Pallas kernels: 20.7 us -> 13.6 us
    ppermute x14 -> x15, waiting for transfers between devices: 24.6 us -> 14.7 us  [shift(): return lax.ppermute(value, 'resp', moves)]
    ppermute x4, starting transfers between devices: 6.76 us -> 14.7 us  [swap(): return lax.ppermute(value, 'resp', pair)]
    pallas_call x1, Pallas kernels: 14.7 us -> 7.54 us  [per_device(): call(main_kernel, 's' + 'v' * (ZN + 3), [shape((CHUNK, HD), BF16), rows,...]
    ppermute x14 -> x15, starting transfers between devices: 23.7 us -> 27.4 us  [shift(): return lax.ppermute(value, 'resp', moves)]
  transfers between devices with their start and end apart: 22 -> 23, of which waited for: 11 -> 11; matrix products, arithmetic and copies ran while one was open for 0% -> 0% of each run, Pallas kernels for 3% -> 3%
where the time goes in v3:
time: 88.8 us; the launch traced here: 87.2 us
  starting transfers between devices  46.7 us (53%)
  waiting for transfers between devices  23 us (26%)
  Pallas kernels  13.6 us (15%)
  local copies, waits for them, and re-layouts  3.12 us (4%)
    ppermute x15, starting transfers between devices, shift(): return lax.ppermute(value, 'resp', moves)  27.4 us
    ppermute x15, waiting for transfers between devices, shift(): return lax.ppermute(value, 'resp', moves)  14.7 us
    ppermute x4, starting transfers between devices, swap(): return lax.ppermute(value, 'resp', pair)  14.7 us
    pallas_call x1, Pallas kernels, per_device(): call(main_kernel, 's' + 'v' * (ZN + 3), [shape((CHUNK, HD), BF16), rows,...  7.54 us
    ppermute x4, waiting for transfers between devices, add_count(): lax.ppermute(value, 'prompt', [(i, i ^ step) for i in range(PROMPTS)])  7.16 us
    ppermute x4, starting transfers between devices, add_count(): lax.ppermute(value, 'prompt', [(i, i ^ step) for i in range(PROMPTS)])  4.53 us
    unnamed x20, local copies, waits for them, and re-layouts  3.12 us
  transfers between devices with their start and end apart: 23, of which 11 were waited for; matrix products, arithmetic and copies ran while one was open for 0% of the time, Pallas kernels for 3%

profile of v3, /device:TPU:16, one launch (start us, length us, event | category | flops | bytes accessed | tf_op | source)
XLA Modules:
  0.0 87.2 jit_solution(15644631547446282501)
XLA Ops:
  0.6 0.0 copy-start.4
  0.6 1.6 %keys.1 = (bf16[384,128]{1,0:T(8,128)(2,1)}, f32[8,128]{1,0:T(8,128)}) custom-call(s32[1,4]{1,0:T(1,128)} %lengths.11, bf16[1,4,64,128]{3,2,1,0:T(8,128)(2,1)} %kr.3, bf16[1,4,64,128]{3,2,1,0:T(8,128)(2,1)} %vr.3, bf16[1,64,128]{2,1,0:T(8,128)(2,1)} %kp.3, bf16[1,64,128]{2,1,0:T(8,128)(2,1)} %vp.3), custom_call_target="tpu_custom_call" | custom-call | flops 1048576 | bytes 2097152 | tf_op jit(solution)/shard_map/keys/pallas_call | solution.py:310
  2.2 1.5 %collective-permute-start = (bf16[384,128]{1,0:T(8,128)(2,1)}, bf16[384,128]{1,0:T(8,128)(2,1)S(1)}, u32[]{:S(2)}, u32[]{:S(2)}) collective-permute-start(bf16[384,128]{1,0:T(8,128)(2,1)} %get-tuple-element.37), channel_id=1, source_target_pairs={{0,8},{1,9},{2,10},{3,11},{4,12},{5,13},{6,14},{7,15},{8,0},{9,1},... | collective-permute-start | bytes 294920 | tf_op jit(solution)/shard_map/ppermute | solution.py:299
  3.7 0.0 copy-done.4
  3.7 0.0 copy-done.8
  3.7 1.0 %copy-done = bf16[1,4,64,1024]{3,2,1,0:T(8,128)(2,1)S(1)} copy-done((bf16[1,4,64,1024]{3,2,1,0:T(8,128)(2,1)S(1)}, bf16[1,4,64,1024]{3,2,1,0:T(8,128)(2,1)}, u32[]{:S(2)}) %copy-start) | copy-done | bytes 524312
  4.8 1.0 %copy-done.1 = bf16[1,4,64,1024]{3,2,1,0:T(8,128)(2,1)S(1)} copy-done((bf16[1,4,64,1024]{3,2,1,0:T(8,128)(2,1)S(1)}, bf16[1,4,64,1024]{3,2,1,0:T(8,128)(2,1)}, u32[]{:S(2)}) %copy-start.1) | copy-done | bytes 524312
  5.8 0.9 %copy-done.5 = bf16[1,64,1024]{2,1,0:T(8,128)(2,1)S(1)} copy-done((bf16[1,64,1024]{2,1,0:T(8,128)(2,1)S(1)}, bf16[1,64,1024]{2,1,0:T(8,128)(2,1)}, u32[]{:S(2)}) %copy-start.5) | copy-done | bytes 131096
  6.7 0.7 queries.1
  7.5 0.0 collective-permute-done.got
  7.5 0.1 copy-done.2
  7.6 0.0 copy-done.3
  7.6 0.0 copy-done.6
  7.6 0.6 block.1.rest_0_
  8.2 2.0 %collective-permute-start.1 = (bf16[768,128]{1,0:T(8,128)(2,1)S(1)}, bf16[768,128]{1,0:T(8,128)(2,1)S(1)}, u32[]{:S(2)}, u32[]{:S(2)}) collective-permute-start(bf16[768,128]{1,0:T(8,128)(2,1)S(1)} %block.1.rest_0_), channel_id=1, source_target_pairs={{0,1},{1,2},{2,3},{3,4},{4,5},{5,6},{6,7},{7,0},{8,9},{9,10},{10,1... | collective-permute-start | bytes 589832 | tf_op jit(solution)/shard_map/ppermute | solution.py:303
  10.2 2.7 %collective-permute-start.2 = (f32[8,128]{1,0:T(8,128)S(1)}, f32[8,128]{1,0:T(8,128)S(1)}, u32[]{:S(2)}, u32[]{:S(2)}) collective-permute-start(f32[8,128]{1,0:T(8,128)S(1)} %copy-done.9), channel_id=1, source_target_pairs={{0,32},{16,48},{32,0},{48,16},{64,96},{80,112},{96,64},{112,80},{1... | collective-permute-start | bytes 12296 | tf_op jit(solution)/shard_map/ppermute | solution.py:306
  12.9 2.4 %collective-permute-done.2 = f32[8,128]{1,0:T(8,128)S(1)} collective-permute-done((f32[8,128]{1,0:T(8,128)S(1)}, f32[8,128]{1,0:T(8,128)S(1)}, u32[]{:S(2)}, u32[]{:S(2)}) %collective-permute-start.2) | collective-permute-done | bytes 4128 | tf_op jit(solution)/shard_map/ppermute | solution.py:306
  15.3 4.0 %collective-permute-start.10 = (bf16[768,128]{1,0:T(8,128)(2,1)S(1)}, bf16[768,128]{1,0:T(8,128)(2,1)S(1)}, u32[]{:S(2)}, u32[]{:S(2)}) collective-permute-start(bf16[768,128]{1,0:T(8,128)(2,1)S(1)} %block.1.rest_0_), channel_id=1, source_target_pairs={{0,7},{1,0},{2,1},{3,2},{4,3},{5,4},{6,5},{7,6},{8,15},{9,8},{10,9... | collective-permute-start | bytes 589832 | tf_op jit(solution)/shard_map/ppermute | solution.py:303
  19.3 0.0 collective-permute-done.1.rest_1_
  19.4 0.0 collective-permute-start.3
  19.4 1.0 %collective-permute-start.8 = (bf16[2,2,512,128]{3,2,1,0:T(8,128)(2,1)S(1)}, bf16[2,2,512,128]{3,2,1,0:T(8,128)(2,1)S(1)}, u32[]{:S(2)}, u32[]{:S(2)}) collective-permute-start(bf16[2,2,512,128]{3,2,1,0:T(8,128)(2,1)S(1)} %get-tuple-element.46), channel_id=1, source_target_pairs={{0,8},{1,9},{2,10},{3,11},{4,12},{5,13},{6,14},{7,15},{8,0},{9,1},... | collective-permute-start | bytes 1572872 | tf_op jit(solution)/shard_map/ppermute | solution.py:299
  20.3 0.0 collective-permute-start.4
  20.3 2.2 %collective-permute-done.10.rest_7_ = bf16[768,128]{1,0:T(8,128)(2,1)S(1)} collective-permute-done((bf16[768,128]{1,0:T(8,128)(2,1)S(1)}, bf16[768,128]{1,0:T(8,128)(2,1)S(1)}, u32[]{:S(2)}, u32[]{:S(2)}) %collective-permute-start.10) | collective-permute-done | bytes 196640 | tf_op jit(solution)/shard_map/ppermute | solution.py:303
  22.5 3.7 %collective-permute-start.11 = (bf16[768,128]{1,0:T(8,128)(2,1)S(1)}, bf16[768,128]{1,0:T(8,128)(2,1)S(1)}, u32[]{:S(2)}, u32[]{:S(2)}) collective-permute-start(bf16[768,128]{1,0:T(8,128)(2,1)S(1)} %collective-permute-done.10.rest_7_), channel_id=1, source_target_pairs={{0,7},{1,0},{2,1},{3,2},{4,3},{5,4},{6,5},{7,6},{8,15},{9,8},{10,9... | collective-permute-start | bytes 589832 | tf_op jit(solution)/shard_map/ppermute | solution.py:303
  26.2 0.0 collective-permute-done.4
  26.2 0.0 collective-permute-done.3.rest_2_
  26.2 0.1 collective-permute-start.5
  26.3 1.4 %collective-permute-start.6 = (f32[8,128]{1,0:T(8,128)S(1)}, f32[8,128]{1,0:T(8,128)S(1)}, u32[]{:S(2)}, u32[]{:S(2)}) collective-permute-start(f32[8,128]{1,0:T(8,128)S(1)} %add.19), channel_id=1, source_target_pairs={{0,64},{16,80},{32,96},{48,112},{64,0},{80,16},{96,32},{112,48},{1... | collective-permute-start | bytes 12296 | tf_op jit(solution)/shard_map/ppermute | solution.py:306
  27.7 1.7 %collective-permute-done.11.rest_6_ = bf16[768,128]{1,0:T(8,128)(2,1)S(1)} collective-permute-done((bf16[768,128]{1,0:T(8,128)(2,1)S(1)}, bf16[768,128]{1,0:T(8,128)(2,1)S(1)}, u32[]{:S(2)}, u32[]{:S(2)}) %collective-permute-start.11) | collective-permute-done | bytes 196640 | tf_op jit(solution)/shard_map/ppermute | solution.py:303
  29.4 3.7 %collective-permute-start.12 = (bf16[768,128]{1,0:T(8,128)(2,1)S(1)}, bf16[768,128]{1,0:T(8,128)(2,1)S(1)}, u32[]{:S(2)}, u32[]{:S(2)}) collective-permute-start(bf16[768,128]{1,0:T(8,128)(2,1)S(1)} %collective-permute-done.11.rest_6_), channel_id=1, source_target_pairs={{0,7},{1,0},{2,1},{3,2},{4,3},{5,4},{6,5},{7,6},{8,15},{9,8},{10,9... | collective-permute-start | bytes 589832 | tf_op jit(solution)/shard_map/ppermute | solution.py:303
  33.1 0.0 collective-permute-done.6
  33.1 0.1 collective-permute-done.5.rest_3_
  33.2 0.0 collective-permute-start.9
  33.2 0.4 collective-permute-start.7
  33.6 4.8 %collective-permute-done.7 = f32[8,128]{1,0:T(8,128)S(1)} collective-permute-done((f32[8,128]{1,0:T(8,128)S(1)}, f32[8,128]{1,0:T(8,128)S(1)}, u32[]{:S(2)}, u32[]{:S(2)}) %collective-permute-start.7) | collective-permute-done | bytes 4128 | tf_op jit(solution)/shard_map/ppermute | solution.py:306
  38.4 0.0 collective-permute-done.8.got
  38.4 0.0 collective-permute-done.12.rest_5_
  38.4 1.7 %collective-permute-done.9.rest_4_ = bf16[768,128]{1,0:T(8,128)(2,1)S(1)} collective-permute-done((bf16[768,128]{1,0:T(8,128)(2,1)S(1)}, bf16[768,128]{1,0:T(8,128)(2,1)S(1)}, u32[]{:S(2)}, u32[]{:S(2)}) %collective-permute-start.9) | collective-permute-done | bytes 196640 | tf_op jit(solution)/shard_map/ppermute | solution.py:303
  40.1 7.5 %main.1 = (bf16[512,128]{1,0:T(8,128)(2,1)S(1)}, bf16[2,512,128]{2,1,0:T(8,128)(2,1)S(1)}, bf16[2,512,128]{2,1,0:T(8,128)(2,1)S(1)}, bf16[768,128]{1,0:T(8,128)(...) custom-call(s32[1,4]{1,0:T(1,128)S(1)} %copy-done.8, ...), custom_call_target="tpu_custom_call" | custom-call | flops 9663676416 | bytes 2097152 | tf_op jit(solution)/shard_map/main/pallas_call | solution.py:335
  47.6 2.4 %collective-permute-start.18 = (bf16[384,128]{1,0:T(8,128)(2,1)S(1)}, bf16[384,128]{1,0:T(8,128)(2,1)S(1)}, u32[]{:S(2)}, u32[]{:S(2)}) collective-permute-start(bf16[384,128]{1,0:T(8,128)(2,1)S(1)} %get-tuple-element.58), channel_id=1, source_target_pairs={{0,7},{1,0},{2,1},{3,2},{4,3},{5,4},{6,5},{7,6},{8,15},{9,8},{10,9... | collective-permute-start | bytes 294920 | tf_op jit(solution)/shard_map/ppermute | solution.py:303
  50.1 0.0 collective-permute-start.14
  50.1 2.2 %collective-permute-done.18.got = bf16[384,128]{1,0:T(8,128)(2,1)S(1)} collective-permute-done((bf16[384,128]{1,0:T(8,128)(2,1)S(1)}, bf16[384,128]{1,0:T(8,128)(2,1)S(1)}, u32[]{:S(2)}, u32[]{:S(2)}) %collective-permute-start.18) | collective-permute-done | bytes 98336 | tf_op jit(solution)/shard_map/ppermute | solution.py:303
  52.4 3.7 %collective-permute-start.19 = (bf16[768,128]{1,0:T(8,128)(2,1)S(1)}, bf16[768,128]{1,0:T(8,128)(2,1)S(1)}, u32[]{:S(2)}, u32[]{:S(2)}) collective-permute-start(bf16[768,128]{1,0:T(8,128)(2,1)S(1)} %add.25), channel_id=1, source_target_pairs={{0,7},{1,0},{2,1},{3,2},{4,3},{5,4},{6,5},{7,6},{8,15},{9,8},{10,9... | collective-permute-start | bytes 589832 | tf_op jit(solution)/shard_map/ppermute | solution.py:303
  56.0 0.0 collective-permute-done.14.got
  56.1 0.1 collective-permute-start.15
  56.2 3.0 %collective-permute-done.19.got = bf16[768,128]{1,0:T(8,128)(2,1)S(1)} collective-permute-done((bf16[768,128]{1,0:T(8,128)(2,1)S(1)}, bf16[768,128]{1,0:T(8,128)(2,1)S(1)}, u32[]{:S(2)}, u32[]{:S(2)}) %collective-permute-start.19) | collective-permute-done | bytes 196640 | tf_op jit(solution)/shard_map/ppermute | solution.py:303
  59.3 3.8 %collective-permute-start.20 = (bf16[768,128]{1,0:T(8,128)(2,1)S(1)}, bf16[768,128]{1,0:T(8,128)(2,1)S(1)}, u32[]{:S(2)}, u32[]{:S(2)}) collective-permute-start(bf16[768,128]{1,0:T(8,128)(2,1)S(1)} %add.26), channel_id=1, source_target_pairs={{0,7},{1,0},{2,1},{3,2},{4,3},{5,4},{6,5},{7,6},{8,15},{9,8},{10,9... | collective-permute-start | bytes 589832 | tf_op jit(solution)/shard_map/ppermute | solution.py:303
  63.0 0.0 collective-permute-done.15.got
  63.1 0.1 collective-permute-start.16
  63.2 3.0 %collective-permute-done.20.got = bf16[768,128]{1,0:T(8,128)(2,1)S(1)} collective-permute-done((bf16[768,128]{1,0:T(8,128)(2,1)S(1)}, bf16[768,128]{1,0:T(8,128)(2,1)S(1)}, u32[]{:S(2)}, u32[]{:S(2)}) %collective-permute-start.20) | collective-permute-done | bytes 196640 | tf_op jit(solution)/shard_map/ppermute | solution.py:303
  66.2 0.1 add.27
  66.3 3.8 %collective-permute-start.21 = (bf16[768,128]{1,0:T(8,128)(2,1)S(1)}, bf16[768,128]{1,0:T(8,128)(2,1)S(1)}, u32[]{:S(2)}, u32[]{:S(2)}) collective-permute-start(bf16[768,128]{1,0:T(8,128)(2,1)S(1)} %add.27), channel_id=1, source_target_pairs={{0,7},{1,0},{2,1},{3,2},{4,3},{5,4},{6,5},{7,6},{8,15},{9,8},{10,9... | collective-permute-start | bytes 589832 | tf_op jit(solution)/shard_map/ppermute | solution.py:303
  70.0 0.0 collective-permute-done.16.got
  70.0 0.1 add.24
  70.1 0.1 collective-permute-start.17
  70.2 6.1 %collective-permute-start.13 = (bf16[2,512,128]{2,1,0:T(8,128)(2,1)S(1)}, bf16[2,512,128]{2,1,0:T(8,128)(2,1)S(1)}, u32[]{:S(2)}, u32[]{:S(2)}) collective-permute-start(bf16[2,512,128]{2,1,0:T(8,128)(2,1)S(1)} %get-tuple-element.50), channel_id=1, source_target_pairs={{0,8},{1,9},{2,10},{3,11},{4,12},{5,13},{6,14},{7,15},{8,0},{9,1},... | collective-permute-start | bytes 786440 | tf_op jit(solution)/shard_map/ppermute | solution.py:299
  76.3 0.0 collective-permute-done.21.down
  76.3 0.7 collective-permute-done.17.up
  77.1 0.1 column.1
  77.1 6.1 %collective-permute-start.22 = (bf16[384,128]{1,0:T(8,128)(2,1)S(1)}, bf16[384,128]{1,0:T(8,128)(2,1)S(1)}, u32[]{:S(2)}, u32[]{:S(2)}) collective-permute-start(bf16[384,128]{1,0:T(8,128)(2,1)S(1)} %get-tuple-element.63), channel_id=1, source_target_pairs={{0,8},{1,9},{2,10},{3,11},{4,12},{5,13},{6,14},{7,15},{8,0},{9,1},... | collective-permute-start | bytes 294920 | tf_op jit(solution)/shard_map/ppermute | solution.py:299
  83.3 0.0 collective-permute-done.13.got
  83.3 1.5 %rows.1 = (bf16[1,64,1024]{2,1,0:T(8,128)(2,1)}, bf16[1,4,64,1024]{3,2,1,0:T(8,128)(2,1)}) custom-call(s32[1,4]{1,0:T(1,128)S(1)} %copy-done.8, bf16[512,128]{1,0:T(8,128)(2,1)S(1)} %get-tuple-element.48.prefix, bf16[2,512,128]{2,1,0:T(8,128)(2,1)S(1)} %get-tuple-element.49.own, bf16[2,512,128]{2,1,0:T(8,128)(2,1)S(1)} %collective-permute-done.13.got), custom_call_target="tpu_custom_call" | custom-call | flops 1048576 | bytes 2097152 | tf_op jit(solution)/shard_map/rows/pallas_call | solution.py:359
  84.7 1.1 %collective-permute-done.22.got = bf16[384,128]{1,0:T(8,128)(2,1)S(1)} collective-permute-done((bf16[384,128]{1,0:T(8,128)(2,1)S(1)}, bf16[384,128]{1,0:T(8,128)(2,1)S(1)}, u32[]{:S(2)}, u32[]{:S(2)}) %collective-permute-start.22) | collective-permute-done | bytes 98336 | tf_op jit(solution)/shard_map/ppermute | solution.py:299
  85.9 1.3 %sums.1 = (f32[1,64,128]{2,1,0:T(8,128)}, f32[1,64,128]{2,1,0:T(8,128)}, f32[1,4,64,128]{3,2,1,0:T(8,128)}, f32[1,4,64,128]{3,2,1,0:T(8,128)}) custom-call(s32[1,4]{1,0:T(1,128)S(1)} %copy-done.8, f32[8,128]{1,0:T(8,128)S(1)} %add.21.total, f32[384,128]{1,0:T(8,128)S(1)} %get-tuple-element.62.mine, bf16[384,128]{1,0:T(8,128)(2,1)S(1)} %collective-permute-done.22.got), custom_call_target="tpu_custom_call" | custom-call | flops 1048576 | bytes 2097152 | tf_op jit(solution)/shard_map/sums/pallas_call | solution.py:366
  (19 shorter events, 0.2 us)
Async XLA Ops:
  0.6 3.1 %copy-start.4 = (bf16[1,64,1024]{2,1,0:T(8,128)(2,1)S(1)}, bf16[1,64,1024]{2,1,0:T(8,128)(2,1)}, u32[]{:S(2)}) copy-start(bf16[1,64,1024]{2,1,0:T(8,128)(2,1)} %qp.1) | copy-start | bytes 393220
  2.2 1.5 %copy-start.8 = (s32[1,4]{1,0:T(1,128)S(1)}, s32[1,4]{1,0:T(1,128)}, u32[]{:S(2)}) copy-start(s32[1,4]{1,0:T(1,128)} %lengths.11) | copy-start | bytes 52
  2.2 5.2 %collective-permute-start = (bf16[384,128]{1,0:T(8,128)(2,1)}, bf16[384,128]{1,0:T(8,128)(2,1)S(1)}, u32[]{:S(2)}, u32[]{:S(2)}) collective-permute-start(bf16[384,128]{1,0:T(8,128)(2,1)} %get-tuple-element.37), channel_id=1, source_target_pairs={{0,8},{1,9},{2,10},{3,11},{4,12},{5,13},{6,14},{7,15},{8,0},{9,1},... | collective-permute-start | bytes 294920 | tf_op jit(solution)/shard_map/ppermute | solution.py:299
  3.7 1.0 %copy-start = (bf16[1,4,64,1024]{3,2,1,0:T(8,128)(2,1)S(1)}, bf16[1,4,64,1024]{3,2,1,0:T(8,128)(2,1)}, u32[]{:S(2)}) copy-start(bf16[1,4,64,1024]{3,2,1,0:T(8,128)(2,1)} %qr.1) | copy-start | bytes 1572868
  4.8 1.0 %copy-start.1 = (bf16[1,4,64,1024]{3,2,1,0:T(8,128)(2,1)S(1)}, bf16[1,4,64,1024]{3,2,1,0:T(8,128)(2,1)}, u32[]{:S(2)}) copy-start(bf16[1,4,64,1024]{3,2,1,0:T(8,128)(2,1)} %dr.1) | copy-start | bytes 1572868
  5.8 0.9 %copy-start.5 = (bf16[1,64,1024]{2,1,0:T(8,128)(2,1)S(1)}, bf16[1,64,1024]{2,1,0:T(8,128)(2,1)}, u32[]{:S(2)}) copy-start(bf16[1,64,1024]{2,1,0:T(8,128)(2,1)} %dp.1) | copy-start | bytes 393220
  6.7 0.8 copy-start.2
  6.7 0.9 copy-start.3
  6.7 0.9 copy-start.6
  6.7 0.9 copy-start.7
  7.6 2.6 %copy-start.9 = (f32[8,128]{1,0:T(8,128)S(1)}, f32[8,128]{1,0:T(8,128)}, u32[]{:S(2)}) copy-start(f32[8,128]{1,0:T(8,128)} %get-tuple-element.39) | copy-start | bytes 12292
  8.2 11.2 %collective-permute-start.1 = (bf16[768,128]{1,0:T(8,128)(2,1)S(1)}, bf16[768,128]{1,0:T(8,128)(2,1)S(1)}, u32[]{:S(2)}, u32[]{:S(2)}) collective-permute-start(bf16[768,128]{1,0:T(8,128)(2,1)S(1)} %block.1.rest_0_), channel_id=1, source_target_pairs={{0,1},{1,2},{2,3},{3,4},{4,5},{5,6},{6,7},{7,0},{8,9},{9,10},{10,1... | collective-permute-start | bytes 589832 | tf_op jit(solution)/shard_map/ppermute | solution.py:303
  10.2 5.1 %collective-permute-start.2 = (f32[8,128]{1,0:T(8,128)S(1)}, f32[8,128]{1,0:T(8,128)S(1)}, u32[]{:S(2)}, u32[]{:S(2)}) collective-permute-start(f32[8,128]{1,0:T(8,128)S(1)} %copy-done.9), channel_id=1, source_target_pairs={{0,32},{16,48},{32,0},{48,16},{64,96},{80,112},{96,64},{112,80},{1... | collective-permute-start | bytes 12296 | tf_op jit(solution)/shard_map/ppermute | solution.py:306
  15.3 7.2 %collective-permute-start.10 = (bf16[768,128]{1,0:T(8,128)(2,1)S(1)}, bf16[768,128]{1,0:T(8,128)(2,1)S(1)}, u32[]{:S(2)}, u32[]{:S(2)}) collective-permute-start(bf16[768,128]{1,0:T(8,128)(2,1)S(1)} %block.1.rest_0_), channel_id=1, source_target_pairs={{0,7},{1,0},{2,1},{3,2},{4,3},{5,4},{6,5},{7,6},{8,15},{9,8},{10,9... | collective-permute-start | bytes 589832 | tf_op jit(solution)/shard_map/ppermute | solution.py:303
  19.4 6.9 %collective-permute-start.3 = (bf16[768,128]{1,0:T(8,128)(2,1)S(1)}, bf16[768,128]{1,0:T(8,128)(2,1)S(1)}, u32[]{:S(2)}, u32[]{:S(2)}) collective-permute-start(bf16[768,128]{1,0:T(8,128)(2,1)S(1)} %collective-permute-done.1.rest_1_), channel_id=1, source_target_pairs={{0,1},{1,2},{2,3},{3,4},{4,5},{5,6},{6,7},{7,0},{8,9},{9,10},{10,1... | collective-permute-start | bytes 589832 | tf_op jit(solution)/shard_map/ppermute | solution.py:303
  19.4 19.1 %collective-permute-start.8 = (bf16[2,2,512,128]{3,2,1,0:T(8,128)(2,1)S(1)}, bf16[2,2,512,128]{3,2,1,0:T(8,128)(2,1)S(1)}, u32[]{:S(2)}, u32[]{:S(2)}) collective-permute-start(bf16[2,2,512,128]{3,2,1,0:T(8,128)(2,1)S(1)} %get-tuple-element.46), channel_id=1, source_target_pairs={{0,8},{1,9},{2,10},{3,11},{4,12},{5,13},{6,14},{7,15},{8,0},{9,1},... | collective-permute-start | bytes 1572872 | tf_op jit(solution)/shard_map/ppermute | solution.py:299
  20.3 5.9 %collective-permute-start.4 = (f32[8,128]{1,0:T(8,128)S(1)}, f32[8,128]{1,0:T(8,128)S(1)}, u32[]{:S(2)}, u32[]{:S(2)}) collective-permute-start(f32[8,128]{1,0:T(8,128)S(1)} %add.18), channel_id=1, source_target_pairs={{0,16},{16,0},{32,48},{48,32},{64,80},{80,64},{96,112},{112,96},{1... | collective-permute-start | bytes 12296 | tf_op jit(solution)/shard_map/ppermute | solution.py:306
  22.5 6.9 %collective-permute-start.11 = (bf16[768,128]{1,0:T(8,128)(2,1)S(1)}, bf16[768,128]{1,0:T(8,128)(2,1)S(1)}, u32[]{:S(2)}, u32[]{:S(2)}) collective-permute-start(bf16[768,128]{1,0:T(8,128)(2,1)S(1)} %collective-permute-done.10.rest_7_), channel_id=1, source_target_pairs={{0,7},{1,0},{2,1},{3,2},{4,3},{5,4},{6,5},{7,6},{8,15},{9,8},{10,9... | collective-permute-start | bytes 589832 | tf_op jit(solution)/shard_map/ppermute | solution.py:303
  26.2 7.0 %collective-permute-start.5 = (bf16[768,128]{1,0:T(8,128)(2,1)S(1)}, bf16[768,128]{1,0:T(8,128)(2,1)S(1)}, u32[]{:S(2)}, u32[]{:S(2)}) collective-permute-start(bf16[768,128]{1,0:T(8,128)(2,1)S(1)} %collective-permute-done.3.rest_2_), channel_id=1, source_target_pairs={{0,1},{1,2},{2,3},{3,4},{4,5},{5,6},{6,7},{7,0},{8,9},{9,10},{10,1... | collective-permute-start | bytes 589832 | tf_op jit(solution)/shard_map/ppermute | solution.py:303
  26.3 6.8 %collective-permute-start.6 = (f32[8,128]{1,0:T(8,128)S(1)}, f32[8,128]{1,0:T(8,128)S(1)}, u32[]{:S(2)}, u32[]{:S(2)}) collective-permute-start(f32[8,128]{1,0:T(8,128)S(1)} %add.19), channel_id=1, source_target_pairs={{0,64},{16,80},{32,96},{48,112},{64,0},{80,16},{96,32},{112,48},{1... | collective-permute-start | bytes 12296 | tf_op jit(solution)/shard_map/ppermute | solution.py:306
  29.4 9.0 %collective-permute-start.12 = (bf16[768,128]{1,0:T(8,128)(2,1)S(1)}, bf16[768,128]{1,0:T(8,128)(2,1)S(1)}, u32[]{:S(2)}, u32[]{:S(2)}) collective-permute-start(bf16[768,128]{1,0:T(8,128)(2,1)S(1)} %collective-permute-done.11.rest_6_), channel_id=1, source_target_pairs={{0,7},{1,0},{2,1},{3,2},{4,3},{5,4},{6,5},{7,6},{8,15},{9,8},{10,9... | collective-permute-start | bytes 589832 | tf_op jit(solution)/shard_map/ppermute | solution.py:303
  33.2 6.9 %collective-permute-start.9 = (bf16[768,128]{1,0:T(8,128)(2,1)S(1)}, bf16[768,128]{1,0:T(8,128)(2,1)S(1)}, u32[]{:S(2)}, u32[]{:S(2)}) collective-permute-start(bf16[768,128]{1,0:T(8,128)(2,1)S(1)} %collective-permute-done.5.rest_3_), channel_id=1, source_target_pairs={{0,1},{1,2},{2,3},{3,4},{4,5},{5,6},{6,7},{7,0},{8,9},{9,10},{10,1... | collective-permute-start | bytes 589832 | tf_op jit(solution)/shard_map/ppermute | solution.py:303
  33.2 5.2 %collective-permute-start.7 = (f32[8,128]{1,0:T(8,128)S(1)}, f32[8,128]{1,0:T(8,128)S(1)}, u32[]{:S(2)}, u32[]{:S(2)}) collective-permute-start(f32[8,128]{1,0:T(8,128)S(1)} %add.20), channel_id=1, source_target_pairs={{0,128},{16,144},{32,160},{48,176},{64,192},{80,208},{96,224},{112... | collective-permute-start | bytes 12296 | tf_op jit(solution)/shard_map/ppermute | solution.py:306
  47.6 4.7 %collective-permute-start.18 = (bf16[384,128]{1,0:T(8,128)(2,1)S(1)}, bf16[384,128]{1,0:T(8,128)(2,1)S(1)}, u32[]{:S(2)}, u32[]{:S(2)}) collective-permute-start(bf16[384,128]{1,0:T(8,128)(2,1)S(1)} %get-tuple-element.58), channel_id=1, source_target_pairs={{0,7},{1,0},{2,1},{3,2},{4,3},{5,4},{6,5},{7,6},{8,15},{9,8},{10,9... | collective-permute-start | bytes 294920 | tf_op jit(solution)/shard_map/ppermute | solution.py:303
  50.1 5.9 %collective-permute-start.14 = (bf16[384,128]{1,0:T(8,128)(2,1)S(1)}, bf16[384,128]{1,0:T(8,128)(2,1)S(1)}, u32[]{:S(2)}, u32[]{:S(2)}) collective-permute-start(bf16[384,128]{1,0:T(8,128)(2,1)S(1)} %get-tuple-element.54), channel_id=1, source_target_pairs={{0,1},{1,2},{2,3},{3,4},{4,5},{5,6},{6,7},{7,0},{8,9},{9,10},{10,1... | collective-permute-start | bytes 294920 | tf_op jit(solution)/shard_map/ppermute | solution.py:303
  52.4 6.8 %collective-permute-start.19 = (bf16[768,128]{1,0:T(8,128)(2,1)S(1)}, bf16[768,128]{1,0:T(8,128)(2,1)S(1)}, u32[]{:S(2)}, u32[]{:S(2)}) collective-permute-start(bf16[768,128]{1,0:T(8,128)(2,1)S(1)} %add.25), channel_id=1, source_target_pairs={{0,7},{1,0},{2,1},{3,2},{4,3},{5,4},{6,5},{7,6},{8,15},{9,8},{10,9... | collective-permute-start | bytes 589832 | tf_op jit(solution)/shard_map/ppermute | solution.py:303
  56.1 7.0 %collective-permute-start.15 = (bf16[768,128]{1,0:T(8,128)(2,1)S(1)}, bf16[768,128]{1,0:T(8,128)(2,1)S(1)}, u32[]{:S(2)}, u32[]{:S(2)}) collective-permute-start(bf16[768,128]{1,0:T(8,128)(2,1)S(1)} %add.22), channel_id=1, source_target_pairs={{0,1},{1,2},{2,3},{3,4},{4,5},{5,6},{6,7},{7,0},{8,9},{9,10},{10,1... | collective-permute-start | bytes 589832 | tf_op jit(solution)/shard_map/ppermute | solution.py:303
  59.3 7.0 %collective-permute-start.20 = (bf16[768,128]{1,0:T(8,128)(2,1)S(1)}, bf16[768,128]{1,0:T(8,128)(2,1)S(1)}, u32[]{:S(2)}, u32[]{:S(2)}) collective-permute-start(bf16[768,128]{1,0:T(8,128)(2,1)S(1)} %add.26), channel_id=1, source_target_pairs={{0,7},{1,0},{2,1},{3,2},{4,3},{5,4},{6,5},{7,6},{8,15},{9,8},{10,9... | collective-permute-start | bytes 589832 | tf_op jit(solution)/shard_map/ppermute | solution.py:303
  63.1 7.0 %collective-permute-start.16 = (bf16[768,128]{1,0:T(8,128)(2,1)S(1)}, bf16[768,128]{1,0:T(8,128)(2,1)S(1)}, u32[]{:S(2)}, u32[]{:S(2)}) collective-permute-start(bf16[768,128]{1,0:T(8,128)(2,1)S(1)} %add.23), channel_id=1, source_target_pairs={{0,1},{1,2},{2,3},{3,4},{4,5},{5,6},{6,7},{7,0},{8,9},{9,10},{10,1... | collective-permute-start | bytes 589832 | tf_op jit(solution)/shard_map/ppermute | solution.py:303
  66.3 10.0 %collective-permute-start.21 = (bf16[768,128]{1,0:T(8,128)(2,1)S(1)}, bf16[768,128]{1,0:T(8,128)(2,1)S(1)}, u32[]{:S(2)}, u32[]{:S(2)}) collective-permute-start(bf16[768,128]{1,0:T(8,128)(2,1)S(1)} %add.27), channel_id=1, source_target_pairs={{0,7},{1,0},{2,1},{3,2},{4,3},{5,4},{6,5},{7,6},{8,15},{9,8},{10,9... | collective-permute-start | bytes 589832 | tf_op jit(solution)/shard_map/ppermute | solution.py:303
  70.1 7.0 %collective-permute-start.17 = (bf16[768,128]{1,0:T(8,128)(2,1)S(1)}, bf16[768,128]{1,0:T(8,128)(2,1)S(1)}, u32[]{:S(2)}, u32[]{:S(2)}) collective-permute-start(bf16[768,128]{1,0:T(8,128)(2,1)S(1)} %add.24), channel_id=1, source_target_pairs={{0,1},{1,2},{2,3},{3,4},{4,5},{5,6},{6,7},{7,0},{8,9},{9,10},{10,1... | collective-permute-start | bytes 589832 | tf_op jit(solution)/shard_map/ppermute | solution.py:303
  70.2 13.1 %collective-permute-start.13 = (bf16[2,512,128]{2,1,0:T(8,128)(2,1)S(1)}, bf16[2,512,128]{2,1,0:T(8,128)(2,1)S(1)}, u32[]{:S(2)}, u32[]{:S(2)}) collective-permute-start(bf16[2,512,128]{2,1,0:T(8,128)(2,1)S(1)} %get-tuple-element.50), channel_id=1, source_target_pairs={{0,8},{1,9},{2,10},{3,11},{4,12},{5,13},{6,14},{7,15},{8,0},{9,1},... | collective-permute-start | bytes 786440 | tf_op jit(solution)/shard_map/ppermute | solution.py:299
  77.1 8.7 %collective-permute-start.22 = (bf16[384,128]{1,0:T(8,128)(2,1)S(1)}, bf16[384,128]{1,0:T(8,128)(2,1)S(1)}, u32[]{:S(2)}, u32[]{:S(2)}) collective-permute-start(bf16[384,128]{1,0:T(8,128)(2,1)S(1)} %get-tuple-element.63), channel_id=1, source_target_pairs={{0,8},{1,9},{2,10},{3,11},{4,12},{5,13},{6,14},{7,15},{8,0},{9,1},... | collective-permute-start | bytes 294920 | tf_op jit(solution)/shard_map/ppermute | solution.py:299

commit v4 on v3

--- a/solution.py
+++ b/solution.py
@@ -186,7 +186,7 @@
 def main_kernel(lengths, total, own, got, *rest):
     blocks, rest = rest[:ZN], rest[ZN:]
     dqp_out, dq_own, dq_pair, rest = rest[0], rest[1], rest[2], rest[3:]
-    terms, (far, kv, acc, q_st, d_st, dq_st, *work) = rest[:ZN], rest[ZN:]
+    terms, (far, near, kv, acc, q_st, d_st, dq_st, *work) = rest[:ZN], rest[ZN:]
     half, z = place()
     factor = token_factor(total) * SCALE
     for step, block in enumerate(blocks):
@@ -231,7 +231,9 @@
         for which in range(2):
             at = (half ^ which) * ZN + ((z + step) & (ZN - 1))
             rows = acc[at].reshape(HALF_ROWS, HD).astype(BF16)
-            if step == ZN // 2:
+            if step == 0:
+                (out, near)[which][...] = rows
+            elif step == ZN // 2:
                 (out, far)[which][...] = rows
             else:
                 out[which * HALF_ROWS : (which + 1) * HALF_ROWS] = rows
@@ -244,10 +246,10 @@
     out[rows] = (got[...].astype(F32) + term[rows].astype(F32)).astype(BF16)
 
 
-def column_kernel(own, up, down, mine, sent):
-    total = own[...].astype(F32) + up[...].astype(F32) + down[...].astype(F32)
-    mine[...] = total[:HALF_ROWS]
-    sent[...] = total[HALF_ROWS:].astype(BF16)
+def last_add_kernel(got, term, same, other):
+    for at, out in enumerate((same, other)):
+        rows = slice(at * HALF_ROWS, (at + 1) * HALF_ROWS)
+        out[...] = (got[rows].astype(F32) + term[rows].astype(F32)).astype(BF16)
 
 
 def rows_kernel(lengths, prefix, own, got, prefix_out, out):
@@ -260,16 +262,21 @@
         out[0, resp] = unstack_heads(got[slot])
 
 
-def sums_kernel(lengths, total, mine, got, dkp, dvp, dkr, dvr):
+def sums_kernel(lengths, total, *rest):
+    mine, got, (dkp, dvp, dkr, dvr) = rest[:3], rest[3:6], rest[6:]
     half, _ = place()
     both = dealt(lengths)
     factor = token_factor(total)
+
+    def summed(sources, block):
+        rows = slice(block * ROWS, (block + 1) * ROWS)
+        return sum(source[rows].astype(F32) for source in sources)
+
     for kind, outs, by in ((0, (dkp, dkr), factor * SCALE), (1, (dvp, dvr), factor)):
-        outs[0][0] = (mine[kind * ROWS : (kind + 1) * ROWS] + got[kind * ROWS : (kind + 1) * ROWS].astype(F32)) * by
-        for source, responses in ((mine, of_half(both, half)), (got, of_half(both, 1 - half))):
+        outs[0][0] = (summed(mine, kind) + summed(got, kind)) * by
+        for sources, responses in ((mine, of_half(both, half)), (got, of_half(both, 1 - half))):
             for slot, resp in enumerate(responses):
-                at = ((1 + slot) * 2 + kind) * ROWS
-                outs[1][0, resp] = source[at : at + ROWS].astype(F32) * by
+                outs[1][0, resp] = summed(sources, (1 + slot) * 2 + kind) * by
 
 
 def shape(dims, dtype):
@@ -332,10 +339,10 @@
     total = total + add_count(total, 8)
     rows = shape((2, CHUNK, HD), BF16)
     whole_keys = shape((2 * HALF_ROWS, HD), BF16)
-    dqp, dq_own, dq_pair, *terms, down = call(
+    dqp, dq_own, dq_pair, *terms, down, near = call(
         main_kernel, "s" + "v" * (ZN + 3),
         [shape((CHUNK, HD), BF16), rows, rows]
-        + [whole_keys] * (ZN // 2) + [half_keys] + [whole_keys] * (ZN // 2 - 1) + [half_keys],
+        + ([half_keys] + [whole_keys] * (ZN // 2 - 1)) * 2 + [half_keys] * 2,
         [pltpu.VMEM((2 * ZN, 3, 2, ROWS, HD), BF16), pltpu.VMEM((2 * ZN, 3, 2, ROWS, HD), F32),
          pltpu.VMEM((4, CHUNK, HD), BF16), pltpu.VMEM((4, CHUNK, HD), BF16),
          pltpu.VMEM((4, CHUNK, HD), BF16), pltpu.VMEM((HD, CHUNK), F32),
@@ -347,14 +354,20 @@
         body = functools.partial(add_kernel, first)
         return call(body, "vv", [whole_keys], name="add")(got, term)[0]
 
+    def last(got, term, by):
+        same, other = call(last_add_kernel, "vv", [half_keys] * 2, name="last")(got, term)
+        moves = [
+            (c + i, (c + ZN) % (2 * ZN) + (i + by) % ZN) for c in (0, ZN) for i in range(ZN)
+        ]
+        return shift(same, by), lax.ppermute(other, "resp", moves)
+
     up = terms[ZN // 2]
-    for step in range(ZN // 2 - 1, 0, -1):
+    for step in range(ZN // 2 - 1, 1, -1):
         up = add(shift(up, 1), terms[step])
         down = add(shift(down, -1), terms[ZN - step], HALF_ROWS if step == ZN // 2 - 1 else 0)
-    mine, sent = call(column_kernel, "vvv", [shape((HALF_ROWS, HD), F32), half_keys], name="column")(
-        terms[0], shift(up, 1), shift(down, -1)
-    )
-    terms_got = swap(sent)
+    up, up_got = last(shift(up, 1), terms[1], 1)
+    down, down_got = last(shift(down, -1), terms[ZN - 1], -1)
+    near_got = swap(near)
     dq_got = swap(dq_pair)
     dqp_out, dq_all = call(
         rows_kernel, "svvv",
@@ -364,9 +377,9 @@
     prefix_out = shape((1, ROWS, HD), F32)
     resp_out = shape((1, RESPS, ROWS, HD), F32)
     dkp, dvp, dkr, dvr = call(
-        sums_kernel, "svvv", [prefix_out, prefix_out, resp_out, resp_out],
+        sums_kernel, "s" + "v" * 7, [prefix_out, prefix_out, resp_out, resp_out],
         name="sums",
-    )(lengths, total, mine, terms_got)
+    )(lengths, total, terms[0], up, down, near_got, up_got, down_got)
     return dqp_out, dq_all, dkp, dvp, dkr, dvr
 
 

time: 88.8 us -> 87.1 us (0.981); the launches traced: 87.2 us -> 86.8 us
  waiting for transfers between devices: 23 us -> 20.7 us
  starting transfers between devices: 46.7 us -> 48.8 us
    ppermute x0 -> x2, starting transfers between devices: none -> 4.09 us  [last(): return (shift(same, by), lax.ppermute(other, 'resp', moves))]
    ppermute x15, waiting for transfers between devices: 14.7 us -> 10.7 us  [shift(): return lax.ppermute(value, 'resp', moves)]
    ppermute x0 -> x2, waiting for transfers between devices: none -> 2.84 us  [last(): return (shift(same, by), lax.ppermute(other, 'resp', moves))]
    ppermute x4, starting transfers between devices: 14.7 us -> 13.6 us  [swap(): return lax.ppermute(value, 'resp', pair)]
    ppermute x4, waiting for transfers between devices: 1.14 us -> 0.01 us  [swap(): return lax.ppermute(value, 'resp', pair)]
  transfers between devices with their start and end apart: 23 -> 25, of which waited for: 11 -> 9; matrix products, arithmetic and copies ran while one was open for 0% -> 0% of each run, Pallas kernels for 3% -> 3%
where the time goes in v4:
time: 87.1 us; the launch traced here: 86.8 us
  starting transfers between devices  48.8 us (56%)
  waiting for transfers between devices  20.7 us (24%)
  Pallas kernels  13.5 us (15%)
  local copies, waits for them, and re-layouts  3.12 us (4%)
    ppermute x15, starting transfers between devices, shift(): return lax.ppermute(value, 'resp', moves)  26.6 us
    ppermute x4, starting transfers between devices, swap(): return lax.ppermute(value, 'resp', pair)  13.6 us
    ppermute x15, waiting for transfers between devices, shift(): return lax.ppermute(value, 'resp', moves)  10.7 us
    pallas_call x1, Pallas kernels, per_device(): call(main_kernel, 's' + 'v' * (ZN + 3), [shape((CHUNK, HD), BF16), rows,...  7.52 us
    ppermute x4, waiting for transfers between devices, add_count(): lax.ppermute(value, 'prompt', [(i, i ^ step) for i in range(PROMPTS)])  7.16 us
    ppermute x4, starting transfers between devices, add_count(): lax.ppermute(value, 'prompt', [(i, i ^ step) for i in range(PROMPTS)])  4.53 us
    ppermute x2, starting transfers between devices, last(): return (shift(same, by), lax.ppermute(other, 'resp', moves))  4.09 us
    unnamed x20, local copies, waits for them, and re-layouts  3.12 us
  transfers between devices with their start and end apart: 25, of which 9 were waited for; matrix products, arithmetic and copies ran while one was open for 0% of the time, Pallas kernels for 3%

profile of v4, /device:TPU:16, one launch (start us, length us, event | category | flops | bytes accessed | tf_op | source)
XLA Modules:
  0.0 86.8 jit_solution(9337190099528633972)
XLA Ops:
  0.6 0.0 copy-start.4
  0.6 1.6 %keys.1 = (bf16[384,128]{1,0:T(8,128)(2,1)}, f32[8,128]{1,0:T(8,128)}) custom-call(s32[1,4]{1,0:T(1,128)} %lengths.11, bf16[1,4,64,128]{3,2,1,0:T(8,128)(2,1)} %kr.3, bf16[1,4,64,128]{3,2,1,0:T(8,128)(2,1)} %vr.3, bf16[1,64,128]{2,1,0:T(8,128)(2,1)} %kp.3, bf16[1,64,128]{2,1,0:T(8,128)(2,1)} %vp.3), custom_call_target="tpu_custom_call" | custom-call | flops 1048576 | bytes 2097152 | tf_op jit(solution)/shard_map/keys/pallas_call | solution.py:317
  2.2 1.5 %collective-permute-start = (bf16[384,128]{1,0:T(8,128)(2,1)}, bf16[384,128]{1,0:T(8,128)(2,1)S(1)}, u32[]{:S(2)}, u32[]{:S(2)}) collective-permute-start(bf16[384,128]{1,0:T(8,128)(2,1)} %get-tuple-element.40), channel_id=1, source_target_pairs={{0,8},{1,9},{2,10},{3,11},{4,12},{5,13},{6,14},{7,15},{8,0},{9,1},... | collective-permute-start | bytes 294920 | tf_op jit(solution)/shard_map/ppermute | solution.py:306
  3.7 0.0 copy-done.8
  3.7 1.0 %copy-done = bf16[1,4,64,1024]{3,2,1,0:T(8,128)(2,1)S(1)} copy-done((bf16[1,4,64,1024]{3,2,1,0:T(8,128)(2,1)S(1)}, bf16[1,4,64,1024]{3,2,1,0:T(8,128)(2,1)}, u32[]{:S(2)}) %copy-start) | copy-done | bytes 524312
  4.8 1.0 %copy-done.1 = bf16[1,4,64,1024]{3,2,1,0:T(8,128)(2,1)S(1)} copy-done((bf16[1,4,64,1024]{3,2,1,0:T(8,128)(2,1)S(1)}, bf16[1,4,64,1024]{3,2,1,0:T(8,128)(2,1)}, u32[]{:S(2)}) %copy-start.1) | copy-done | bytes 524312
  5.8 0.9 %copy-done.5 = bf16[1,64,1024]{2,1,0:T(8,128)(2,1)S(1)} copy-done((bf16[1,64,1024]{2,1,0:T(8,128)(2,1)S(1)}, bf16[1,64,1024]{2,1,0:T(8,128)(2,1)}, u32[]{:S(2)}) %copy-start.5) | copy-done | bytes 131096
  6.7 0.7 queries.1
  7.5 0.0 collective-permute-done.got
  7.5 0.1 copy-done.2
  7.6 0.0 copy-done.3
  7.6 0.6 block.1.rest_0_
  8.2 2.0 %collective-permute-start.1 = (bf16[768,128]{1,0:T(8,128)(2,1)S(1)}, bf16[768,128]{1,0:T(8,128)(2,1)S(1)}, u32[]{:S(2)}, u32[]{:S(2)}) collective-permute-start(bf16[768,128]{1,0:T(8,128)(2,1)S(1)} %block.1.rest_0_), channel_id=1, source_target_pairs={{0,1},{1,2},{2,3},{3,4},{4,5},{5,6},{6,7},{7,0},{8,9},{9,10},{10,1... | collective-permute-start | bytes 589832 | tf_op jit(solution)/shard_map/ppermute | solution.py:310
  10.2 2.7 %collective-permute-start.2 = (f32[8,128]{1,0:T(8,128)S(1)}, f32[8,128]{1,0:T(8,128)S(1)}, u32[]{:S(2)}, u32[]{:S(2)}) collective-permute-start(f32[8,128]{1,0:T(8,128)S(1)} %copy-done.9), channel_id=1, source_target_pairs={{0,32},{16,48},{32,0},{48,16},{64,96},{80,112},{96,64},{112,80},{1... | collective-permute-start | bytes 12296 | tf_op jit(solution)/shard_map/ppermute | solution.py:313
  12.9 2.4 %collective-permute-done.2 = f32[8,128]{1,0:T(8,128)S(1)} collective-permute-done((f32[8,128]{1,0:T(8,128)S(1)}, f32[8,128]{1,0:T(8,128)S(1)}, u32[]{:S(2)}, u32[]{:S(2)}) %collective-permute-start.2) | collective-permute-done | bytes 4128 | tf_op jit(solution)/shard_map/ppermute | solution.py:313
  15.3 4.0 %collective-permute-start.10 = (bf16[768,128]{1,0:T(8,128)(2,1)S(1)}, bf16[768,128]{1,0:T(8,128)(2,1)S(1)}, u32[]{:S(2)}, u32[]{:S(2)}) collective-permute-start(bf16[768,128]{1,0:T(8,128)(2,1)S(1)} %block.1.rest_0_), channel_id=1, source_target_pairs={{0,7},{1,0},{2,1},{3,2},{4,3},{5,4},{6,5},{7,6},{8,15},{9,8},{10,9... | collective-permute-start | bytes 589832 | tf_op jit(solution)/shard_map/ppermute | solution.py:310
  19.3 0.0 collective-permute-done.1.rest_1_
  19.4 0.0 collective-permute-start.3
  19.4 1.0 %collective-permute-start.8 = (bf16[2,2,512,128]{3,2,1,0:T(8,128)(2,1)S(1)}, bf16[2,2,512,128]{3,2,1,0:T(8,128)(2,1)S(1)}, u32[]{:S(2)}, u32[]{:S(2)}) collective-permute-start(bf16[2,2,512,128]{3,2,1,0:T(8,128)(2,1)S(1)} %get-tuple-element.49), channel_id=1, source_target_pairs={{0,8},{1,9},{2,10},{3,11},{4,12},{5,13},{6,14},{7,15},{8,0},{9,1},... | collective-permute-start | bytes 1572872 | tf_op jit(solution)/shard_map/ppermute | solution.py:306
  20.3 0.0 collective-permute-start.4
  20.3 2.2 %collective-permute-done.10.rest_7_ = bf16[768,128]{1,0:T(8,128)(2,1)S(1)} collective-permute-done((bf16[768,128]{1,0:T(8,128)(2,1)S(1)}, bf16[768,128]{1,0:T(8,128)(2,1)S(1)}, u32[]{:S(2)}, u32[]{:S(2)}) %collective-permute-start.10) | collective-permute-done | bytes 196640 | tf_op jit(solution)/shard_map/ppermute | solution.py:310
  22.5 3.7 %collective-permute-start.11 = (bf16[768,128]{1,0:T(8,128)(2,1)S(1)}, bf16[768,128]{1,0:T(8,128)(2,1)S(1)}, u32[]{:S(2)}, u32[]{:S(2)}) collective-permute-start(bf16[768,128]{1,0:T(8,128)(2,1)S(1)} %collective-permute-done.10.rest_7_), channel_id=1, source_target_pairs={{0,7},{1,0},{2,1},{3,2},{4,3},{5,4},{6,5},{7,6},{8,15},{9,8},{10,9... | collective-permute-start | bytes 589832 | tf_op jit(solution)/shard_map/ppermute | solution.py:310
  26.2 0.0 collective-permute-done.4
  26.2 0.0 collective-permute-done.3.rest_2_
  26.2 0.1 collective-permute-start.5
  26.3 1.4 %collective-permute-start.6 = (f32[8,128]{1,0:T(8,128)S(1)}, f32[8,128]{1,0:T(8,128)S(1)}, u32[]{:S(2)}, u32[]{:S(2)}) collective-permute-start(f32[8,128]{1,0:T(8,128)S(1)} %add.17), channel_id=1, source_target_pairs={{0,64},{16,80},{32,96},{48,112},{64,0},{80,16},{96,32},{112,48},{1... | collective-permute-start | bytes 12296 | tf_op jit(solution)/shard_map/ppermute | solution.py:313
  27.7 1.7 %collective-permute-done.11.rest_6_ = bf16[768,128]{1,0:T(8,128)(2,1)S(1)} collective-permute-done((bf16[768,128]{1,0:T(8,128)(2,1)S(1)}, bf16[768,128]{1,0:T(8,128)(2,1)S(1)}, u32[]{:S(2)}, u32[]{:S(2)}) %collective-permute-start.11) | collective-permute-done | bytes 196640 | tf_op jit(solution)/shard_map/ppermute | solution.py:310
  29.4 3.7 %collective-permute-start.12 = (bf16[768,128]{1,0:T(8,128)(2,1)S(1)}, bf16[768,128]{1,0:T(8,128)(2,1)S(1)}, u32[]{:S(2)}, u32[]{:S(2)}) collective-permute-start(bf16[768,128]{1,0:T(8,128)(2,1)S(1)} %collective-permute-done.11.rest_6_), channel_id=1, source_target_pairs={{0,7},{1,0},{2,1},{3,2},{4,3},{5,4},{6,5},{7,6},{8,15},{9,8},{10,9... | collective-permute-start | bytes 589832 | tf_op jit(solution)/shard_map/ppermute | solution.py:310
  33.1 0.0 collective-permute-done.6
  33.1 0.1 collective-permute-done.5.rest_3_
  33.2 0.0 collective-permute-start.9
  33.2 0.4 collective-permute-start.7
  33.6 4.8 %collective-permute-done.7 = f32[8,128]{1,0:T(8,128)S(1)} collective-permute-done((f32[8,128]{1,0:T(8,128)S(1)}, f32[8,128]{1,0:T(8,128)S(1)}, u32[]{:S(2)}, u32[]{:S(2)}) %collective-permute-start.7) | collective-permute-done | bytes 4128 | tf_op jit(solution)/shard_map/ppermute | solution.py:313
  38.4 0.0 collective-permute-done.8.got
  38.4 0.0 collective-permute-done.12.rest_5_
  38.4 1.7 %collective-permute-done.9.rest_4_ = bf16[768,128]{1,0:T(8,128)(2,1)S(1)} collective-permute-done((bf16[768,128]{1,0:T(8,128)(2,1)S(1)}, bf16[768,128]{1,0:T(8,128)(2,1)S(1)}, u32[]{:S(2)}, u32[]{:S(2)}) %collective-permute-start.9) | collective-permute-done | bytes 196640 | tf_op jit(solution)/shard_map/ppermute | solution.py:310
  40.1 7.5 %main.1 = (bf16[512,128]{1,0:T(8,128)(2,1)S(1)}, bf16[2,512,128]{2,1,0:T(8,128)(2,1)S(1)}, bf16[2,512,128]{2,1,0:T(8,128)(2,1)S(1)}, bf16[384,128]{1,0:T(8,128)(...) custom-call(s32[1,4]{1,0:T(1,128)S(1)} %copy-done.8, ...), custom_call_target="tpu_custom_call" | custom-call | flops 9663676416 | bytes 2097152 | tf_op jit(solution)/shard_map/main/pallas_call | solution.py:342
  47.6 0.1 collective-permute-start.18
  47.7 2.0 %collective-permute-start.14 = (bf16[384,128]{1,0:T(8,128)(2,1)S(1)}, bf16[384,128]{1,0:T(8,128)(2,1)S(1)}, u32[]{:S(2)}, u32[]{:S(2)}) collective-permute-start(bf16[384,128]{1,0:T(8,128)(2,1)S(1)} %get-tuple-element.57), channel_id=1, source_target_pairs={{0,1},{1,2},{2,3},{3,4},{4,5},{5,6},{6,7},{7,0},{8,9},{9,10},{10,1... | collective-permute-start | bytes 294920 | tf_op jit(solution)/shard_map/ppermute | solution.py:310
  49.7 2.6 %collective-permute-done.18.got = bf16[384,128]{1,0:T(8,128)(2,1)S(1)} collective-permute-done((bf16[384,128]{1,0:T(8,128)(2,1)S(1)}, bf16[384,128]{1,0:T(8,128)(2,1)S(1)}, u32[]{:S(2)}, u32[]{:S(2)}) %collective-permute-start.18) | collective-permute-done | bytes 98336 | tf_op jit(solution)/shard_map/ppermute | solution.py:310
  52.3 1.3 %collective-permute-start.19 = (bf16[768,128]{1,0:T(8,128)(2,1)S(1)}, bf16[768,128]{1,0:T(8,128)(2,1)S(1)}, u32[]{:S(2)}, u32[]{:S(2)}) collective-permute-start(bf16[768,128]{1,0:T(8,128)(2,1)S(1)} %add.22), channel_id=1, source_target_pairs={{0,7},{1,0},{2,1},{3,2},{4,3},{5,4},{6,5},{7,6},{8,15},{9,8},{10,9... | collective-permute-start | bytes 589832 | tf_op jit(solution)/shard_map/ppermute | solution.py:310
  53.6 0.0 collective-permute-done.14.got
  53.7 0.9 %collective-permute-start.15 = (bf16[768,128]{1,0:T(8,128)(2,1)S(1)}, bf16[768,128]{1,0:T(8,128)(2,1)S(1)}, u32[]{:S(2)}, u32[]{:S(2)}) collective-permute-start(bf16[768,128]{1,0:T(8,128)(2,1)S(1)} %add.20), channel_id=1, source_target_pairs={{0,1},{1,2},{2,3},{3,4},{4,5},{5,6},{6,7},{7,0},{8,9},{9,10},{10,1... | collective-permute-start | bytes 589832 | tf_op jit(solution)/shard_map/ppermute | solution.py:310
  54.6 6.0 %collective-permute-start.13 = (bf16[2,512,128]{2,1,0:T(8,128)(2,1)S(1)}, bf16[2,512,128]{2,1,0:T(8,128)(2,1)S(1)}, u32[]{:S(2)}, u32[]{:S(2)}) collective-permute-start(bf16[2,512,128]{2,1,0:T(8,128)(2,1)S(1)} %get-tuple-element.53), channel_id=1, source_target_pairs={{0,8},{1,9},{2,10},{3,11},{4,12},{5,13},{6,14},{7,15},{8,0},{9,1},... | collective-permute-start | bytes 786440 | tf_op jit(solution)/shard_map/ppermute | solution.py:306
  60.6 0.0 collective-permute-done.19.got
  60.6 3.2 %collective-permute-start.20 = (bf16[768,128]{1,0:T(8,128)(2,1)S(1)}, bf16[768,128]{1,0:T(8,128)(2,1)S(1)}, u32[]{:S(2)}, u32[]{:S(2)}) collective-permute-start(bf16[768,128]{1,0:T(8,128)(2,1)S(1)} %add.23), channel_id=1, source_target_pairs={{0,7},{1,0},{2,1},{3,2},{4,3},{5,4},{6,5},{7,6},{8,15},{9,8},{10,9... | collective-permute-start | bytes 589832 | tf_op jit(solution)/shard_map/ppermute | solution.py:310
  63.9 0.0 collective-permute-done.15.got
  63.9 0.1 collective-permute-start.16
  64.0 5.1 %collective-permute-start.22 = (bf16[384,128]{1,0:T(8,128)(2,1)S(1)}, bf16[384,128]{1,0:T(8,128)(2,1)S(1)}, u32[]{:S(2)}, u32[]{:S(2)}) collective-permute-start(bf16[384,128]{1,0:T(8,128)(2,1)S(1)} %get-tuple-element.67), channel_id=1, source_target_pairs={{0,8},{1,9},{2,10},{3,11},{4,12},{5,13},{6,14},{7,15},{8,0},{9,1},... | collective-permute-start | bytes 294920 | tf_op jit(solution)/shard_map/ppermute | solution.py:306
  69.1 0.0 collective-permute-done.20.got
  69.1 3.5 %collective-permute-start.21 = (bf16[384,128]{1,0:T(8,128)(2,1)S(1)}, bf16[384,128]{1,0:T(8,128)(2,1)S(1)}, u32[]{:S(2)}, u32[]{:S(2)}) collective-permute-start(bf16[384,128]{1,0:T(8,128)(2,1)S(1)} %get-tuple-element.66), channel_id=1, source_target_pairs={{0,7},{1,0},{2,1},{3,2},{4,3},{5,4},{6,5},{7,6},{8,15},{9,8},{10,9... | collective-permute-start | bytes 294920 | tf_op jit(solution)/shard_map/ppermute | solution.py:310
  72.6 4.1 %collective-permute-start.24 = (bf16[384,128]{1,0:T(8,128)(2,1)S(1)}, bf16[384,128]{1,0:T(8,128)(2,1)S(1)}, u32[]{:S(2)}, u32[]{:S(2)}) collective-permute-start(bf16[384,128]{1,0:T(8,128)(2,1)S(1)} %get-tuple-element.69), channel_id=1, source_target_pairs={{0,15},{1,8},{2,9},{3,10},{4,11},{5,12},{6,13},{7,14},{8,7},{9,0},... | collective-permute-start | bytes 294920 | tf_op jit(solution)/shard_map/ppermute | solution.py:362
  76.7 0.0 collective-permute-done.16.got
  76.7 0.1 last.2
  76.8 2.0 %collective-permute-start.17 = (bf16[384,128]{1,0:T(8,128)(2,1)S(1)}, bf16[384,128]{1,0:T(8,128)(2,1)S(1)}, u32[]{:S(2)}, u32[]{:S(2)}) collective-permute-start(bf16[384,128]{1,0:T(8,128)(2,1)S(1)} %get-tuple-element.61), channel_id=1, source_target_pairs={{0,1},{1,2},{2,3},{3,4},{4,5},{5,6},{6,7},{7,0},{8,9},{9,10},{10,1... | collective-permute-start | bytes 294920 | tf_op jit(solution)/shard_map/ppermute | solution.py:310
  78.8 0.0 collective-permute-done.13.got
  78.8 0.0 collective-permute-start.23
  78.8 1.5 %rows.1 = (bf16[1,64,1024]{2,1,0:T(8,128)(2,1)}, bf16[1,4,64,1024]{3,2,1,0:T(8,128)(2,1)}) custom-call(s32[1,4]{1,0:T(1,128)S(1)} %copy-done.8, bf16[512,128]{1,0:T(8,128)(2,1)S(1)} %get-tuple-element.51.prefix, bf16[2,512,128]{2,1,0:T(8,128)(2,1)S(1)} %get-tuple-element.52.own, bf16[2,512,128]{2,1,0:T(8,128)(2,1)S(1)} %collective-permute-done.13.got), custom_call_target="tpu_custom_call" | custom-call | flops 1048576 | bytes 2097152 | tf_op jit(solution)/shard_map/rows/pallas_call | solution.py:372
  80.3 0.0 collective-permute-done.22.rest_3_
  80.3 0.0 collective-permute-done.21.rest_2_
  80.3 0.0 collective-permute-done.24.rest_5_
  80.3 2.4 %collective-permute-done.17.rest_1_ = bf16[384,128]{1,0:T(8,128)(2,1)S(1)} collective-permute-done((bf16[384,128]{1,0:T(8,128)(2,1)S(1)}, bf16[384,128]{1,0:T(8,128)(2,1)S(1)}, u32[]{:S(2)}, u32[]{:S(2)}) %collective-permute-start.17) | collective-permute-done | bytes 98336 | tf_op jit(solution)/shard_map/ppermute | solution.py:310
  82.7 2.8 %collective-permute-done.23.rest_4_ = bf16[384,128]{1,0:T(8,128)(2,1)S(1)} collective-permute-done((bf16[384,128]{1,0:T(8,128)(2,1)S(1)}, bf16[384,128]{1,0:T(8,128)(2,1)S(1)}, u32[]{:S(2)}, u32[]{:S(2)}) %collective-permute-start.23) | collective-permute-done | bytes 98336 | tf_op jit(solution)/shard_map/ppermute | solution.py:362
  85.5 1.3 %sums.1 = (f32[1,64,128]{2,1,0:T(8,128)}, f32[1,64,128]{2,1,0:T(8,128)}, f32[1,4,64,128]{3,2,1,0:T(8,128)}, f32[1,4,64,128]{3,2,1,0:T(8,128)}) custom-call(s32[1,4]{1,0:T(1,128)S(1)} %copy-done.8, f32[8,128]{1,0:T(8,128)S(1)} %add.19.total, bf16[384,128]{1,0:T(8,128)(2,1)S(1)} %get-tuple-element.56.rest_0_, ...), custom_call_target="tpu_custom_call" | custom-call | flops 1048576 | bytes 2097152 | tf_op jit(solution)/shard_map/sums/pallas_call | solution.py:379
  (22 shorter events, 0.3 us)
Async XLA Ops:
  0.6 3.1 %copy-start.4 = (bf16[1,64,1024]{2,1,0:T(8,128)(2,1)S(1)}, bf16[1,64,1024]{2,1,0:T(8,128)(2,1)}, u32[]{:S(2)}) copy-start(bf16[1,64,1024]{2,1,0:T(8,128)(2,1)} %qp.1) | copy-start | bytes 393220
  2.2 1.5 %copy-start.8 = (s32[1,4]{1,0:T(1,128)S(1)}, s32[1,4]{1,0:T(1,128)}, u32[]{:S(2)}) copy-start(s32[1,4]{1,0:T(1,128)} %lengths.11) | copy-start | bytes 52
  2.2 5.2 %collective-permute-start = (bf16[384,128]{1,0:T(8,128)(2,1)}, bf16[384,128]{1,0:T(8,128)(2,1)S(1)}, u32[]{:S(2)}, u32[]{:S(2)}) collective-permute-start(bf16[384,128]{1,0:T(8,128)(2,1)} %get-tuple-element.40), channel_id=1, source_target_pairs={{0,8},{1,9},{2,10},{3,11},{4,12},{5,13},{6,14},{7,15},{8,0},{9,1},... | collective-permute-start | bytes 294920 | tf_op jit(solution)/shard_map/ppermute | solution.py:306
  3.7 1.0 %copy-start = (bf16[1,4,64,1024]{3,2,1,0:T(8,128)(2,1)S(1)}, bf16[1,4,64,1024]{3,2,1,0:T(8,128)(2,1)}, u32[]{:S(2)}) copy-start(bf16[1,4,64,1024]{3,2,1,0:T(8,128)(2,1)} %qr.1) | copy-start | bytes 1572868
  4.8 1.0 %copy-start.1 = (bf16[1,4,64,1024]{3,2,1,0:T(8,128)(2,1)S(1)}, bf16[1,4,64,1024]{3,2,1,0:T(8,128)(2,1)}, u32[]{:S(2)}) copy-start(bf16[1,4,64,1024]{3,2,1,0:T(8,128)(2,1)} %dr.1) | copy-start | bytes 1572868
  5.8 0.9 %copy-start.5 = (bf16[1,64,1024]{2,1,0:T(8,128)(2,1)S(1)}, bf16[1,64,1024]{2,1,0:T(8,128)(2,1)}, u32[]{:S(2)}) copy-start(bf16[1,64,1024]{2,1,0:T(8,128)(2,1)} %dp.1) | copy-start | bytes 393220
  6.7 0.8 copy-start.2
  6.7 0.9 %copy-start.3 = (bf16[1,4,64,128]{3,2,1,0:T(8,128)(2,1)S(1)}, bf16[1,4,64,128]{3,2,1,0:T(8,128)(2,1)}, u32[]{:S(2)}) copy-start(bf16[1,4,64,128]{3,2,1,0:T(8,128)(2,1)} %vr.3) | copy-start | bytes 196612
  6.7 0.9 %copy-start.6 = (bf16[1,64,128]{2,1,0:T(8,128)(2,1)S(1)}, bf16[1,64,128]{2,1,0:T(8,128)(2,1)}, u32[]{:S(2)}) copy-start(bf16[1,64,128]{2,1,0:T(8,128)(2,1)} %kp.3) | copy-start | bytes 49156
  6.7 0.9 %copy-start.7 = (bf16[1,64,128]{2,1,0:T(8,128)(2,1)S(1)}, bf16[1,64,128]{2,1,0:T(8,128)(2,1)}, u32[]{:S(2)}) copy-start(bf16[1,64,128]{2,1,0:T(8,128)(2,1)} %vp.3) | copy-start | bytes 49156
  7.6 2.6 %copy-start.9 = (f32[8,128]{1,0:T(8,128)S(1)}, f32[8,128]{1,0:T(8,128)}, u32[]{:S(2)}) copy-start(f32[8,128]{1,0:T(8,128)} %get-tuple-element.42) | copy-start | bytes 12292
  8.2 11.2 %collective-permute-start.1 = (bf16[768,128]{1,0:T(8,128)(2,1)S(1)}, bf16[768,128]{1,0:T(8,128)(2,1)S(1)}, u32[]{:S(2)}, u32[]{:S(2)}) collective-permute-start(bf16[768,128]{1,0:T(8,128)(2,1)S(1)} %block.1.rest_0_), channel_id=1, source_target_pairs={{0,1},{1,2},{2,3},{3,4},{4,5},{5,6},{6,7},{7,0},{8,9},{9,10},{10,1... | collective-permute-start | bytes 589832 | tf_op jit(solution)/shard_map/ppermute | solution.py:310
  10.2 5.1 %collective-permute-start.2 = (f32[8,128]{1,0:T(8,128)S(1)}, f32[8,128]{1,0:T(8,128)S(1)}, u32[]{:S(2)}, u32[]{:S(2)}) collective-permute-start(f32[8,128]{1,0:T(8,128)S(1)} %copy-done.9), channel_id=1, source_target_pairs={{0,32},{16,48},{32,0},{48,16},{64,96},{80,112},{96,64},{112,80},{1... | collective-permute-start | bytes 12296 | tf_op jit(solution)/shard_map/ppermute | solution.py:313
  15.3 7.2 %collective-permute-start.10 = (bf16[768,128]{1,0:T(8,128)(2,1)S(1)}, bf16[768,128]{1,0:T(8,128)(2,1)S(1)}, u32[]{:S(2)}, u32[]{:S(2)}) collective-permute-start(bf16[768,128]{1,0:T(8,128)(2,1)S(1)} %block.1.rest_0_), channel_id=1, source_target_pairs={{0,7},{1,0},{2,1},{3,2},{4,3},{5,4},{6,5},{7,6},{8,15},{9,8},{10,9... | collective-permute-start | bytes 589832 | tf_op jit(solution)/shard_map/ppermute | solution.py:310
  19.4 6.9 %collective-permute-start.3 = (bf16[768,128]{1,0:T(8,128)(2,1)S(1)}, bf16[768,128]{1,0:T(8,128)(2,1)S(1)}, u32[]{:S(2)}, u32[]{:S(2)}) collective-permute-start(bf16[768,128]{1,0:T(8,128)(2,1)S(1)} %collective-permute-done.1.rest_1_), channel_id=1, source_target_pairs={{0,1},{1,2},{2,3},{3,4},{4,5},{5,6},{6,7},{7,0},{8,9},{9,10},{10,1... | collective-permute-start | bytes 589832 | tf_op jit(solution)/shard_map/ppermute | solution.py:310
  19.4 19.1 %collective-permute-start.8 = (bf16[2,2,512,128]{3,2,1,0:T(8,128)(2,1)S(1)}, bf16[2,2,512,128]{3,2,1,0:T(8,128)(2,1)S(1)}, u32[]{:S(2)}, u32[]{:S(2)}) collective-permute-start(bf16[2,2,512,128]{3,2,1,0:T(8,128)(2,1)S(1)} %get-tuple-element.49), channel_id=1, source_target_pairs={{0,8},{1,9},{2,10},{3,11},{4,12},{5,13},{6,14},{7,15},{8,0},{9,1},... | collective-permute-start | bytes 1572872 | tf_op jit(solution)/shard_map/ppermute | solution.py:306
  20.3 5.9 %collective-permute-start.4 = (f32[8,128]{1,0:T(8,128)S(1)}, f32[8,128]{1,0:T(8,128)S(1)}, u32[]{:S(2)}, u32[]{:S(2)}) collective-permute-start(f32[8,128]{1,0:T(8,128)S(1)} %add.16), channel_id=1, source_target_pairs={{0,16},{16,0},{32,48},{48,32},{64,80},{80,64},{96,112},{112,96},{1... | collective-permute-start | bytes 12296 | tf_op jit(solution)/shard_map/ppermute | solution.py:313
  22.5 6.9 %collective-permute-start.11 = (bf16[768,128]{1,0:T(8,128)(2,1)S(1)}, bf16[768,128]{1,0:T(8,128)(2,1)S(1)}, u32[]{:S(2)}, u32[]{:S(2)}) collective-permute-start(bf16[768,128]{1,0:T(8,128)(2,1)S(1)} %collective-permute-done.10.rest_7_), channel_id=1, source_target_pairs={{0,7},{1,0},{2,1},{3,2},{4,3},{5,4},{6,5},{7,6},{8,15},{9,8},{10,9... | collective-permute-start | bytes 589832 | tf_op jit(solution)/shard_map/ppermute | solution.py:310
  26.2 7.0 %collective-permute-start.5 = (bf16[768,128]{1,0:T(8,128)(2,1)S(1)}, bf16[768,128]{1,0:T(8,128)(2,1)S(1)}, u32[]{:S(2)}, u32[]{:S(2)}) collective-permute-start(bf16[768,128]{1,0:T(8,128)(2,1)S(1)} %collective-permute-done.3.rest_2_), channel_id=1, source_target_pairs={{0,1},{1,2},{2,3},{3,4},{4,5},{5,6},{6,7},{7,0},{8,9},{9,10},{10,1... | collective-permute-start | bytes 589832 | tf_op jit(solution)/shard_map/ppermute | solution.py:310
  26.3 6.8 %collective-permute-start.6 = (f32[8,128]{1,0:T(8,128)S(1)}, f32[8,128]{1,0:T(8,128)S(1)}, u32[]{:S(2)}, u32[]{:S(2)}) collective-permute-start(f32[8,128]{1,0:T(8,128)S(1)} %add.17), channel_id=1, source_target_pairs={{0,64},{16,80},{32,96},{48,112},{64,0},{80,16},{96,32},{112,48},{1... | collective-permute-start | bytes 12296 | tf_op jit(solution)/shard_map/ppermute | solution.py:313
  29.4 9.0 %collective-permute-start.12 = (bf16[768,128]{1,0:T(8,128)(2,1)S(1)}, bf16[768,128]{1,0:T(8,128)(2,1)S(1)}, u32[]{:S(2)}, u32[]{:S(2)}) collective-permute-start(bf16[768,128]{1,0:T(8,128)(2,1)S(1)} %collective-permute-done.11.rest_6_), channel_id=1, source_target_pairs={{0,7},{1,0},{2,1},{3,2},{4,3},{5,4},{6,5},{7,6},{8,15},{9,8},{10,9... | collective-permute-start | bytes 589832 | tf_op jit(solution)/shard_map/ppermute | solution.py:310
  33.2 6.9 %collective-permute-start.9 = (bf16[768,128]{1,0:T(8,128)(2,1)S(1)}, bf16[768,128]{1,0:T(8,128)(2,1)S(1)}, u32[]{:S(2)}, u32[]{:S(2)}) collective-permute-start(bf16[768,128]{1,0:T(8,128)(2,1)S(1)} %collective-permute-done.5.rest_3_), channel_id=1, source_target_pairs={{0,1},{1,2},{2,3},{3,4},{4,5},{5,6},{6,7},{7,0},{8,9},{9,10},{10,1... | collective-permute-start | bytes 589832 | tf_op jit(solution)/shard_map/ppermute | solution.py:310
  33.2 5.2 %collective-permute-start.7 = (f32[8,128]{1,0:T(8,128)S(1)}, f32[8,128]{1,0:T(8,128)S(1)}, u32[]{:S(2)}, u32[]{:S(2)}) collective-permute-start(f32[8,128]{1,0:T(8,128)S(1)} %add.18), channel_id=1, source_target_pairs={{0,128},{16,144},{32,160},{48,176},{64,192},{80,208},{96,224},{112... | collective-permute-start | bytes 12296 | tf_op jit(solution)/shard_map/ppermute | solution.py:313
  47.6 4.7 %collective-permute-start.18 = (bf16[384,128]{1,0:T(8,128)(2,1)S(1)}, bf16[384,128]{1,0:T(8,128)(2,1)S(1)}, u32[]{:S(2)}, u32[]{:S(2)}) collective-permute-start(bf16[384,128]{1,0:T(8,128)(2,1)S(1)} %get-tuple-element.62), channel_id=1, source_target_pairs={{0,7},{1,0},{2,1},{3,2},{4,3},{5,4},{6,5},{7,6},{8,15},{9,8},{10,9... | collective-permute-start | bytes 294920 | tf_op jit(solution)/shard_map/ppermute | solution.py:310
  47.7 5.9 %collective-permute-start.14 = (bf16[384,128]{1,0:T(8,128)(2,1)S(1)}, bf16[384,128]{1,0:T(8,128)(2,1)S(1)}, u32[]{:S(2)}, u32[]{:S(2)}) collective-permute-start(bf16[384,128]{1,0:T(8,128)(2,1)S(1)} %get-tuple-element.57), channel_id=1, source_target_pairs={{0,1},{1,2},{2,3},{3,4},{4,5},{5,6},{6,7},{7,0},{8,9},{9,10},{10,1... | collective-permute-start | bytes 294920 | tf_op jit(solution)/shard_map/ppermute | solution.py:310
  52.3 8.2 %collective-permute-start.19 = (bf16[768,128]{1,0:T(8,128)(2,1)S(1)}, bf16[768,128]{1,0:T(8,128)(2,1)S(1)}, u32[]{:S(2)}, u32[]{:S(2)}) collective-permute-start(bf16[768,128]{1,0:T(8,128)(2,1)S(1)} %add.22), channel_id=1, source_target_pairs={{0,7},{1,0},{2,1},{3,2},{4,3},{5,4},{6,5},{7,6},{8,15},{9,8},{10,9... | collective-permute-start | bytes 589832 | tf_op jit(solution)/shard_map/ppermute | solution.py:310
  53.7 10.2 %collective-permute-start.15 = (bf16[768,128]{1,0:T(8,128)(2,1)S(1)}, bf16[768,128]{1,0:T(8,128)(2,1)S(1)}, u32[]{:S(2)}, u32[]{:S(2)}) collective-permute-start(bf16[768,128]{1,0:T(8,128)(2,1)S(1)} %add.20), channel_id=1, source_target_pairs={{0,1},{1,2},{2,3},{3,4},{4,5},{5,6},{6,7},{7,0},{8,9},{9,10},{10,1... | collective-permute-start | bytes 589832 | tf_op jit(solution)/shard_map/ppermute | solution.py:310
  54.6 24.2 %collective-permute-start.13 = (bf16[2,512,128]{2,1,0:T(8,128)(2,1)S(1)}, bf16[2,512,128]{2,1,0:T(8,128)(2,1)S(1)}, u32[]{:S(2)}, u32[]{:S(2)}) collective-permute-start(bf16[2,512,128]{2,1,0:T(8,128)(2,1)S(1)} %get-tuple-element.53), channel_id=1, source_target_pairs={{0,8},{1,9},{2,10},{3,11},{4,12},{5,13},{6,14},{7,15},{8,0},{9,1},... | collective-permute-start | bytes 786440 | tf_op jit(solution)/shard_map/ppermute | solution.py:306
  60.6 8.5 %collective-permute-start.20 = (bf16[768,128]{1,0:T(8,128)(2,1)S(1)}, bf16[768,128]{1,0:T(8,128)(2,1)S(1)}, u32[]{:S(2)}, u32[]{:S(2)}) collective-permute-start(bf16[768,128]{1,0:T(8,128)(2,1)S(1)} %add.23), channel_id=1, source_target_pairs={{0,7},{1,0},{2,1},{3,2},{4,3},{5,4},{6,5},{7,6},{8,15},{9,8},{10,9... | collective-permute-start | bytes 589832 | tf_op jit(solution)/shard_map/ppermute | solution.py:310
  63.9 12.8 %collective-permute-start.16 = (bf16[768,128]{1,0:T(8,128)(2,1)S(1)}, bf16[768,128]{1,0:T(8,128)(2,1)S(1)}, u32[]{:S(2)}, u32[]{:S(2)}) collective-permute-start(bf16[768,128]{1,0:T(8,128)(2,1)S(1)} %add.21), channel_id=1, source_target_pairs={{0,1},{1,2},{2,3},{3,4},{4,5},{5,6},{6,7},{7,0},{8,9},{9,10},{10,1... | collective-permute-start | bytes 589832 | tf_op jit(solution)/shard_map/ppermute | solution.py:310
  64.0 16.3 %collective-permute-start.22 = (bf16[384,128]{1,0:T(8,128)(2,1)S(1)}, bf16[384,128]{1,0:T(8,128)(2,1)S(1)}, u32[]{:S(2)}, u32[]{:S(2)}) collective-permute-start(bf16[384,128]{1,0:T(8,128)(2,1)S(1)} %get-tuple-element.67), channel_id=1, source_target_pairs={{0,8},{1,9},{2,10},{3,11},{4,12},{5,13},{6,14},{7,15},{8,0},{9,1},... | collective-permute-start | bytes 294920 | tf_op jit(solution)/shard_map/ppermute | solution.py:306
  69.1 11.1 %collective-permute-start.21 = (bf16[384,128]{1,0:T(8,128)(2,1)S(1)}, bf16[384,128]{1,0:T(8,128)(2,1)S(1)}, u32[]{:S(2)}, u32[]{:S(2)}) collective-permute-start(bf16[384,128]{1,0:T(8,128)(2,1)S(1)} %get-tuple-element.66), channel_id=1, source_target_pairs={{0,7},{1,0},{2,1},{3,2},{4,3},{5,4},{6,5},{7,6},{8,15},{9,8},{10,9... | collective-permute-start | bytes 294920 | tf_op jit(solution)/shard_map/ppermute | solution.py:310
  72.6 7.6 %collective-permute-start.24 = (bf16[384,128]{1,0:T(8,128)(2,1)S(1)}, bf16[384,128]{1,0:T(8,128)(2,1)S(1)}, u32[]{:S(2)}, u32[]{:S(2)}) collective-permute-start(bf16[384,128]{1,0:T(8,128)(2,1)S(1)} %get-tuple-element.69), channel_id=1, source_target_pairs={{0,15},{1,8},{2,9},{3,10},{4,11},{5,12},{6,13},{7,14},{8,7},{9,0},... | collective-permute-start | bytes 294920 | tf_op jit(solution)/shard_map/ppermute | solution.py:362
  76.8 5.9 %collective-permute-start.17 = (bf16[384,128]{1,0:T(8,128)(2,1)S(1)}, bf16[384,128]{1,0:T(8,128)(2,1)S(1)}, u32[]{:S(2)}, u32[]{:S(2)}) collective-permute-start(bf16[384,128]{1,0:T(8,128)(2,1)S(1)} %get-tuple-element.61), channel_id=1, source_target_pairs={{0,1},{1,2},{2,3},{3,4},{4,5},{5,6},{6,7},{7,0},{8,9},{9,10},{10,1... | collective-permute-start | bytes 294920 | tf_op jit(solution)/shard_map/ppermute | solution.py:310
  78.8 6.7 %collective-permute-start.23 = (bf16[384,128]{1,0:T(8,128)(2,1)S(1)}, bf16[384,128]{1,0:T(8,128)(2,1)S(1)}, u32[]{:S(2)}, u32[]{:S(2)}) collective-permute-start(bf16[384,128]{1,0:T(8,128)(2,1)S(1)} %get-tuple-element.68), channel_id=1, source_target_pairs={{0,9},{1,10},{2,11},{3,12},{4,13},{5,14},{6,15},{7,8},{8,1},{9,2},... | collective-permute-start | bytes 294920 | tf_op jit(solution)/shard_map/ppermute | solution.py:362
